TPU v7x, 256 devices: a whole 4x4x8 slice. The times are simulated.
256 devices in a mesh: dp: 4 (over x), seq: 64 (over y, z, core).
Axes of the slice: x: 4, y: 4, z: 8, core: 2. Of those that a mesh axis runs over, the one named last changes fastest.
Arguments:
- queries: bfloat16 [4, 64, 192, 1536], P('dp', 'seq'), may hold values from -100 to 100
- key_field: bfloat16 [4, 64, 192, 1536], P('dp', 'seq'), may hold values from -7 to 7
- value_field: bfloat16 [4, 64, 192, 1536], P('dp', 'seq'), may hold values from -6 to 6
- out_grad: bfloat16 [4, 64, 192, 1536], P('dp', 'seq'), may hold values from -6 to 6
- out_weight: bfloat16 [1536, 1536], P('seq'), may hold values from -0.15625 to 0.15625
- frame_video: int32 [4, 64], P('dp'), may hold values from 0 to 15, never falling along the last dimension, each value on 1 to 32 neighbouring positions
Outputs:
- mixed_out: bfloat16 [4, 64, 192, 1536], P('dp', 'seq')
- query_grad: bfloat16 [4, 64, 192, 1536], P('dp', 'seq')
- key_grad: bfloat16 [4, 64, 192, 1536], P('dp', 'seq')
- value_grad: bfloat16 [4, 64, 192, 1536], P('dp', 'seq')
- weight_grad: float32 [1536, 1536], P('seq')
Inputs may be any that keep to these rules, and one draw needn't show every extreme that they name: `frame_video`: each replica's frames are grouped into whole videos in order: ids never fall, each video has 1 to min(32, 32) frames and one has exactly that many.
All inputs are finite; a program needn't handle non-finite values.
Results may differ from a plain program's by a relative error of at most 0.04.
Values may be sent and summed in bfloat16 or wider, within the bound.
No kernel may reach another device: no remote copies, remote signals or barrier semaphores. Data moves between devices by JAX's collectives and lax.ppermute only.
A program may use at most 128 MiB of HBM per device.

v0:
```python
import functools

import jax
import jax.numpy as jnp
import numpy as np
from jax import lax
from jax.experimental import pallas as pl
from jax.experimental.pallas import tpu as pltpu
from jax.sharding import PartitionSpec as P

HEAD = 128
HEADS = 12
WIDTH = HEAD * HEADS
HALF = WIDTH // 2
FRAMES = 64
PLACES = 3
ROWS = FRAMES * PLACES
NX, NY, NZ = 4, 4, 8
SEQ = NY * NZ * 2
STRIP = WIDTH // SEQ
QUARTER = WIDTH // NX
BF = jnp.bfloat16
F32 = jnp.float32
FACTOR = HEAD ** (-0.5)
MIB = 1 << 20


def params(mib):
    return pltpu.CompilerParams(vmem_limit_bytes=mib * MIB)


def dot(a, b, dims=((1,), (0,))):
    return lax.dot_general(a, b, (dims, ((), ())), preferred_element_type=F32)


def swap_matrix(to_blocks):
    a = lax.broadcasted_iota(jnp.int32, (256, 256), 0 if to_blocks else 1)
    b = lax.broadcasted_iota(jnp.int32, (256, 256), 1 if to_blocks else 0)
    return jnp.where(8 * (a % 32) + a // 32 == b, F32(1), F32(0)).astype(BF)


def pack(sources, out_ref):
    swap = swap_matrix(False)
    for half in range(2):
        for tile in range(HALF // 256):
            parts = [
                src[32 * half : 32 * half + 32, HALF * e + 256 * tile : HALF * e + 256 * tile + 256]
                for src in sources
                for e in range(2)
            ]
            mixed = dot(swap, jnp.concatenate(parts, axis=0))
            out_ref[256 * half : 256 * half + 256, 256 * tile : 256 * tile + 256] = mixed.astype(BF)


def unpack(in_ref, sinks):
    swap = swap_matrix(True)
    for half in range(2):
        for tile in range(HALF // 256):
            piece = in_ref[256 * half : 256 * half + 256, 256 * tile : 256 * tile + 256]
            rows = dot(swap, piece).astype(BF)
            for n in range(8):
                col = HALF * (n % 2) + 256 * tile
                sinks[n // 2][32 * half : 32 * half + 32, col : col + 256] = rows[32 * n : 32 * n + 32]


def pack_kernel(a, b, c, d, out_ref):
    pack((a, b, c, d), out_ref)


def unpack_kernel(in_ref, a, b, c, d):
    unpack(in_ref, (a, b, c, d))


place_block = pl.BlockSpec((FRAMES, WIDTH), lambda j: (j, 0))
message_block = pl.BlockSpec((8 * SEQ, HALF), lambda j: (0, j))
rows_shape = jax.ShapeDtypeStruct((ROWS, WIDTH), BF)
message_shape = jax.ShapeDtypeStruct((8 * SEQ, PLACES * HALF), BF)


def pack_call(*arrays):
    return pl.pallas_call(
        pack_kernel,
        grid=(PLACES,),
        in_specs=[place_block] * 4,
        out_specs=message_block,
        out_shape=message_shape,
        compiler_params=params(24),
        name="pack",
    )(*arrays)


def unpack_call(message):
    return pl.pallas_call(
        unpack_kernel,
        grid=(PLACES,),
        in_specs=[message_block],
        out_specs=[place_block] * 4,
        out_shape=[rows_shape] * 4,
        compiler_params=params(24),
        name="unpack",
    )(message)


def pair(ref, n):
    at = 2 * HEAD * n
    return jnp.concatenate([ref[:, at : at + HEAD], ref[:, at + HEAD : at + 2 * HEAD]], axis=0)


def put_pair(ref, n, value):
    at = 2 * HEAD * n
    ref[:, at : at + HEAD] = value[:FRAMES]
    ref[:, at + HEAD : at + 2 * HEAD] = value[FRAMES:]


def forward_kernel(mask_ref, in_ref, q, k, v, g, mixed, probs_ref):
    unpack(in_ref, (q, k, v, g))
    allowed = mask_ref[...] > 0.5
    for n in range(HEADS // 2):
        logits = dot(pair(q, n), pair(k, n), ((1,), (1,))) * FACTOR
        logits = jnp.where(allowed, logits, F32(-1e30))
        shifted = jnp.exp(logits - jnp.max(logits, axis=-1, keepdims=True))
        probs = shifted / jnp.sum(shifted, axis=-1, keepdims=True)
        probs_ref[n] = probs
        put_pair(mixed, n, dot(probs.astype(BF), pair(v, n)).astype(BF))


probs_block = pl.BlockSpec((HEADS // 2, 2 * FRAMES, 2 * FRAMES), lambda j: (j, 0, 0))


def forward_call(mask, message):
    return pl.pallas_call(
        forward_kernel,
        grid=(PLACES,),
        in_specs=[pl.BlockSpec((128, 128), lambda j: (0, 0)), message_block],
        out_specs=[place_block] * 5 + [probs_block],
        out_shape=[rows_shape] * 5 + [jax.ShapeDtypeStruct((HEADS // 2 * PLACES, 128, 128), F32)],
        compiler_params=params(32),
        name="forward",
    )(mask, message)


def weight_kernel(at, mixed, grad, keep, send, turned, strips):
    @pl.when(pl.program_id(0) == 0)
    def _():
        turned[...] = mixed[...].astype(F32).T
        for side in range(2):
            core = at[0] if side == 0 else 1 - at[0]
            for dy in range(NY):
                for dz in range(NZ):
                    y, z = (at[2] + dy) % NY, (at[3] + dz) % NZ
                    src = pl.multiple_of((y * NZ + z) * 2 * STRIP + core * STRIP, 8)
                    dst = (dy * NZ + dz) * STRIP
                    strips[side, dst : dst + STRIP, :] = turned[pl.ds(src, STRIP), :]

    for side, out in ((0, keep), (1, send)):
        out[0] = dot(strips[side].astype(BF), grad[...]).astype(BF)


def weight_call(at, mixed, grad):
    return pl.pallas_call(
        weight_kernel,
        grid_spec=pltpu.PrefetchScalarGridSpec(
            num_scalar_prefetch=1,
            grid=(NX,),
            in_specs=[
                pl.BlockSpec((ROWS, WIDTH), lambda d, at: (0, 0)),
                pl.BlockSpec((ROWS, QUARTER), lambda d, at: (0, (at[1] + d) % NX)),
            ],
            out_specs=[pl.BlockSpec((1, HALF, QUARTER), lambda d, at: (d, 0, 0))] * 2,
            scratch_shapes=[pltpu.VMEM((WIDTH, ROWS), F32), pltpu.VMEM((2, HALF, ROWS), F32)],
        ),
        out_shape=[jax.ShapeDtypeStruct((NX, HALF, QUARTER), BF)] * 2,
        compiler_params=params(32),
        name="weight",
    )(at, mixed, grad)


def project_kernel(mixed, grad, weight, out, mixed_grad, total):
    step = pl.program_id(0)
    w = weight[...]
    part = dot(mixed[...], w)

    @pl.when(step == 0)
    def _():
        total[...] = part

    @pl.when(step > 0)
    def _():
        total[...] += part

    mixed_grad[...] = dot(grad[...], w, ((1,), (1,))).astype(BF)

    @pl.when(step == pl.num_programs(0) - 1)
    def _():
        out[...] = total[...].astype(BF)


def project_call(mixed, grad, weight):
    depth = 256
    return pl.pallas_call(
        project_kernel,
        grid=(WIDTH // depth,),
        in_specs=[
            pl.BlockSpec((ROWS, depth), lambda i: (0, i)),
            pl.BlockSpec((ROWS, WIDTH), lambda i: (0, 0)),
            pl.BlockSpec((depth, WIDTH), lambda i: (i, 0)),
        ],
        out_specs=[
            pl.BlockSpec((ROWS, WIDTH), lambda i: (0, 0)),
            pl.BlockSpec((ROWS, depth), lambda i: (0, i)),
        ],
        out_shape=[rows_shape] * 2,
        scratch_shapes=[pltpu.VMEM((ROWS, WIDTH), F32)],
        compiler_params=params(32),
        name="project",
    )(mixed, grad, weight)


def backward_kernel(q, k, v, mixed, mixed_grad, out, probs_ref, message, q_grad, k_grad, v_grad):
    for n in range(HEADS // 2):
        probs = probs_ref[n]
        grad = pair(mixed_grad, n)
        put_pair(v_grad, n, dot(probs.astype(BF), grad, ((0,), (0,))).astype(BF))
        through = dot(grad, pair(v, n), ((1,), (1,)))
        inner = jnp.sum(grad.astype(F32) * pair(mixed, n).astype(F32), axis=-1, keepdims=True)
        score = (probs * (through - inner)).astype(BF)
        put_pair(q_grad, n, (dot(score, pair(k, n)) * FACTOR).astype(BF))
        put_pair(k_grad, n, (dot(score, pair(q, n), ((0,), (0,))) * FACTOR).astype(BF))
    pack((out, q_grad, k_grad, v_grad), message)


def backward_call(*arrays):
    return pl.pallas_call(
        backward_kernel,
        grid=(PLACES,),
        in_specs=[place_block] * 6 + [probs_block],
        out_specs=message_block,
        out_shape=message_shape,
        scratch_shapes=[pltpu.VMEM((FRAMES, WIDTH), BF)] * 3,
        compiler_params=params(32),
        name="backward",
    )(*arrays)


def seq_shift(dy, dz, dc):
    seq = np.arange(SEQ).reshape(NY, NZ, 2)
    return [
        (int(seq[y, z, c]), int(seq[(y + dy) % NY, (z + dz) % NZ, c ^ dc]))
        for y in range(NY)
        for z in range(NZ)
        for c in range(2)
    ]


def add_up(parts):
    total = parts[0].astype(F32)
    for part in parts[1:]:
        total = total + part.astype(F32)
    return total


def reduce_weight(keep, send):
    came = lax.ppermute(send, "seq", seq_shift(0, 0, 1))
    parts = [add_up([keep[d], came[d]]).astype(BF) for d in range(NX)]
    came = [lax.ppermute(parts[d], "dp", [(i, (i + d) % NX) for i in range(NX)]) for d in (1, 3, 2)]
    chip = add_up([parts[0]] + came).astype(BF).reshape(NY, NZ * STRIP, QUARTER)
    came = [lax.ppermute(chip[d], "seq", seq_shift(d, 0, 0)) for d in (1, 3, 2)]
    column = add_up([chip[0]] + came).astype(BF).reshape(NZ, STRIP, QUARTER)
    came = [lax.ppermute(column[d], "seq", seq_shift(0, d, 0)) for d in (1, 7, 2, 6, 3, 5, 4)]
    strip = add_up([column[0]] + came)
    return lax.all_gather(strip, "dp", axis=1, tiled=True)


def gather_weight(out_weight):
    seq = np.arange(SEQ).reshape(NY, NZ * 2)
    rows = [list(map(int, seq[y])) for y in range(NY)]
    columns = [list(map(int, seq[:, n])) for n in range(NZ * 2)]
    part = lax.all_gather(out_weight, "seq", axis=0, tiled=True, axis_index_groups=rows)
    return lax.all_gather(part, "seq", axis=0, tiled=True, axis_index_groups=columns)


def exchange(message):
    return lax.all_to_all(message, "seq", split_axis=0, concat_axis=0, tiled=True)


def local(queries, key_field, value_field, out_grad, out_weight, frame_video):
    weight = gather_weight(out_weight)
    videos = frame_video[0]
    same = jnp.tile((videos[:, None] == videos[None, :]), (2, 2))
    head = jnp.arange(2 * FRAMES) // FRAMES
    mask = (same & (head[:, None] == head[None, :])).astype(F32)
    rank = lax.axis_index("seq")
    at = jnp.stack([rank % 2, lax.axis_index("dp"), rank // (2 * NZ), rank // 2 % NZ]).astype(jnp.int32)

    flat = [x.reshape(ROWS, WIDTH) for x in (queries, key_field, value_field, out_grad)]
    arrived = exchange(pack_call(*flat))
    q, k, v, g, mixed, probs = forward_call(mask, arrived)
    keep, send = weight_call(at, mixed, g)
    out, mixed_grad = project_call(mixed, g, weight)
    message = backward_call(q, k, v, mixed, mixed_grad, out, probs)
    results = unpack_call(exchange(message))
    weight_grad = reduce_weight(keep, send)
    return tuple(x.reshape(queries.shape) for x in results) + (weight_grad,)


def solution(mesh):
    placed = P("dp", "seq", None, None)
    return jax.shard_map(
        local,
        mesh=mesh,
        in_specs=(placed, placed, placed, placed, P("seq", None), P("dp", None)),
        out_specs=(placed, placed, placed, placed, P("seq", None)),
        check_vma=False,
    )
```

profile of v0, /device:TPU:8, one launch (start us, length us, event | category | flops | bytes accessed | tf_op | source)
XLA Modules:
  0.0 251.8 jit_solution(9331703747742068648)
XLA Ops:
  7.2 0.0 all-gather.3.cloned.1.call-start
  7.2 0.7 all-gather.3.cloned.1.call-update
  7.9 0.0 all-gather.5.cloned.1.call-start
  8.0 43.6 %all-gather.3.cloned.1.call-done = bf16[384,1536]{1,0:T(8,128)(2,1)} async-done(((bf16[24,1536]{1,0:T(8,128)(2,1)}), bf16[384,1536]{1,0:T(8,128)(2,1)}) %all-gather.3.cloned.1.call-update) | async-done | bytes 1179664 | tf_op jit(solution)/shard_map/all_gather | solution.py:278
  51.6 0.0 all-gather.5.cloned.1.call-update
  51.6 0.0 copy-done.5
  51.6 0.0 copy-done.6
  51.6 1.1 copy-done.7
  52.7 1.1 copy-done.8
  53.8 1.3 pack.1
  55.0 1.4 copy-done
  56.4 8.1 %all-to-all-start = ((bf16[64,8,2304]{2,1,0:T(8,128)(2,1)}), bf16[64,8,2304]{2,1,0:T(8,128)(2,1)S(1)}, u32[]{:S(2)}, u32[]{:S(2)}) async-start(bf16[64,8,2304]{2,1,0:T(8,128)(2,1)} %bitcast.30), calls=%async_computation | async-start | bytes 4718592 | tf_op jit(solution)/shard_map/all_to_all | solution.py:283
  64.6 0.1 broadcast_compare_fusion
  64.7 0.1 tile.10
  64.9 0.1 pad_add_fusion.at
  64.9 0.7 and_convert_fusion.mask_ref
  65.7 54.1 %all-to-all-done = bf16[64,8,2304]{2,1,0:T(8,128)(2,1)S(1)} async-done(((bf16[64,8,2304]{2,1,0:T(8,128)(2,1)}), bf16[64,8,2304]{2,1,0:T(8,128)(2,1)S(1)}, u32[]{:S(2)}, u32[]{:S(2)}) %all-to-all-start) | async-done | bytes 2359328 | tf_op jit(solution)/shard_map/all_to_all | solution.py:283
  119.8 0.8 copy-done.15
  120.6 6.4 %forward.1 = (bf16[192,1536]{1,0:T(8,128)(2,1)S(1)}, bf16[192,1536]{1,0:T(8,128)(2,1)S(1)}, bf16[192,1536]{1,0:T(8,128)(2,1)S(1)}, bf16[192,1536]{1,0:T(8,128)(2...) custom-call(f32[128,128]{1,0:T(8,128)S(1)} %copy-done.15, bf16[512,2304]{1,0:T(8,128)(2,1)S(1)} %bitcast.29), custom_call_target="tpu_custom_call" | custom-call | tf_op jit(solution)/shard_map/forward/pallas_call | solution.py:131
  127.0 1.0 copy-done.3
  128.0 0.8 copy-done.9
  128.9 0.8 copy-done.11
  129.7 0.8 copy-done.13
  130.5 4.5 %weight.1 = (bf16[4,768,384]{2,1,0:T(8,128)(2,1)S(1)}, bf16[4,768,384]{2,1,0:T(8,128)(2,1)}) custom-call(s32[4]{0:T(128)S(1)} %pad_add_fusion.at, bf16[192,1536]{1,0:T(8,128)(2,1)S(1)} %get-tuple-element.22.mixed, bf16[192,1536]{1,0:T(8,128)(2,1)S(1)} %get-tuple-element.23.grad), custom_call_target="tpu_custom_call" | custom-call | tf_op jit(solution)/shard_map/weight/pallas_call | solution.py:160
  135.0 1.4 copy-done.2
  136.4 1.4 collective-permute-start
  137.8 2.3 copy-done.1
  140.1 5.3 %project.1 = (bf16[192,1536]{1,0:T(8,128)(2,1)S(1)}, bf16[192,1536]{1,0:T(8,128)(2,1)S(1)}) custom-call(bf16[192,1536]{1,0:T(8,128)(2,1)S(1)} %get-tuple-element.22.mixed, bf16[192,1536]{1,0:T(8,128)(2,1)S(1)} %get-tuple-element.23.grad, bf16[1536,1536]{1,0:T(8,128)(2,1)S(1)} %copy-done.1), custom_call_target="tpu_custom_call" | custom-call | tf_op jit(solution)/shard_map/project/pallas_call | solution.py:200
  145.4 6.1 %backward.1 = bf16[512,2304]{1,0:T(8,128)(2,1)} custom-call(bf16[192,1536]{1,0:T(8,128)(2,1)S(1)} %copy-done.10, bf16[192,1536]{1,0:T(8,128)(2,1)S(1)} %copy-done.12, bf16[192,1536]{1,0:T(8,128)(2,1)S(1)} %copy-done.14, bf16[192,1536]{1,0:T(8,128)(2,1)S(1)} %get-tuple-element.22.mixed, bf16[192,1536]{1,0:T(8,128)(2,1)S(1)} %get-tuple-element.24.mixed_grad, ...), custom_call_target="tpu_custom_call" | custom-call | tf_op jit(solution)/shard_map/backward/pallas_call | solution.py:233
  151.5 6.3 %all-to-all-start.1 = ((bf16[64,8,2304]{2,1,0:T(8,128)(2,1)}), bf16[64,8,2304]{2,1,0:T(8,128)(2,1)S(1)}, u32[]{:S(2)}, u32[]{:S(2)}) async-start(bf16[64,8,2304]{2,1,0:T(8,128)(2,1)} %bitcast.7), calls=%async_computation.1 | async-start | bytes 4718592 | tf_op jit(solution)/shard_map/all_to_all | solution.py:283
  157.8 0.0 collective-permute-done
  157.8 2.4 fusion.4
  160.1 3.1 %collective-permute-start.3 = (bf16[768,384]{1,0:T(8,128)(2,1)S(1)}, bf16[768,384]{1,0:T(8,128)(2,1)S(1)}, u32[]{:S(2)}, u32[]{:S(2)}) collective-permute-start(bf16[768,384]{1,0:T(8,128)(2,1)S(1)} %get-tuple-element.34), channel_id=1, source_target_pairs={{0,128},{64,192},{128,0},{192,64},{1,129},{65,193},{129,1},{193,65... | collective-permute-start | bytes 1769480 | tf_op jit(solution)/shard_map/ppermute | solution.py:265
  163.2 1.2 collective-permute-start.2
  164.4 0.9 collective-permute-start.1
  165.2 12.7 %collective-permute-done.3 = bf16[768,384]{1,0:T(8,128)(2,1)S(1)} collective-permute-done((bf16[768,384]{1,0:T(8,128)(2,1)S(1)}, bf16[768,384]{1,0:T(8,128)(2,1)S(1)}, u32[]{:S(2)}, u32[]{:S(2)}) %collective-permute-start.3) | collective-permute-done | bytes 589856 | tf_op jit(solution)/shard_map/ppermute | solution.py:265
  178.0 11.9 %collective-permute-done.2 = bf16[768,384]{1,0:T(8,128)(2,1)S(1)} collective-permute-done((bf16[768,384]{1,0:T(8,128)(2,1)S(1)}, bf16[768,384]{1,0:T(8,128)(2,1)S(1)}, u32[]{:S(2)}, u32[]{:S(2)}) %collective-permute-start.2) | collective-permute-done | bytes 589856 | tf_op jit(solution)/shard_map/ppermute | solution.py:265
  189.8 0.0 collective-permute-done.1
  189.8 1.7 fusion.2
  191.5 2.4 collective-permute-start.6
  193.9 1.4 collective-permute-start.5
  195.3 0.7 collective-permute-start.4
  195.9 6.9 %collective-permute-done.6 = bf16[192,384]{1,0:T(8,128)(2,1)S(1)} collective-permute-done((bf16[192,384]{1,0:T(8,128)(2,1)S(1)}, bf16[192,384]{1,0:T(8,128)(2,1)S(1)}, u32[]{:S(2)}, u32[]{:S(2)}) %collective-permute-start.6) | collective-permute-done | bytes 147488 | tf_op jit(solution)/shard_map/ppermute | solution.py:267
  202.8 5.6 %collective-permute-done.5 = bf16[192,384]{1,0:T(8,128)(2,1)S(1)} collective-permute-done((bf16[192,384]{1,0:T(8,128)(2,1)S(1)}, bf16[192,384]{1,0:T(8,128)(2,1)S(1)}, u32[]{:S(2)}, u32[]{:S(2)}) %collective-permute-start.5) | collective-permute-done | bytes 147488 | tf_op jit(solution)/shard_map/ppermute | solution.py:267
  208.4 0.0 collective-permute-done.4
  208.4 0.1 add_convert_fusion.4
  208.5 7.4 %collective-permute-start.13 = (bf16[24,384]{1,0:T(8,128)(2,1)S(1)}, bf16[24,384]{1,0:T(8,128)(2,1)S(1)}, u32[]{:S(2)}, u32[]{:S(2)}) collective-permute-start(bf16[24,384]{1,0:T(8,128)(2,1)S(1)} %get-tuple-element.40), channel_id=1, source_target_pairs={{0,8},{1,9},{2,10},{3,11},{4,12},{5,13},{6,14},{7,15},{8,0},{9,1},... | collective-permute-start | bytes 55304 | tf_op jit(solution)/shard_map/ppermute | solution.py:269
  215.8 0.0 collective-permute-start.12
  215.8 3.8 %collective-permute-start.11 = (bf16[24,384]{1,0:T(8,128)(2,1)S(1)}, bf16[24,384]{1,0:T(8,128)(2,1)S(1)}, u32[]{:S(2)}, u32[]{:S(2)}) collective-permute-start(bf16[24,384]{1,0:T(8,128)(2,1)S(1)} %get-tuple-element.42), channel_id=1, source_target_pairs={{0,6},{1,7},{2,8},{3,9},{4,10},{5,11},{6,12},{7,13},{8,14},{9,15},... | collective-permute-start | bytes 55304 | tf_op jit(solution)/shard_map/ppermute | solution.py:269
  219.7 0.6 collective-permute-start.10
  220.3 2.3 collective-permute-start.9
  222.6 0.0 collective-permute-done.13
  222.6 1.8 collective-permute-start.8
  224.4 0.0 collective-permute-done.12
  224.4 0.3 collective-permute-start.7
  224.7 0.0 collective-permute-done.11
  224.7 0.0 collective-permute-done.10
  224.7 1.4 collective-permute-done.9
  226.1 0.2 collective-permute-done.8
  226.4 3.0 %collective-permute-done.7 = bf16[24,384]{1,0:T(8,128)(2,1)S(1)} collective-permute-done((bf16[24,384]{1,0:T(8,128)(2,1)S(1)}, bf16[24,384]{1,0:T(8,128)(2,1)S(1)}, u32[]{:S(2)}, u32[]{:S(2)}) %collective-permute-start.7) | collective-permute-done | bytes 18464 | tf_op jit(solution)/shard_map/ppermute | solution.py:269
  229.4 12.3 %all_gather.11 = f32[24,1536]{1,0:T(8,128)S(1)} all-gather(f32[24,384]{1,0:T(8,128)S(1)} %convert_add_fusion.1), channel_id=1, replica_groups=mesh['dp'=4,'seq'=64] {'dp'}, dimensions={1}, use_global_device_ids=true | all-gather | bytes 184320 | tf_op jit(solution)/shard_map/all_gather | solution.py:271
  241.7 0.0 all-to-all-done.1
  241.7 2.5 %unpack.1 = (bf16[192,1536]{1,0:T(8,128)(2,1)}, bf16[192,1536]{1,0:T(8,128)(2,1)}, bf16[192,1536]{1,0:T(8,128)(2,1)}, bf16[192,1536]{1,0:T(8,128)(2,1)}) custom-call(bf16[512,2304]{1,0:T(8,128)(2,1)S(1)} %bitcast.28), custom_call_target="tpu_custom_call" | custom-call | tf_op jit(solution)/shard_map/unpack/pallas_call | solution.py:93
  244.2 0.7 copy.12
  (28 shorter events, 0.2 us)
Async XLA Ops:
  7.2 44.4 %copy-start.5 = (bf16[1,1,192,1536]{3,2,1,0:T(8,128)(2,1)S(1)}, bf16[1,1,192,1536]{3,2,1,0:T(8,128)(2,1)}, u32[]{:S(2)}) copy-start(bf16[1,1,192,1536]{3,2,1,0:T(8,128)(2,1)} %param.6) | copy-start | bytes 1769476
  7.2 44.4 %copy-start.6 = (bf16[1,1,192,1536]{3,2,1,0:T(8,128)(2,1)S(1)}, bf16[1,1,192,1536]{3,2,1,0:T(8,128)(2,1)}, u32[]{:S(2)}) copy-start(bf16[1,1,192,1536]{3,2,1,0:T(8,128)(2,1)} %param.7) | copy-start | bytes 1769476
  7.2 44.4 %all-gather.3.cloned.1.call-start = ((), (), s32[]{:S(2)}) async-start(), calls=%async_computation.2 | async-start | bytes 1253376 | tf_op jit(solution)/shard_map/all_gather | solution.py:278
  7.9 129.8 %all-gather.5.cloned.1.call-start = ((), (), s32[]{:S(2)}) async-start(), calls=%async_computation.3 | async-start | bytes 5898240 | tf_op jit(solution)/shard_map/all_gather | solution.py:279
  51.6 1.1 copy-start.7
  52.7 1.1 copy-start.8
  55.0 1.4 copy-start
  56.4 8.1 %copy-start.16 = (s32[1,64]{1,0:T(1,128)S(1)}, s32[1,64]{1,0:T(1,128)}, u32[]{:S(2)}) copy-start(s32[1,64]{1,0:T(1,128)} %param.11) | copy-start | bytes 772
  56.4 63.3 %all-to-all-start = ((bf16[64,8,2304]{2,1,0:T(8,128)(2,1)}), bf16[64,8,2304]{2,1,0:T(8,128)(2,1)S(1)}, u32[]{:S(2)}, u32[]{:S(2)}) async-start(bf16[64,8,2304]{2,1,0:T(8,128)(2,1)} %bitcast.30), calls=%async_computation | async-start | bytes 4718592 | tf_op jit(solution)/shard_map/all_to_all | solution.py:283
  119.8 0.8 copy-start.15
  127.0 1.0 copy-start.3
  128.0 0.8 copy-start.9
  128.9 0.8 copy-start.11
  129.7 0.8 copy-start.13
  135.0 1.4 copy-start.2
  136.4 21.4 %collective-permute-start = (bf16[4,768,384]{2,1,0:T(8,128)(2,1)}, bf16[4,768,384]{2,1,0:T(8,128)(2,1)}, u32[]{:S(2)}, u32[]{:S(2)}) collective-permute-start(bf16[4,768,384]{2,1,0:T(8,128)(2,1)} %get-tuple-element.32), channel_id=1, source_target_pairs={{0,1},{1,0},{2,3},{3,2},{4,5},{5,4},{6,7},{7,6},{8,9},{9,8},{10,11... | collective-permute-start | bytes 7077896 | tf_op jit(solution)/shard_map/ppermute | solution.py:263
  137.8 2.3 copy-start.1
  140.1 5.3 %copy-start.4 = (f32[18,128,128]{2,1,0:T(8,128)S(1)}, f32[18,128,128]{2,1,0:T(8,128)}, u32[]{:S(2)}) copy-start(f32[18,128,128]{2,1,0:T(8,128)} %copy-done.3) | copy-start | bytes 3538948
  140.1 5.3 %copy-start.10 = (bf16[192,1536]{1,0:T(8,128)(2,1)S(1)}, bf16[192,1536]{1,0:T(8,128)(2,1)}, u32[]{:S(2)}) copy-start(bf16[192,1536]{1,0:T(8,128)(2,1)} %copy-done.9) | copy-start | bytes 1769476
  140.1 5.3 %copy-start.12 = (bf16[192,1536]{1,0:T(8,128)(2,1)S(1)}, bf16[192,1536]{1,0:T(8,128)(2,1)}, u32[]{:S(2)}) copy-start(bf16[192,1536]{1,0:T(8,128)(2,1)} %copy-done.11) | copy-start | bytes 1769476
  140.1 5.3 %copy-start.14 = (bf16[192,1536]{1,0:T(8,128)(2,1)S(1)}, bf16[192,1536]{1,0:T(8,128)(2,1)}, u32[]{:S(2)}) copy-start(bf16[192,1536]{1,0:T(8,128)(2,1)} %copy-done.13) | copy-start | bytes 1769476
  151.5 90.2 %all-to-all-start.1 = ((bf16[64,8,2304]{2,1,0:T(8,128)(2,1)}), bf16[64,8,2304]{2,1,0:T(8,128)(2,1)S(1)}, u32[]{:S(2)}, u32[]{:S(2)}) async-start(bf16[64,8,2304]{2,1,0:T(8,128)(2,1)} %bitcast.7), calls=%async_computation.1 | async-start | bytes 4718592 | tf_op jit(solution)/shard_map/all_to_all | solution.py:283
  160.1 17.8 %collective-permute-start.3 = (bf16[768,384]{1,0:T(8,128)(2,1)S(1)}, bf16[768,384]{1,0:T(8,128)(2,1)S(1)}, u32[]{:S(2)}, u32[]{:S(2)}) collective-permute-start(bf16[768,384]{1,0:T(8,128)(2,1)S(1)} %get-tuple-element.34), channel_id=1, source_target_pairs={{0,128},{64,192},{128,0},{192,64},{1,129},{65,193},{129,1},{193,65... | collective-permute-start | bytes 1769480 | tf_op jit(solution)/shard_map/ppermute | solution.py:265
  163.2 26.6 %collective-permute-start.2 = (bf16[768,384]{1,0:T(8,128)(2,1)S(1)}, bf16[768,384]{1,0:T(8,128)(2,1)S(1)}, u32[]{:S(2)}, u32[]{:S(2)}) collective-permute-start(bf16[768,384]{1,0:T(8,128)(2,1)S(1)} %get-tuple-element.35), channel_id=1, source_target_pairs={{0,192},{64,0},{128,64},{192,128},{1,193},{65,1},{129,65},{193,129... | collective-permute-start | bytes 1769480 | tf_op jit(solution)/shard_map/ppermute | solution.py:265
  164.4 25.4 %collective-permute-start.1 = (bf16[768,384]{1,0:T(8,128)(2,1)S(1)}, bf16[768,384]{1,0:T(8,128)(2,1)S(1)}, u32[]{:S(2)}, u32[]{:S(2)}) collective-permute-start(bf16[768,384]{1,0:T(8,128)(2,1)S(1)} %get-tuple-element.33), channel_id=1, source_target_pairs={{0,64},{64,128},{128,192},{192,0},{1,65},{65,129},{129,193},{193,1... | collective-permute-start | bytes 1769480 | tf_op jit(solution)/shard_map/ppermute | solution.py:265
  191.5 11.2 %collective-permute-start.6 = (bf16[192,384]{1,0:T(8,128)(2,1)S(1)}, bf16[192,384]{1,0:T(8,128)(2,1)S(1)}, u32[]{:S(2)}, u32[]{:S(2)}) collective-permute-start(bf16[192,384]{1,0:T(8,128)(2,1)S(1)} %get-tuple-element.37), channel_id=1, source_target_pairs={{0,32},{1,33},{2,34},{3,35},{4,36},{5,37},{6,38},{7,39},{8,40},{9,... | collective-permute-start | bytes 442376 | tf_op jit(solution)/shard_map/ppermute | solution.py:267
  193.9 14.4 %collective-permute-start.5 = (bf16[192,384]{1,0:T(8,128)(2,1)S(1)}, bf16[192,384]{1,0:T(8,128)(2,1)S(1)}, u32[]{:S(2)}, u32[]{:S(2)}) collective-permute-start(bf16[192,384]{1,0:T(8,128)(2,1)S(1)} %get-tuple-element.38), channel_id=1, source_target_pairs={{0,48},{1,49},{2,50},{3,51},{4,52},{5,53},{6,54},{7,55},{8,56},{9,... | collective-permute-start | bytes 442376 | tf_op jit(solution)/shard_map/ppermute | solution.py:267
  195.3 13.1 %collective-permute-start.4 = (bf16[192,384]{1,0:T(8,128)(2,1)S(1)}, bf16[192,384]{1,0:T(8,128)(2,1)S(1)}, u32[]{:S(2)}, u32[]{:S(2)}) collective-permute-start(bf16[192,384]{1,0:T(8,128)(2,1)S(1)} %get-tuple-element.36), channel_id=1, source_target_pairs={{0,16},{1,17},{2,18},{3,19},{4,20},{5,21},{6,22},{7,23},{8,24},{9,... | collective-permute-start | bytes 442376 | tf_op jit(solution)/shard_map/ppermute | solution.py:267
  208.5 14.1 %collective-permute-start.13 = (bf16[24,384]{1,0:T(8,128)(2,1)S(1)}, bf16[24,384]{1,0:T(8,128)(2,1)S(1)}, u32[]{:S(2)}, u32[]{:S(2)}) collective-permute-start(bf16[24,384]{1,0:T(8,128)(2,1)S(1)} %get-tuple-element.40), channel_id=1, source_target_pairs={{0,8},{1,9},{2,10},{3,11},{4,12},{5,13},{6,14},{7,15},{8,0},{9,1},... | collective-permute-start | bytes 55304 | tf_op jit(solution)/shard_map/ppermute | solution.py:269
  215.8 8.6 %collective-permute-start.12 = (bf16[24,384]{1,0:T(8,128)(2,1)S(1)}, bf16[24,384]{1,0:T(8,128)(2,1)S(1)}, u32[]{:S(2)}, u32[]{:S(2)}) collective-permute-start(bf16[24,384]{1,0:T(8,128)(2,1)S(1)} %get-tuple-element.41), channel_id=1, source_target_pairs={{0,10},{1,11},{2,12},{3,13},{4,14},{5,15},{6,0},{7,1},{8,2},{9,3},... | collective-permute-start | bytes 55304 | tf_op jit(solution)/shard_map/ppermute | solution.py:269
  215.8 8.9 %collective-permute-start.11 = (bf16[24,384]{1,0:T(8,128)(2,1)S(1)}, bf16[24,384]{1,0:T(8,128)(2,1)S(1)}, u32[]{:S(2)}, u32[]{:S(2)}) collective-permute-start(bf16[24,384]{1,0:T(8,128)(2,1)S(1)} %get-tuple-element.42), channel_id=1, source_target_pairs={{0,6},{1,7},{2,8},{3,9},{4,10},{5,11},{6,12},{7,13},{8,14},{9,15},... | collective-permute-start | bytes 55304 | tf_op jit(solution)/shard_map/ppermute | solution.py:269
  219.7 5.1 %collective-permute-start.10 = (bf16[24,384]{1,0:T(8,128)(2,1)S(1)}, bf16[24,384]{1,0:T(8,128)(2,1)S(1)}, u32[]{:S(2)}, u32[]{:S(2)}) collective-permute-start(bf16[24,384]{1,0:T(8,128)(2,1)S(1)} %get-tuple-element.43), channel_id=1, source_target_pairs={{0,12},{1,13},{2,14},{3,15},{4,0},{5,1},{6,2},{7,3},{8,4},{9,5},{1... | collective-permute-start | bytes 55304 | tf_op jit(solution)/shard_map/ppermute | solution.py:269
  220.3 5.9 %collective-permute-start.9 = (bf16[24,384]{1,0:T(8,128)(2,1)S(1)}, bf16[24,384]{1,0:T(8,128)(2,1)S(1)}, u32[]{:S(2)}, u32[]{:S(2)}) collective-permute-start(bf16[24,384]{1,0:T(8,128)(2,1)S(1)} %get-tuple-element.44), channel_id=1, source_target_pairs={{0,4},{1,5},{2,6},{3,7},{4,8},{5,9},{6,10},{7,11},{8,12},{9,13},{1... | collective-permute-start | bytes 55304 | tf_op jit(solution)/shard_map/ppermute | solution.py:269
  222.6 3.8 %collective-permute-start.8 = (bf16[24,384]{1,0:T(8,128)(2,1)S(1)}, bf16[24,384]{1,0:T(8,128)(2,1)S(1)}, u32[]{:S(2)}, u32[]{:S(2)}) collective-permute-start(bf16[24,384]{1,0:T(8,128)(2,1)S(1)} %get-tuple-element.45), channel_id=1, source_target_pairs={{0,14},{1,15},{2,0},{3,1},{4,2},{5,3},{6,4},{7,5},{8,6},{9,7},{10,... | collective-permute-start | bytes 55304 | tf_op jit(solution)/shard_map/ppermute | solution.py:269
  224.4 5.0 %collective-permute-start.7 = (bf16[24,384]{1,0:T(8,128)(2,1)S(1)}, bf16[24,384]{1,0:T(8,128)(2,1)S(1)}, u32[]{:S(2)}, u32[]{:S(2)}) collective-permute-start(bf16[24,384]{1,0:T(8,128)(2,1)S(1)} %get-tuple-element.39), channel_id=1, source_target_pairs={{0,2},{1,3},{2,4},{3,5},{4,6},{5,7},{6,8},{7,9},{8,10},{9,11},{10,... | collective-permute-start | bytes 55304 | tf_op jit(solution)/shard_map/ppermute | solution.py:269
Sparse Core Ops, SparseCore 0:
  9.9 41.6 all-gather.2
  53.4 77.0 all-gather.4
where the time goes:
time: 252 us
  waiting for transfers between devices  140 us (56%)
  starting transfers between devices  41.5 us (16%)
  Pallas kernels  26 us (10%)
  between operations  14.3 us (6%)
  local copies, waits for them, and re-layouts  12.4 us (5%)
  blocking collectives  12.3 us (5%)
  other arithmetic  5.02 us (2%)
    all_to_all x2, waiting for transfers between devices, exchange(): lax.all_to_all(message, 'seq', split_axis=0, concat_axis=0, tiled=True)  54.1 us
    all_gather x1, waiting for transfers between devices, gather_weight(): lax.all_gather(out_weight, 'seq', axis=0, tiled=True, axis_index_groups=r...  43.6 us
    ppermute x3, waiting for transfers between devices, reduce_weight(): lax.ppermute(parts[d], 'dp', [(i, (i + d) % NX) for i in range(NX)])  24.6 us
    ppermute x7, starting transfers between devices, reduce_weight(): lax.ppermute(column[d], 'seq', seq_shift(0, d, 0))  16.3 us
    all_to_all x2, starting transfers between devices, exchange(): lax.all_to_all(message, 'seq', split_axis=0, concat_axis=0, tiled=True)  14.3 us
    ppermute x3, waiting for transfers between devices, reduce_weight(): came = [lax.ppermute(chip[d], 'seq', seq_shift(d, 0, 0)) for d in (1, 3, 2)]  12.4 us
    all_gather x1, blocking collectives, reduce_weight(): return lax.all_gather(strip, 'dp', axis=1, tiled=True)  12.3 us
    unnamed x35, local copies, waits for them, and re-layouts  12.2 us
  transfers between devices with their start and end apart: 18, of which 9 were waited for; matrix products, arithmetic and copies ran while one was open for 2% of the time, Pallas kernels for 9%

commit v1 on v0

--- a/solution.py
+++ b/solution.py
@@ -84,7 +84,7 @@
         in_specs=[place_block] * 4,
         out_specs=message_block,
         out_shape=message_shape,
-        compiler_params=params(24),
+        compiler_params=params(60),
         name="pack",
     )(*arrays)
 
@@ -96,7 +96,7 @@
         in_specs=[message_block],
         out_specs=[place_block] * 4,
         out_shape=[rows_shape] * 4,
-        compiler_params=params(24),
+        compiler_params=params(60),
         name="unpack",
     )(message)
 
@@ -134,7 +134,7 @@
         in_specs=[pl.BlockSpec((128, 128), lambda j: (0, 0)), message_block],
         out_specs=[place_block] * 5 + [probs_block],
         out_shape=[rows_shape] * 5 + [jax.ShapeDtypeStruct((HEADS // 2 * PLACES, 128, 128), F32)],
-        compiler_params=params(32),
+        compiler_params=params(60),
         name="forward",
     )(mask, message)
 
@@ -147,7 +147,7 @@
             core = at[0] if side == 0 else 1 - at[0]
             for dy in range(NY):
                 for dz in range(NZ):
-                    y, z = (at[2] + dy) % NY, (at[3] + dz) % NZ
+                    y, z = (at[2] + dy) % NY, at[3] ^ dz
                     src = pl.multiple_of((y * NZ + z) * 2 * STRIP + core * STRIP, 8)
                     dst = (dy * NZ + dz) * STRIP
                     strips[side, dst : dst + STRIP, :] = turned[pl.ds(src, STRIP), :]
@@ -170,7 +170,7 @@
             scratch_shapes=[pltpu.VMEM((WIDTH, ROWS), F32), pltpu.VMEM((2, HALF, ROWS), F32)],
         ),
         out_shape=[jax.ShapeDtypeStruct((NX, HALF, QUARTER), BF)] * 2,
-        compiler_params=params(32),
+        compiler_params=params(60),
         name="weight",
     )(at, mixed, grad)
 
@@ -211,7 +211,7 @@
         ],
         out_shape=[rows_shape] * 2,
         scratch_shapes=[pltpu.VMEM((ROWS, WIDTH), F32)],
-        compiler_params=params(32),
+        compiler_params=params(60),
         name="project",
     )(mixed, grad, weight)
 
@@ -237,7 +237,7 @@
         out_specs=message_block,
         out_shape=message_shape,
         scratch_shapes=[pltpu.VMEM((FRAMES, WIDTH), BF)] * 3,
-        compiler_params=params(32),
+        compiler_params=params(60),
         name="backward",
     )(*arrays)
 
@@ -252,6 +252,13 @@
     ]
 
 
+def seq_flip(bit):
+    seq = np.arange(SEQ).reshape(NY, NZ, 2)
+    return [
+        (int(seq[y, z, c]), int(seq[y, z ^ bit, c])) for y in range(NY) for z in range(NZ) for c in range(2)
+    ]
+
+
 def add_up(parts):
     total = parts[0].astype(F32)
     for part in parts[1:]:
@@ -259,24 +266,34 @@
     return total
 
 
-def reduce_weight(keep, send):
-    came = lax.ppermute(send, "seq", seq_shift(0, 0, 1))
-    parts = [add_up([keep[d], came[d]]).astype(BF) for d in range(NX)]
+def reduce_chip(keep, came):
+    return [add_up([keep[d], came[d]]).astype(BF) for d in range(NX)]
+
+
+def reduce_rest(parts):
     came = [lax.ppermute(parts[d], "dp", [(i, (i + d) % NX) for i in range(NX)]) for d in (1, 3, 2)]
     chip = add_up([parts[0]] + came).astype(BF).reshape(NY, NZ * STRIP, QUARTER)
     came = [lax.ppermute(chip[d], "seq", seq_shift(d, 0, 0)) for d in (1, 3, 2)]
-    column = add_up([chip[0]] + came).astype(BF).reshape(NZ, STRIP, QUARTER)
-    came = [lax.ppermute(column[d], "seq", seq_shift(0, d, 0)) for d in (1, 7, 2, 6, 3, 5, 4)]
-    strip = add_up([column[0]] + came)
-    return lax.all_gather(strip, "dp", axis=1, tiled=True)
+    strips = add_up([chip[0]] + came).astype(BF).reshape(NZ, STRIP, QUARTER)
+    for bit in (4, 2, 1):
+        came = lax.ppermute(strips[bit:], "seq", seq_flip(bit))
+        strips = add_up([strips[:bit], came])
+        if bit > 1:
+            strips = strips.astype(BF)
+    own = strips[0]
+    came = {d: lax.ppermute(own, "dp", [(i, (i + d) % NX) for i in range(NX)]) for d in (1, 3, 2)}
+    place = lax.axis_index("dp")
+    quarters = [lax.select_n((place - n) % NX, own, came[1], came[2], came[3]) for n in range(NX)]
+    return jnp.concatenate(quarters, axis=1)
 
 
 def gather_weight(out_weight):
-    seq = np.arange(SEQ).reshape(NY, NZ * 2)
-    rows = [list(map(int, seq[y])) for y in range(NY)]
-    columns = [list(map(int, seq[:, n])) for n in range(NZ * 2)]
-    part = lax.all_gather(out_weight, "seq", axis=0, tiled=True, axis_index_groups=rows)
-    return lax.all_gather(part, "seq", axis=0, tiled=True, axis_index_groups=columns)
+    cores = [list(range(core, SEQ, 2)) for core in range(2)]
+    own = lax.all_gather(out_weight, "seq", axis=0, axis_index_groups=cores)
+    other = lax.ppermute(own, "seq", seq_shift(0, 0, 1))
+    first = lax.axis_index("seq") % 2 == 0
+    both = [jnp.where(first, own, other), jnp.where(first, other, own)]
+    return jnp.stack(both, axis=1).reshape(WIDTH, WIDTH)
 
 
 def exchange(message):
@@ -296,10 +313,12 @@
     arrived = exchange(pack_call(*flat))
     q, k, v, g, mixed, probs = forward_call(mask, arrived)
     keep, send = weight_call(at, mixed, g)
+    came = lax.ppermute(send, "seq", seq_shift(0, 0, 1))
     out, mixed_grad = project_call(mixed, g, weight)
+    parts, mixed_grad = lax.optimization_barrier((reduce_chip(keep, came), mixed_grad))
     message = backward_call(q, k, v, mixed, mixed_grad, out, probs)
     results = unpack_call(exchange(message))
-    weight_grad = reduce_weight(keep, send)
+    weight_grad = reduce_rest(parts)
     return tuple(x.reshape(queries.shape) for x in results) + (weight_grad,)
 
 

time: 252 us -> 243 us (0.964)
  Pallas kernels: 26 us -> 39.2 us
  blocking collectives: 12.3 us -> 0 us
  waiting for transfers between devices: 140 us -> 128 us
  local copies, waits for them, and re-layouts: 12.4 us -> 3.1 us
  other arithmetic: 5.02 us -> 11 us
  starting transfers between devices: 41.5 us -> 47 us
    all_to_all x2, waiting for transfers between devices: 54.1 us -> 0.01 us  [exchange(): lax.all_to_all(message, 'seq', split_axis=0, concat_axis=0, tiled=True)]
    all_gather x2 -> x1, waiting for transfers between devices: 43.6 us -> 75.9 us  [gather_weight(): own = lax.all_gather(out_weight, 'seq', axis=0, axis_index_groups=cores)]
    all_gather x1 -> x0, blocking collectives: 12.3 us -> none  [reduce_weight(): return lax.all_gather(strip, 'dp', axis=1, tiled=True)]
    ppermute x14, waiting for transfers between devices: 41.6 us -> 51 us  [the longest x3 25.4 us: reduce_rest(): lax.ppermute(parts[d], 'dp', [(i, (i + d) % NX) for i in range(NX)])]
    unnamed x35 -> x8, local copies, waits for them, and re-layouts: 12.2 us -> 2.88 us
    all_to_all x2, starting transfers between devices: 14.3 us -> 20.6 us  [exchange(): lax.all_to_all(message, 'seq', split_axis=0, concat_axis=0, tiled=True)]
    another operation x0 -> x2, other arithmetic: none -> 5.27 us  [gather_weight(): return jnp.stack(both, axis=1).reshape(WIDTH, WIDTH)]
    pallas_call x1, Pallas kernels: 1.26 us -> 4.71 us  [pack_call(): pl.pallas_call(pack_kernel, grid=(PLACES,), in_specs=[place_block] * 4, o...]
  transfers between devices with their start and end apart: 18 -> 17, of which waited for: 9 -> 12; matrix products, arithmetic and copies ran while one was open for 2% -> 3% of each run, Pallas kernels for 9% -> 11%
where the time goes in v1:
time: 243 us; the launch traced here: 242 us
  waiting for transfers between devices  128 us (53%)
  starting transfers between devices  47 us (19%)
  Pallas kernels  39.2 us (16%)
  between operations  14.2 us (6%)
  other arithmetic  11 us (5%)
  local copies, waits for them, and re-layouts  3.1 us (1%)
    all_gather x1, waiting for transfers between devices, gather_weight(): own = lax.all_gather(out_weight, 'seq', axis=0, axis_index_groups=cores)  75.9 us
    ppermute x3, waiting for transfers between devices, reduce_rest(): lax.ppermute(parts[d], 'dp', [(i, (i + d) % NX) for i in range(NX)])  25.4 us
    all_to_all x2, starting transfers between devices, exchange(): lax.all_to_all(message, 'seq', split_axis=0, concat_axis=0, tiled=True)  20.6 us
    ppermute x3, waiting for transfers between devices, reduce_rest(): came = lax.ppermute(strips[bit:], 'seq', seq_flip(bit))  12.1 us
    ppermute x3, waiting for transfers between devices, reduce_rest(): came = [lax.ppermute(chip[d], 'seq', seq_shift(d, 0, 0)) for d in (1, 3, 2)]  11 us
    ppermute x3, starting transfers between devices, reduce_rest(): came = lax.ppermute(strips[bit:], 'seq', seq_flip(bit))  10 us
    pallas_call x1, Pallas kernels, project_call(): pl.pallas_call(project_kernel, grid=(WIDTH // depth,), in_specs=[pl.Block...  8.32 us
    pallas_call x1, Pallas kernels, forward_call(): pl.pallas_call(forward_kernel, grid=(PLACES,), in_specs=[pl.BlockSpec((12...  8.27 us
  transfers between devices with their start and end apart: 17, of which 12 were waited for; matrix products, arithmetic and copies ran while one was open for 3% of the time, Pallas kernels for 11%

profile of v1, /device:TPU:8, one launch (start us, length us, event | category | flops | bytes accessed | tf_op | source)
XLA Modules:
  0.0 242.1 jit_solution(13783903830039755931)
XLA Ops:
  7.2 0.0 all-gather.3.cloned.1.call-start
  7.2 0.7 all-gather.3.cloned.1.call-update
  7.9 4.7 %pack.1 = bf16[512,2304]{1,0:T(8,128)(2,1)} custom-call(bf16[192,1536]{1,0:T(8,128)(2,1)} %bitcast.53, bf16[192,1536]{1,0:T(8,128)(2,1)} %bitcast.54, bf16[192,1536]{1,0:T(8,128)(2,1)} %bitcast.55, bf16[192,1536]{1,0:T(8,128)(2,1)} %bitcast.56), custom_call_target="tpu_custom_call" | custom-call | tf_op jit(solution)/shard_map/pack/pallas_call | solution.py:81
  12.6 0.0 copy-start.3
  12.6 12.2 %all-to-all-start = ((bf16[64,8,2304]{2,1,0:T(8,128)(2,1)}), bf16[64,8,2304]{2,1,0:T(8,128)(2,1)S(1)}, u32[]{:S(2)}, u32[]{:S(2)}) async-start(bf16[64,8,2304]{2,1,0:T(8,128)(2,1)} %bitcast.50), calls=%async_computation | async-start | bytes 4718592 | tf_op jit(solution)/shard_map/all_to_all | solution.py:300
  24.9 75.9 %all-gather.3.cloned.1.call-done = bf16[768,1536]{1,0:T(8,128)(2,1)} async-done(((bf16[24,1536]{1,0:T(8,128)(2,1)}), bf16[768,1536]{1,0:T(8,128)(2,1)}) %all-gather.3.cloned.1.call-update) | async-done | bytes 2359312 | tf_op jit(solution)/shard_map/all_gather | solution.py:292
  100.8 0.0 collective-permute-start.1
  100.8 0.0 copy-done.3
  100.8 0.1 broadcast_compare_fusion
  100.9 0.1 tile.10
  101.0 0.6 pad_add_fusion.at
  101.6 0.7 and_convert_fusion.mask_ref
  102.3 0.0 all-to-all-done
  102.3 0.0 copy-start.1
  102.3 1.5 copy-done.1
  103.8 8.3 %forward.1 = (bf16[192,1536]{1,0:T(8,128)(2,1)}, bf16[192,1536]{1,0:T(8,128)(2,1)}, bf16[192,1536]{1,0:T(8,128)(2,1)}, bf16[192,1536]{1,0:T(8,128)(2,1)}, bf16[1...) custom-call(f32[128,128]{1,0:T(8,128)} %and_convert_fusion.mask_ref, bf16[512,2304]{1,0:T(8,128)(2,1)} %bitcast.49), custom_call_target="tpu_custom_call" | custom-call | tf_op jit(solution)/shard_map/forward/pallas_call | solution.py:131
  112.1 5.9 %weight.1 = (bf16[4,768,384]{2,1,0:T(8,128)(2,1)}, bf16[4,768,384]{2,1,0:T(8,128)(2,1)}) custom-call(s32[4]{0:T(128)} %pad_add_fusion.at, bf16[192,1536]{1,0:T(8,128)(2,1)} %get-tuple-element.27.mixed, bf16[192,1536]{1,0:T(8,128)(2,1)} %get-tuple-element.28.grad), custom_call_target="tpu_custom_call" | custom-call | tf_op jit(solution)/shard_map/weight/pallas_call | solution.py:160
  118.0 0.5 collective-permute-start
  118.5 0.0 collective-permute-done.1
  118.5 2.7 %select_bitcast_fusion.1 = (bf16[32,1,24,1536]{3,2,1,0:T(8,128)(2,1)S(1)}, bf16[32,1,24,1536]{3,2,1,0:T(8,128)(2,1)S(1)}) fusion(bf16[32,24,1536]{2,1,0:T(8,128)(2,1)} %bitcast.52, bf16[32,24,1536]{2,1,0:T(8,128)(2,1)} %collective-permute-done.1, pred[]{:T(512)S(6)} %eq.50), kind=kLoop, calls=%fused_computation.2 | loop fusion | flops 2359296 | bytes 9437185 | tf_op jit(solution)/shard_map/stack | solution.py:296
  121.2 2.6 %pad_maximum_fusion = bf16[32,2,24,1536]{3,2,1,0:T(8,128)(2,1)} fusion(bf16[32,1,24,1536]{3,2,1,0:T(8,128)(2,1)S(1)} %get-tuple-element.44, bf16[32,1,24,1536]{3,2,1,0:T(8,128)(2,1)S(1)} %get-tuple-element.43), kind=kLoop, calls=%fused_computation | loop fusion | flops 2359296 | bytes 9437184 | tf_op jit(solution)/shard_map/stack | solution.py:296
  123.8 0.0 copy-start.2
  123.8 8.3 %project.1 = (bf16[192,1536]{1,0:T(8,128)(2,1)}, bf16[192,1536]{1,0:T(8,128)(2,1)}) custom-call(bf16[192,1536]{1,0:T(8,128)(2,1)} %get-tuple-element.27.mixed, bf16[192,1536]{1,0:T(8,128)(2,1)} %get-tuple-element.28.grad, bf16[1536,1536]{1,0:T(8,128)(2,1)} %bitcast.46), custom_call_target="tpu_custom_call" | custom-call | tf_op jit(solution)/shard_map/project/pallas_call | solution.py:200
  132.1 0.0 collective-permute-done
  132.1 0.0 copy-done.2
  132.1 3.2 %fusion.3 = (bf16[768,384]{1,0:T(8,128)(2,1)}, bf16[768,384]{1,0:T(8,128)(2,1)S(1)}, bf16[768,384]{1,0:T(8,128)(2,1)}, bf16[768,384]{1,0:T(8,128)(2,1)S(1)}) fusion(bf16[4,768,384]{2,1,0:T(8,128)(2,1)} %collective-permute-done, bf16[4,768,384]{2,1,0:T(8,128)(2,1)S(1)} %copy-done.2), kind=kLoop, calls=%fused_computation.11 | loop fusion | flops 4718592 | bytes 7077888 | tf_op jit(solution)/shard_map/convert_element_type | solution.py:270
  135.3 7.6 %backward.1 = bf16[512,2304]{1,0:T(8,128)(2,1)} custom-call(bf16[192,1536]{1,0:T(8,128)(2,1)} %get-tuple-element.24.q, bf16[192,1536]{1,0:T(8,128)(2,1)} %get-tuple-element.25.k, bf16[192,1536]{1,0:T(8,128)(2,1)} %get-tuple-element.26.v, bf16[192,1536]{1,0:T(8,128)(2,1)} %get-tuple-element.27.mixed, bf16[192,1536]{1,0:T(8,128)(2,1)} %get-tuple-element.32.mixed_grad, ...), custom_call_target="tpu_custom_call" | custom-call | tf_op jit(solution)/shard_map/backward/pallas_call | solution.py:233
  142.9 8.3 %all-to-all-start.1 = ((bf16[64,8,2304]{2,1,0:T(8,128)(2,1)}), bf16[64,8,2304]{2,1,0:T(8,128)(2,1)S(1)}, u32[]{:S(2)}, u32[]{:S(2)}) async-start(bf16[64,8,2304]{2,1,0:T(8,128)(2,1)} %bitcast.47), calls=%async_computation.1 | async-start | bytes 4718592 | tf_op jit(solution)/shard_map/all_to_all | solution.py:300
  151.3 1.6 collective-permute-start.2
  152.8 1.8 collective-permute-start.3
  154.6 1.9 collective-permute-start.4
  156.4 11.7 %collective-permute-done.2 = bf16[768,384]{1,0:T(8,128)(2,1)S(1)} collective-permute-done((bf16[768,384]{1,0:T(8,128)(2,1)}, bf16[768,384]{1,0:T(8,128)(2,1)S(1)}, u32[]{:S(2)}, u32[]{:S(2)}) %collective-permute-start.2) | collective-permute-done | bytes 589856 | tf_op jit(solution)/shard_map/ppermute | solution.py:274
  168.1 12.0 %collective-permute-done.3 = bf16[768,384]{1,0:T(8,128)(2,1)S(1)} collective-permute-done((bf16[768,384]{1,0:T(8,128)(2,1)}, bf16[768,384]{1,0:T(8,128)(2,1)S(1)}, u32[]{:S(2)}, u32[]{:S(2)}) %collective-permute-start.3) | collective-permute-done | bytes 589856 | tf_op jit(solution)/shard_map/ppermute | solution.py:274
  180.2 1.6 collective-permute-done.4
  181.8 0.3 add_convert_fusion
  182.2 1.8 collective-permute-start.5
  184.0 0.5 collective-permute-start.6
  184.5 2.3 collective-permute-start.7
  186.8 4.4 %collective-permute-done.5 = bf16[192,384]{1,0:T(8,128)(2,1)S(1)} collective-permute-done((bf16[192,384]{1,0:T(8,128)(2,1)S(1)}, bf16[192,384]{1,0:T(8,128)(2,1)S(1)}, u32[]{:S(2)}, u32[]{:S(2)}) %collective-permute-start.5) | collective-permute-done | bytes 147488 | tf_op jit(solution)/shard_map/ppermute | solution.py:276
  191.2 1.0 collective-permute-done.6
  192.3 5.5 %collective-permute-done.7 = bf16[192,384]{1,0:T(8,128)(2,1)S(1)} collective-permute-done((bf16[192,384]{1,0:T(8,128)(2,1)S(1)}, bf16[192,384]{1,0:T(8,128)(2,1)S(1)}, u32[]{:S(2)}, u32[]{:S(2)}) %collective-permute-start.7) | collective-permute-done | bytes 147488 | tf_op jit(solution)/shard_map/ppermute | solution.py:276
  197.8 0.1 add_convert_fusion.5
  197.9 8.8 %collective-permute-start.8 = (bf16[4,24,384]{2,1,0:T(8,128)(2,1)S(1)}, bf16[4,24,384]{2,1,0:T(8,128)(2,1)S(1)}, u32[]{:S(2)}, u32[]{:S(2)}) collective-permute-start(bf16[4,24,384]{2,1,0:T(8,128)(2,1)S(1)} %bitcast.58), channel_id=1, source_target_pairs={{0,8},{1,9},{2,10},{3,11},{4,12},{5,13},{6,14},{7,15},{8,0},{9,1},... | collective-permute-start | bytes 221192 | tf_op jit(solution)/shard_map/ppermute | solution.py:279
  206.7 4.5 %collective-permute-done.8 = bf16[4,24,384]{2,1,0:T(8,128)(2,1)S(1)} collective-permute-done((bf16[4,24,384]{2,1,0:T(8,128)(2,1)S(1)}, bf16[4,24,384]{2,1,0:T(8,128)(2,1)S(1)}, u32[]{:S(2)}, u32[]{:S(2)}) %collective-permute-start.8) | collective-permute-done | bytes 73760 | tf_op jit(solution)/shard_map/ppermute | solution.py:279
  211.3 0.1 collective-permute-start.9
  211.4 4.9 %collective-permute-done.9 = bf16[2,24,384]{2,1,0:T(8,128)(2,1)S(1)} collective-permute-done((bf16[2,24,384]{2,1,0:T(8,128)(2,1)S(1)}, bf16[2,24,384]{2,1,0:T(8,128)(2,1)S(1)}, u32[]{:S(2)}, u32[]{:S(2)}) %collective-permute-start.9) | collective-permute-done | bytes 36896 | tf_op jit(solution)/shard_map/ppermute | solution.py:279
  216.2 1.1 collective-permute-start.10
  217.3 2.7 %collective-permute-done.10 = bf16[1,24,384]{2,1,0:T(8,128)(2,1)S(1)} collective-permute-done((bf16[1,24,384]{2,1,0:T(8,128)(2,1)S(1)}, bf16[1,24,384]{2,1,0:T(8,128)(2,1)S(1)}, u32[]{:S(2)}, u32[]{:S(2)}) %collective-permute-start.10) | collective-permute-done | bytes 18464 | tf_op jit(solution)/shard_map/ppermute | solution.py:279
  220.1 1.9 collective-permute-start.11
  222.0 2.8 %collective-permute-start.12 = (f32[24,384]{1,0:T(8,128)S(1)}, f32[24,384]{1,0:T(8,128)S(1)}, u32[]{:S(2)}, u32[]{:S(2)}) collective-permute-start(f32[24,384]{1,0:T(8,128)S(1)} %add_bitcast_fusion), channel_id=1, source_target_pairs={{0,128},{64,192},{128,0},{192,64},{1,129},{65,193},{129,1},{193,65... | collective-permute-start | bytes 110600 | tf_op jit(solution)/shard_map/ppermute | solution.py:284
  224.8 1.4 collective-permute-start.13
  226.2 0.0 collective-permute-done.11
  226.2 1.2 collective-permute-done.12
  227.4 1.3 collective-permute-done.13
  228.8 0.7 pad_maximum_fusion.1
  229.4 0.0 all-to-all-done.1
  229.5 0.0 copy-start
  229.5 1.4 copy-done
  230.9 4.4 %unpack.1 = (bf16[192,1536]{1,0:T(8,128)(2,1)}, bf16[192,1536]{1,0:T(8,128)(2,1)}, bf16[192,1536]{1,0:T(8,128)(2,1)}, bf16[192,1536]{1,0:T(8,128)(2,1)}) custom-call(bf16[512,2304]{1,0:T(8,128)(2,1)} %bitcast.48), custom_call_target="tpu_custom_call" | custom-call | tf_op jit(solution)/shard_map/unpack/pallas_call | solution.py:93
  (11 shorter events, 0.2 us)
Async XLA Ops:
  7.2 93.6 %all-gather.3.cloned.1.call-start = ((), (), s32[]{:S(2)}) async-start(), calls=%async_computation.2 | async-start | bytes 2433024 | tf_op jit(solution)/shard_map/all_gather | solution.py:292
  12.6 88.2 %copy-start.3 = (s32[1,64]{1,0:T(1,128)S(1)}, s32[1,64]{1,0:T(1,128)}, u32[]{:S(2)}) copy-start(s32[1,64]{1,0:T(1,128)} %param.11) | copy-start | bytes 772
  12.6 89.7 %all-to-all-start = ((bf16[64,8,2304]{2,1,0:T(8,128)(2,1)}), bf16[64,8,2304]{2,1,0:T(8,128)(2,1)S(1)}, u32[]{:S(2)}, u32[]{:S(2)}) async-start(bf16[64,8,2304]{2,1,0:T(8,128)(2,1)} %bitcast.50), calls=%async_computation | async-start | bytes 4718592 | tf_op jit(solution)/shard_map/all_to_all | solution.py:300
  100.8 17.7 %collective-permute-start.1 = (bf16[32,24,1536]{2,1,0:T(8,128)(2,1)}, bf16[32,24,1536]{2,1,0:T(8,128)(2,1)}, u32[]{:S(2)}, u32[]{:S(2)}) collective-permute-start(bf16[32,24,1536]{2,1,0:T(8,128)(2,1)} %bitcast.51), channel_id=1, source_target_pairs={{0,1},{1,0},{2,3},{3,2},{4,5},{5,4},{6,7},{7,6},{8,9},{9,8},{10,11... | collective-permute-start | bytes 7077896 | tf_op jit(solution)/shard_map/ppermute | solution.py:293
  102.3 1.5 copy-start.1
  118.0 14.1 %collective-permute-start = (bf16[4,768,384]{2,1,0:T(8,128)(2,1)}, bf16[4,768,384]{2,1,0:T(8,128)(2,1)}, u32[]{:S(2)}, u32[]{:S(2)}) collective-permute-start(bf16[4,768,384]{2,1,0:T(8,128)(2,1)} %get-tuple-element.30), channel_id=1, source_target_pairs={{0,1},{1,0},{2,3},{3,2},{4,5},{5,4},{6,7},{7,6},{8,9},{9,8},{10,11... | collective-permute-start | bytes 7077896 | tf_op jit(solution)/shard_map/ppermute | solution.py:316
  123.8 8.3 %copy-start.2 = (bf16[4,768,384]{2,1,0:T(8,128)(2,1)S(1)}, bf16[4,768,384]{2,1,0:T(8,128)(2,1)}, u32[]{:S(2)}) copy-start(bf16[4,768,384]{2,1,0:T(8,128)(2,1)} %get-tuple-element.29) | copy-start | bytes 7077892
  142.9 86.5 %all-to-all-start.1 = ((bf16[64,8,2304]{2,1,0:T(8,128)(2,1)}), bf16[64,8,2304]{2,1,0:T(8,128)(2,1)S(1)}, u32[]{:S(2)}, u32[]{:S(2)}) async-start(bf16[64,8,2304]{2,1,0:T(8,128)(2,1)} %bitcast.47), calls=%async_computation.1 | async-start | bytes 4718592 | tf_op jit(solution)/shard_map/all_to_all | solution.py:300
  151.3 16.9 %collective-permute-start.2 = (bf16[768,384]{1,0:T(8,128)(2,1)}, bf16[768,384]{1,0:T(8,128)(2,1)S(1)}, u32[]{:S(2)}, u32[]{:S(2)}) collective-permute-start(bf16[768,384]{1,0:T(8,128)(2,1)} %get-tuple-element.40), channel_id=1, source_target_pairs={{0,64},{64,128},{128,192},{192,0},{1,65},{65,129},{129,193},{193,1... | collective-permute-start | bytes 1769480 | tf_op jit(solution)/shard_map/ppermute | solution.py:274
  152.8 27.4 %collective-permute-start.3 = (bf16[768,384]{1,0:T(8,128)(2,1)}, bf16[768,384]{1,0:T(8,128)(2,1)S(1)}, u32[]{:S(2)}, u32[]{:S(2)}) collective-permute-start(bf16[768,384]{1,0:T(8,128)(2,1)} %get-tuple-element.41), channel_id=1, source_target_pairs={{0,192},{64,0},{128,64},{192,128},{1,193},{65,1},{129,65},{193,129... | collective-permute-start | bytes 1769480 | tf_op jit(solution)/shard_map/ppermute | solution.py:274
  154.6 27.3 %collective-permute-start.4 = (bf16[768,384]{1,0:T(8,128)(2,1)S(1)}, bf16[768,384]{1,0:T(8,128)(2,1)S(1)}, u32[]{:S(2)}, u32[]{:S(2)}) collective-permute-start(bf16[768,384]{1,0:T(8,128)(2,1)S(1)} %get-tuple-element.42), channel_id=1, source_target_pairs={{0,128},{64,192},{128,0},{192,64},{1,129},{65,193},{129,1},{193,65... | collective-permute-start | bytes 1769480 | tf_op jit(solution)/shard_map/ppermute | solution.py:274
  182.2 9.0 %collective-permute-start.5 = (bf16[192,384]{1,0:T(8,128)(2,1)S(1)}, bf16[192,384]{1,0:T(8,128)(2,1)S(1)}, u32[]{:S(2)}, u32[]{:S(2)}) collective-permute-start(bf16[192,384]{1,0:T(8,128)(2,1)S(1)} %get-tuple-element.49), channel_id=1, source_target_pairs={{0,16},{1,17},{2,18},{3,19},{4,20},{5,21},{6,22},{7,23},{8,24},{9,... | collective-permute-start | bytes 442376 | tf_op jit(solution)/shard_map/ppermute | solution.py:276
  184.0 8.2 %collective-permute-start.6 = (bf16[192,384]{1,0:T(8,128)(2,1)S(1)}, bf16[192,384]{1,0:T(8,128)(2,1)S(1)}, u32[]{:S(2)}, u32[]{:S(2)}) collective-permute-start(bf16[192,384]{1,0:T(8,128)(2,1)S(1)} %get-tuple-element.51), channel_id=1, source_target_pairs={{0,48},{1,49},{2,50},{3,51},{4,52},{5,53},{6,54},{7,55},{8,56},{9,... | collective-permute-start | bytes 442376 | tf_op jit(solution)/shard_map/ppermute | solution.py:276
  184.5 13.3 %collective-permute-start.7 = (bf16[192,384]{1,0:T(8,128)(2,1)S(1)}, bf16[192,384]{1,0:T(8,128)(2,1)S(1)}, u32[]{:S(2)}, u32[]{:S(2)}) collective-permute-start(bf16[192,384]{1,0:T(8,128)(2,1)S(1)} %get-tuple-element.50), channel_id=1, source_target_pairs={{0,32},{1,33},{2,34},{3,35},{4,36},{5,37},{6,38},{7,39},{8,40},{9,... | collective-permute-start | bytes 442376 | tf_op jit(solution)/shard_map/ppermute | solution.py:276
  197.9 13.4 %collective-permute-start.8 = (bf16[4,24,384]{2,1,0:T(8,128)(2,1)S(1)}, bf16[4,24,384]{2,1,0:T(8,128)(2,1)S(1)}, u32[]{:S(2)}, u32[]{:S(2)}) collective-permute-start(bf16[4,24,384]{2,1,0:T(8,128)(2,1)S(1)} %bitcast.58), channel_id=1, source_target_pairs={{0,8},{1,9},{2,10},{3,11},{4,12},{5,13},{6,14},{7,15},{8,0},{9,1},... | collective-permute-start | bytes 221192 | tf_op jit(solution)/shard_map/ppermute | solution.py:279
  211.3 5.0 %collective-permute-start.9 = (bf16[2,24,384]{2,1,0:T(8,128)(2,1)S(1)}, bf16[2,24,384]{2,1,0:T(8,128)(2,1)S(1)}, u32[]{:S(2)}, u32[]{:S(2)}) collective-permute-start(bf16[2,24,384]{2,1,0:T(8,128)(2,1)S(1)} %slice.92), channel_id=1, source_target_pairs={{0,4},{1,5},{2,6},{3,7},{4,0},{5,1},{6,2},{7,3},{8,12},{9,13},{10,... | collective-permute-start | bytes 110600 | tf_op jit(solution)/shard_map/ppermute | solution.py:279
  216.2 3.8 %collective-permute-start.10 = (bf16[1,24,384]{2,1,0:T(8,128)(2,1)S(1)}, bf16[1,24,384]{2,1,0:T(8,128)(2,1)S(1)}, u32[]{:S(2)}, u32[]{:S(2)}) collective-permute-start(bf16[1,24,384]{2,1,0:T(8,128)(2,1)S(1)} %slice.94), channel_id=1, source_target_pairs={{0,2},{1,3},{2,0},{3,1},{4,6},{5,7},{6,4},{7,5},{8,10},{9,11},{10,... | collective-permute-start | bytes 55304 | tf_op jit(solution)/shard_map/ppermute | solution.py:279
  220.1 6.1 %collective-permute-start.11 = (f32[24,384]{1,0:T(8,128)S(1)}, f32[24,384]{1,0:T(8,128)S(1)}, u32[]{:S(2)}, u32[]{:S(2)}) collective-permute-start(f32[24,384]{1,0:T(8,128)S(1)} %add_bitcast_fusion), channel_id=1, source_target_pairs={{0,64},{64,128},{128,192},{192,0},{1,65},{65,129},{129,193},{193,1... | collective-permute-start | bytes 110600 | tf_op jit(solution)/shard_map/ppermute | solution.py:284
  222.0 5.5 %collective-permute-start.12 = (f32[24,384]{1,0:T(8,128)S(1)}, f32[24,384]{1,0:T(8,128)S(1)}, u32[]{:S(2)}, u32[]{:S(2)}) collective-permute-start(f32[24,384]{1,0:T(8,128)S(1)} %add_bitcast_fusion), channel_id=1, source_target_pairs={{0,128},{64,192},{128,0},{192,64},{1,129},{65,193},{129,1},{193,65... | collective-permute-start | bytes 110600 | tf_op jit(solution)/shard_map/ppermute | solution.py:284
  224.8 4.0 %collective-permute-start.13 = (f32[24,384]{1,0:T(8,128)S(1)}, f32[24,384]{1,0:T(8,128)S(1)}, u32[]{:S(2)}, u32[]{:S(2)}) collective-permute-start(f32[24,384]{1,0:T(8,128)S(1)} %add_bitcast_fusion), channel_id=1, source_target_pairs={{0,192},{64,0},{128,64},{192,128},{1,193},{65,1},{129,65},{193,129... | collective-permute-start | bytes 110600 | tf_op jit(solution)/shard_map/ppermute | solution.py:284
  229.5 1.4 copy-start
Sparse Core Ops, SparseCore 0:
  10.6 90.1 all-gather.2

commit v2 on v1

--- a/solution.py
+++ b/solution.py
@@ -29,6 +29,10 @@
     return pltpu.CompilerParams(vmem_limit_bytes=mib * MIB)
 
 
+def cost(us):
+    return pl.CostEstimate(flops=0, bytes_accessed=int(us * 3.5e6), transcendentals=0)
+
+
 def dot(a, b, dims=((1,), (0,))):
     return lax.dot_general(a, b, (dims, ((), ())), preferred_element_type=F32)
 
@@ -85,6 +89,7 @@
         out_specs=message_block,
         out_shape=message_shape,
         compiler_params=params(60),
+        cost_estimate=cost(4),
         name="pack",
     )(*arrays)
 
@@ -97,6 +102,7 @@
         out_specs=[place_block] * 4,
         out_shape=[rows_shape] * 4,
         compiler_params=params(60),
+        cost_estimate=cost(4),
         name="unpack",
     )(message)
 
@@ -116,12 +122,12 @@
     unpack(in_ref, (q, k, v, g))
     allowed = mask_ref[...] > 0.5
     for n in range(HEADS // 2):
-        logits = dot(pair(q, n), pair(k, n), ((1,), (1,))) * FACTOR
+        logits = dot(pair(k, n), pair(q, n), ((1,), (1,))) * FACTOR
         logits = jnp.where(allowed, logits, F32(-1e30))
-        shifted = jnp.exp(logits - jnp.max(logits, axis=-1, keepdims=True))
-        probs = shifted / jnp.sum(shifted, axis=-1, keepdims=True)
+        shifted = jnp.exp(logits - jnp.max(logits, axis=0, keepdims=True))
+        probs = shifted * (1 / jnp.sum(shifted, axis=0, keepdims=True))
         probs_ref[n] = probs
-        put_pair(mixed, n, dot(probs.astype(BF), pair(v, n)).astype(BF))
+        put_pair(mixed, n, dot(probs.astype(BF), pair(v, n), ((0,), (0,))).astype(BF))
 
 
 probs_block = pl.BlockSpec((HEADS // 2, 2 * FRAMES, 2 * FRAMES), lambda j: (j, 0, 0))
@@ -134,23 +140,33 @@
         in_specs=[pl.BlockSpec((128, 128), lambda j: (0, 0)), message_block],
         out_specs=[place_block] * 5 + [probs_block],
         out_shape=[rows_shape] * 5 + [jax.ShapeDtypeStruct((HEADS // 2 * PLACES, 128, 128), F32)],
-        compiler_params=params(60),
+        compiler_params=params(14),
+        cost_estimate=cost(6),
         name="forward",
     )(mask, message)
 
 
-def weight_kernel(at, mixed, grad, keep, send, turned, strips):
+def strip_copies(at, copy):
+    for side in range(2):
+        core = at[0] if side == 0 else 1 - at[0]
+        for dy in range(NY):
+            for dz in range(NZ):
+                y, z = (at[2] + dy) % NY, at[3] ^ dz
+                there = pl.multiple_of((y * NZ + z) * 2 * STRIP + core * STRIP, 8)
+                copy(side, (dy * NZ + dz) * STRIP, there)
+
+
+def weight_kernel(at, mixed, grad, keep, send, ordered, turned, strips):
     @pl.when(pl.program_id(0) == 0)
     def _():
         turned[...] = mixed[...].astype(F32).T
+
+        def copy(side, here, there):
+            strips[side, here : here + STRIP, :] = turned[pl.ds(there, STRIP), :]
+
+        strip_copies(at, copy)
         for side in range(2):
-            core = at[0] if side == 0 else 1 - at[0]
-            for dy in range(NY):
-                for dz in range(NZ):
-                    y, z = (at[2] + dy) % NY, at[3] ^ dz
-                    src = pl.multiple_of((y * NZ + z) * 2 * STRIP + core * STRIP, 8)
-                    dst = (dy * NZ + dz) * STRIP
-                    strips[side, dst : dst + STRIP, :] = turned[pl.ds(src, STRIP), :]
+            ordered[:, HALF * side : HALF * side + HALF] = strips[side].T.astype(BF)
 
     for side, out in ((0, keep), (1, send)):
         out[0] = dot(strips[side].astype(BF), grad[...]).astype(BF)
@@ -166,66 +182,72 @@
                 pl.BlockSpec((ROWS, WIDTH), lambda d, at: (0, 0)),
                 pl.BlockSpec((ROWS, QUARTER), lambda d, at: (0, (at[1] + d) % NX)),
             ],
-            out_specs=[pl.BlockSpec((1, HALF, QUARTER), lambda d, at: (d, 0, 0))] * 2,
+            out_specs=[pl.BlockSpec((1, HALF, QUARTER), lambda d, at: (d, 0, 0))] * 2
+            + [pl.BlockSpec((ROWS, WIDTH), lambda d, at: (0, 0))],
             scratch_shapes=[pltpu.VMEM((WIDTH, ROWS), F32), pltpu.VMEM((2, HALF, ROWS), F32)],
         ),
-        out_shape=[jax.ShapeDtypeStruct((NX, HALF, QUARTER), BF)] * 2,
-        compiler_params=params(60),
+        out_shape=[jax.ShapeDtypeStruct((NX, HALF, QUARTER), BF)] * 2 + [rows_shape],
+        compiler_params=params(16),
+        cost_estimate=cost(4),
         name="weight",
     )(at, mixed, grad)
 
 
-def project_kernel(mixed, grad, weight, out, mixed_grad, total):
-    step = pl.program_id(0)
-    w = weight[...]
-    part = dot(mixed[...], w)
-
-    @pl.when(step == 0)
-    def _():
-        total[...] = part
-
-    @pl.when(step > 0)
-    def _():
-        total[...] += part
-
-    mixed_grad[...] = dot(grad[...], w, ((1,), (1,))).astype(BF)
-
-    @pl.when(step == pl.num_programs(0) - 1)
-    def _():
-        out[...] = total[...].astype(BF)
-
-
-def project_call(mixed, grad, weight):
-    depth = 256
+PIECES = ((0, 0, HALF), (-1, 0, HALF), (1, 0, HALF), (2, 0, HALF // 2), (2, HALF // 2, HALF // 2))
+
+
+def project_kernel(at, ordered, grad, *refs):
+    weights, (out, mixed_grad, strips, turned) = refs[: 2 * len(PIECES)], refs[2 * len(PIECES) :]
+    totals = {}
+    for n, (shift, start, size) in enumerate(PIECES):
+        cols = pl.ds(pl.multiple_of((at[1] + shift + NX) % NX * QUARTER, QUARTER), QUARTER)
+        part = None
+        for side in range(2):
+            w = weights[side * len(PIECES) + n][...]
+            term = dot(ordered[:, HALF * side + start : HALF * side + start + size], w)
+            part = term if part is None else part + term
+            turn = dot(w, grad[:, cols], ((1,), (1,)))
+            rows = slice(start, start + size)
+            if n == 0:
+                strips[side, rows, :] = turn
+            else:
+                strips[side, rows, :] += turn
+        totals[shift] = totals[shift] + part if shift in totals else part
+        if start + size == HALF:
+            out[:, cols] = totals[shift].astype(BF)
+
+    def copy(side, here, there):
+        turned[pl.ds(there, STRIP), :] = strips[side, here : here + STRIP, :]
+
+    strip_copies(at, copy)
+    mixed_grad[...] = turned[...].T.astype(BF)
+
+
+def project_call(at, ordered, grad, weights):
+    vmem = pl.BlockSpec(memory_space=pltpu.VMEM)
     return pl.pallas_call(
         project_kernel,
-        grid=(WIDTH // depth,),
-        in_specs=[
-            pl.BlockSpec((ROWS, depth), lambda i: (0, i)),
-            pl.BlockSpec((ROWS, WIDTH), lambda i: (0, 0)),
-            pl.BlockSpec((depth, WIDTH), lambda i: (i, 0)),
-        ],
-        out_specs=[
-            pl.BlockSpec((ROWS, WIDTH), lambda i: (0, 0)),
-            pl.BlockSpec((ROWS, depth), lambda i: (0, i)),
-        ],
+        in_specs=[pl.BlockSpec(memory_space=pltpu.SMEM)] + [vmem] * (2 + 2 * len(PIECES)),
+        out_specs=[vmem] * 2,
         out_shape=[rows_shape] * 2,
-        scratch_shapes=[pltpu.VMEM((ROWS, WIDTH), F32)],
-        compiler_params=params(60),
+        scratch_shapes=[pltpu.VMEM((2, HALF, ROWS), F32), pltpu.VMEM((WIDTH, ROWS), F32)],
+        compiler_params=params(24),
+        cost_estimate=cost(6),
         name="project",
-    )(mixed, grad, weight)
-
-
-def backward_kernel(q, k, v, mixed, mixed_grad, out, probs_ref, message, q_grad, k_grad, v_grad):
+    )(at, ordered, grad, *weights)
+
+
+def backward_kernel(q, k, v, mixed_grad, out, probs_ref, message, q_grad, k_grad, v_grad):
     for n in range(HEADS // 2):
         probs = probs_ref[n]
+        probs_low = probs.astype(BF)
         grad = pair(mixed_grad, n)
-        put_pair(v_grad, n, dot(probs.astype(BF), grad, ((0,), (0,))).astype(BF))
-        through = dot(grad, pair(v, n), ((1,), (1,)))
-        inner = jnp.sum(grad.astype(F32) * pair(mixed, n).astype(F32), axis=-1, keepdims=True)
+        put_pair(v_grad, n, dot(probs_low, grad).astype(BF))
+        through = dot(pair(v, n), grad, ((1,), (1,)))
+        inner = jnp.sum(probs_low.astype(F32) * through, axis=0, keepdims=True)
         score = (probs * (through - inner)).astype(BF)
-        put_pair(q_grad, n, (dot(score, pair(k, n)) * FACTOR).astype(BF))
-        put_pair(k_grad, n, (dot(score, pair(q, n), ((0,), (0,))) * FACTOR).astype(BF))
+        put_pair(q_grad, n, (dot(score, pair(k, n), ((0,), (0,))) * FACTOR).astype(BF))
+        put_pair(k_grad, n, (dot(score, pair(q, n)) * FACTOR).astype(BF))
     pack((out, q_grad, k_grad, v_grad), message)
 
 
@@ -233,11 +255,12 @@
     return pl.pallas_call(
         backward_kernel,
         grid=(PLACES,),
-        in_specs=[place_block] * 6 + [probs_block],
+        in_specs=[place_block] * 5 + [probs_block],
         out_specs=message_block,
         out_shape=message_shape,
         scratch_shapes=[pltpu.VMEM((FRAMES, WIDTH), BF)] * 3,
-        compiler_params=params(60),
+        compiler_params=params(14),
+        cost_estimate=cost(6),
         name="backward",
     )(*arrays)
 
@@ -270,9 +293,21 @@
     return [add_up([keep[d], came[d]]).astype(BF) for d in range(NX)]
 
 
-def reduce_rest(parts):
-    came = [lax.ppermute(parts[d], "dp", [(i, (i + d) % NX) for i in range(NX)]) for d in (1, 3, 2)]
-    chip = add_up([parts[0]] + came).astype(BF).reshape(NY, NZ * STRIP, QUARTER)
+def along_x(x, shift):
+    return lax.ppermute(x, "dp", [(i, (i + shift) % NX) for i in range(NX)])
+
+
+def reduce_x(parts):
+    mid = HALF // 2
+    right = along_x(parts[2][:mid], 1)
+    left = along_x(parts[2][mid:], -1)
+    ahead = jnp.concatenate([add_up([parts[1][:mid], right]).astype(BF), parts[1][mid:]], axis=0)
+    back = jnp.concatenate([parts[3][:mid], add_up([parts[3][mid:], left]).astype(BF)], axis=0)
+    return add_up([parts[0], along_x(ahead, 1), along_x(back, -1)]).astype(BF)
+
+
+def reduce_rest(chip):
+    chip = chip.reshape(NY, NZ * STRIP, QUARTER)
     came = [lax.ppermute(chip[d], "seq", seq_shift(d, 0, 0)) for d in (1, 3, 2)]
     strips = add_up([chip[0]] + came).astype(BF).reshape(NZ, STRIP, QUARTER)
     for bit in (4, 2, 1):
@@ -281,19 +316,25 @@
         if bit > 1:
             strips = strips.astype(BF)
     own = strips[0]
-    came = {d: lax.ppermute(own, "dp", [(i, (i + d) % NX) for i in range(NX)]) for d in (1, 3, 2)}
+    came = {d: along_x(own, d) for d in (1, 3, 2)}
     place = lax.axis_index("dp")
     quarters = [lax.select_n((place - n) % NX, own, came[1], came[2], came[3]) for n in range(NX)]
     return jnp.concatenate(quarters, axis=1)
 
 
 def gather_weight(out_weight):
-    cores = [list(range(core, SEQ, 2)) for core in range(2)]
-    own = lax.all_gather(out_weight, "seq", axis=0, axis_index_groups=cores)
-    other = lax.ppermute(own, "seq", seq_shift(0, 0, 1))
-    first = lax.axis_index("seq") % 2 == 0
-    both = [jnp.where(first, own, other), jnp.where(first, other, own)]
-    return jnp.stack(both, axis=1).reshape(WIDTH, WIDTH)
+    place = lax.axis_index("dp")
+    own = lax.select_n(place, *[out_weight[:, QUARTER * n : QUARTER * n + QUARTER] for n in range(NX)])
+    own = own[None]
+    for bit in (1, 2, 4):
+        own = jnp.concatenate([own, lax.ppermute(own, "seq", seq_flip(bit))], axis=0)
+    own = own.reshape(NZ * STRIP, QUARTER)
+    came = {d: lax.ppermute(own, "seq", seq_shift(NY - d, 0, 0)) for d in (1, 3, 2)}
+    own = jnp.concatenate([own, came[1], came[2], came[3]], axis=0)
+    mid = HALF // 2
+    left, right = along_x(own, 1), along_x(own, -1)
+    pieces = [own, left, right, along_x(left[:mid], 1), along_x(right[mid:], -1)]
+    return pieces + [lax.ppermute(piece, "seq", seq_shift(0, 0, 1)) for piece in pieces]
 
 
 def exchange(message):
@@ -301,7 +342,7 @@
 
 
 def local(queries, key_field, value_field, out_grad, out_weight, frame_video):
-    weight = gather_weight(out_weight)
+    weights = gather_weight(out_weight)
     videos = frame_video[0]
     same = jnp.tile((videos[:, None] == videos[None, :]), (2, 2))
     head = jnp.arange(2 * FRAMES) // FRAMES
@@ -312,13 +353,14 @@
     flat = [x.reshape(ROWS, WIDTH) for x in (queries, key_field, value_field, out_grad)]
     arrived = exchange(pack_call(*flat))
     q, k, v, g, mixed, probs = forward_call(mask, arrived)
-    keep, send = weight_call(at, mixed, g)
-    came = lax.ppermute(send, "seq", seq_shift(0, 0, 1))
-    out, mixed_grad = project_call(mixed, g, weight)
-    parts, mixed_grad = lax.optimization_barrier((reduce_chip(keep, came), mixed_grad))
-    message = backward_call(q, k, v, mixed, mixed_grad, out, probs)
+    keep, send, ordered = weight_call(at, mixed, g)
+    parts = reduce_chip(keep, lax.ppermute(send, "seq", seq_shift(0, 0, 1)))
+    out, mixed_grad = project_call(at, ordered, g, weights)
+    parts, mixed_grad = lax.optimization_barrier((parts, mixed_grad))
+    chip = reduce_x(parts)
+    message = backward_call(q, k, v, mixed_grad, out, probs)
     results = unpack_call(exchange(message))
-    weight_grad = reduce_rest(parts)
+    weight_grad = reduce_rest(chip)
     return tuple(x.reshape(queries.shape) for x in results) + (weight_grad,)
 
 

time: 243 us -> 250 us (1.029)
  waiting for transfers between devices: 128 us -> 143 us
  starting transfers between devices: 47 us -> 61.4 us
  between operations: 14.2 us -> 1.01 us
  Pallas kernels: 39.2 us -> 30.2 us
  other arithmetic: 11 us -> 6.43 us
  local copies, waits for them, and re-layouts: 3.1 us -> 7.28 us
    all_gather x1 -> x0, waiting for transfers between devices: 75.9 us -> none  [gather_weight(): own = lax.all_gather(out_weight, 'seq', axis=0, axis_index_groups=cores)]
    all_to_all x2, waiting for transfers between devices: 0.01 us -> 54.1 us  [exchange(): lax.all_to_all(message, 'seq', split_axis=0, concat_axis=0, tiled=True)]
    ppermute x8 -> x23, waiting for transfers between devices: 27.9 us -> 64.8 us  [the longest x11 44.4 us: along_x(): return lax.ppermute(x, 'dp', [(i, (i + shift) % NX) for i in range(NX)])]
    ppermute x8 -> x23, starting transfers between devices: 11.8 us -> 28.3 us  [the longest x11 17.8 us: along_x(): return lax.ppermute(x, 'dp', [(i, (i + shift) % NX) for i in range(NX)])]
    another operation x2 -> x0, other arithmetic: 5.27 us -> none  [gather_weight(): return jnp.stack(both, axis=1).reshape(WIDTH, WIDTH)]
    pallas_call x1, Pallas kernels: 8.32 us -> 4.06 us  [project_call(): pl.pallas_call(project_kernel, in_specs=[pl.BlockSpec(memory_space=pltpu....]
    unnamed x8 -> x26, local copies, waits for them, and re-layouts: 2.88 us -> 5.76 us
    pallas_call x1, Pallas kernels: 8.27 us -> 5.62 us  [forward_call(): pl.pallas_call(forward_kernel, grid=(PLACES,), in_specs=[pl.BlockSpec((12...]
  transfers between devices with their start and end apart: 17 -> 31, of which waited for: 12 -> 22; matrix products, arithmetic and copies ran while one was open for 3% -> 2% of each run, Pallas kernels for 11% -> 2%
where the time goes in v2:
time: 250 us; the launch traced here: 249 us
  waiting for transfers between devices  143 us (57%)
  starting transfers between devices  61.4 us (25%)
  Pallas kernels  30.2 us (12%)
  local copies, waits for them, and re-layouts  7.28 us (3%)
  other arithmetic  6.43 us (3%)
    all_to_all x2, waiting for transfers between devices, exchange(): lax.all_to_all(message, 'seq', split_axis=0, concat_axis=0, tiled=True)  54.1 us
    ppermute x11, waiting for transfers between devices, along_x(): return lax.ppermute(x, 'dp', [(i, (i + shift) % NX) for i in range(NX)])  44.4 us
    all_to_all x2, starting transfers between devices, exchange(): lax.all_to_all(message, 'seq', split_axis=0, concat_axis=0, tiled=True)  18.8 us
    ppermute x11, starting transfers between devices, along_x(): return lax.ppermute(x, 'dp', [(i, (i + shift) % NX) for i in range(NX)])  17.8 us
    ppermute x3, waiting for transfers between devices, gather_weight(): lax.ppermute(own, 'seq', seq_flip(bit))  14.3 us
    ppermute x3, waiting for transfers between devices, reduce_rest(): came = lax.ppermute(strips[bit:], 'seq', seq_flip(bit))  14.2 us
    ppermute x3, starting transfers between devices, reduce_rest(): came = lax.ppermute(strips[bit:], 'seq', seq_flip(bit))  9.97 us
    ppermute x3, waiting for transfers between devices, reduce_rest(): came = [lax.ppermute(chip[d], 'seq', seq_shift(d, 0, 0)) for d in (1, 3, 2)]  9.78 us
  transfers between devices with their start and end apart: 31, of which 22 were waited for; matrix products, arithmetic and copies ran while one was open for 2% of the time, Pallas kernels for 2%

profile of v2, /device:TPU:8, one launch (start us, length us, event | category | flops | bytes accessed | tf_op | source)
XLA Modules:
  0.0 249.2 jit_solution(6265044238904419751)
XLA Ops:
  0.6 4.7 %pack.1 = bf16[512,2304]{1,0:T(8,128)(2,1)} custom-call(bf16[192,1536]{1,0:T(8,128)(2,1)} %bitcast.44, bf16[192,1536]{1,0:T(8,128)(2,1)} %bitcast.45, bf16[192,1536]{1,0:T(8,128)(2,1)} %bitcast.46, bf16[192,1536]{1,0:T(8,128)(2,1)} %bitcast.47), custom_call_target="tpu_custom_call" | custom-call | bytes 14000000 | tf_op jit(solution)/shard_map/pack/pallas_call | solution.py:85
  5.3 12.2 %all-to-all-start = ((bf16[64,8,2304]{2,1,0:T(8,128)(2,1)}), bf16[64,8,2304]{2,1,0:T(8,128)(2,1)S(1)}, u32[]{:S(2)}, u32[]{:S(2)}) async-start(bf16[64,8,2304]{2,1,0:T(8,128)(2,1)} %bitcast.43), calls=%async_computation | async-start | bytes 4718592 | tf_op jit(solution)/shard_map/all_to_all | solution.py:341
  17.7 0.1 tile.10
  18.0 0.7 and_convert_fusion.mask_ref
  18.7 54.1 %all-to-all-done = bf16[64,8,2304]{2,1,0:T(8,128)(2,1)S(1)} async-done(((bf16[64,8,2304]{2,1,0:T(8,128)(2,1)}), bf16[64,8,2304]{2,1,0:T(8,128)(2,1)S(1)}, u32[]{:S(2)}, u32[]{:S(2)}) %all-to-all-start) | async-done | bytes 2359328 | tf_op jit(solution)/shard_map/all_to_all | solution.py:341
  72.8 0.8 copy-done.8
  73.6 5.6 %forward.1 = (bf16[192,1536]{1,0:T(8,128)(2,1)S(1)}, bf16[192,1536]{1,0:T(8,128)(2,1)S(1)}, bf16[192,1536]{1,0:T(8,128)(2,1)S(1)}, bf16[192,1536]{1,0:T(8,128)(2...) custom-call(f32[128,128]{1,0:T(8,128)S(1)} %copy-done.8, bf16[512,2304]{1,0:T(8,128)(2,1)S(1)} %bitcast.41), custom_call_target="tpu_custom_call" | custom-call | bytes 21000000 | tf_op jit(solution)/shard_map/forward/pallas_call | solution.py:137
  79.3 1.0 copy-done
  80.3 0.8 copy-done.2
  81.1 0.8 copy-done.4
  81.9 4.6 %weight.1 = (bf16[4,768,384]{2,1,0:T(8,128)(2,1)S(1)}, bf16[4,768,384]{2,1,0:T(8,128)(2,1)}, bf16[192,1536]{1,0:T(8,128)(2,1)S(1)}) custom-call(s32[4]{0:T(128)S(1)} %pad_add_fusion.at, bf16[192,1536]{1,0:T(8,128)(2,1)S(1)} %get-tuple-element.28.mixed, bf16[192,1536]{1,0:T(8,128)(2,1)S(1)} %get-tuple-element.29.grad), custom_call_target="tpu_custom_call" | custom-call | bytes 14000000 | tf_op jit(solution)/shard_map/weight/pallas_call | solution.py:176
  86.6 0.8 copy-done.6
  87.4 1.4 collective-permute-start
  88.8 0.8 select_bitcast_fusion
  89.6 0.7 collective-permute-start.1
  90.2 3.2 %collective-permute-done.1 = bf16[1,24,384]{2,1,0:T(8,128)(2,1)S(1)} collective-permute-done((bf16[1,24,384]{2,1,0:T(8,128)(2,1)S(1)}, bf16[1,24,384]{2,1,0:T(8,128)(2,1)S(1)}, u32[]{:S(2)}, u32[]{:S(2)}) %collective-permute-start.1) | collective-permute-done | bytes 18464 | tf_op jit(solution)/shard_map/ppermute | solution.py:330
  93.4 1.5 collective-permute-start.2
  94.9 3.9 %collective-permute-done.2 = bf16[2,24,384]{2,1,0:T(8,128)(2,1)S(1)} collective-permute-done((bf16[2,24,384]{2,1,0:T(8,128)(2,1)S(1)}, bf16[2,24,384]{2,1,0:T(8,128)(2,1)S(1)}, u32[]{:S(2)}, u32[]{:S(2)}) %collective-permute-start.2) | collective-permute-done | bytes 36896 | tf_op jit(solution)/shard_map/ppermute | solution.py:330
  98.8 1.1 collective-permute-start.3
  99.9 7.3 %collective-permute-done.3 = bf16[4,24,384]{2,1,0:T(8,128)(2,1)S(1)} collective-permute-done((bf16[4,24,384]{2,1,0:T(8,128)(2,1)S(1)}, bf16[4,24,384]{2,1,0:T(8,128)(2,1)S(1)}, u32[]{:S(2)}, u32[]{:S(2)}) %collective-permute-start.3) | collective-permute-done | bytes 73760 | tf_op jit(solution)/shard_map/ppermute | solution.py:330
  107.2 2.4 collective-permute-start.6
  109.6 0.3 collective-permute-start.5
  109.9 2.3 collective-permute-start.4
  112.2 0.3 collective-permute-done.6
  112.6 3.8 %collective-permute-done.5 = bf16[192,384]{1,0:T(8,128)(2,1)S(1)} collective-permute-done((bf16[192,384]{1,0:T(8,128)(2,1)S(1)}, bf16[192,384]{1,0:T(8,128)(2,1)S(1)}, u32[]{:S(2)}, u32[]{:S(2)}) %collective-permute-start.5) | collective-permute-done | bytes 147488 | tf_op jit(solution)/shard_map/ppermute | solution.py:332
  116.3 0.3 collective-permute-done.4
  116.7 1.6 collective-permute-start.7
  118.3 1.7 collective-permute-start.8
  120.0 10.1 %collective-permute-done.7.refs_1_ = bf16[768,384]{1,0:T(8,128)(2,1)S(1)} collective-permute-done((bf16[768,384]{1,0:T(8,128)(2,1)S(1)}, bf16[768,384]{1,0:T(8,128)(2,1)S(1)}, u32[]{:S(2)}, u32[]{:S(2)}) %collective-permute-start.7) | collective-permute-done | bytes 589856 | tf_op jit(solution)/shard_map/ppermute | solution.py:297
  130.2 1.6 collective-permute-start.9
  131.8 0.8 collective-permute-start.13
  132.6 1.8 collective-permute-start.10
  134.4 3.9 %collective-permute-done.9.refs_3_ = bf16[384,384]{1,0:T(8,128)(2,1)S(1)} collective-permute-done((bf16[384,384]{1,0:T(8,128)(2,1)S(1)}, bf16[384,384]{1,0:T(8,128)(2,1)S(1)}, u32[]{:S(2)}, u32[]{:S(2)}) %collective-permute-start.9) | collective-permute-done | bytes 294944 | tf_op jit(solution)/shard_map/ppermute | solution.py:297
  138.2 3.4 %collective-permute-done.10.refs_4_ = bf16[384,384]{1,0:T(8,128)(2,1)S(1)} collective-permute-done((bf16[384,384]{1,0:T(8,128)(2,1)S(1)}, bf16[384,384]{1,0:T(8,128)(2,1)S(1)}, u32[]{:S(2)}, u32[]{:S(2)}) %collective-permute-start.10) | collective-permute-done | bytes 294944 | tf_op jit(solution)/shard_map/ppermute | solution.py:297
  141.6 1.6 collective-permute-done.15.refs_9_
  143.2 4.1 %project.1 = (bf16[192,1536]{1,0:T(8,128)(2,1)S(1)}, bf16[192,1536]{1,0:T(8,128)(2,1)S(1)}) custom-call(s32[4]{0:T(128)S(1)} %pad_add_fusion.at, bf16[192,1536]{1,0:T(8,128)(2,1)S(1)} %copy-done.7, bf16[192,1536]{1,0:T(8,128)(2,1)S(1)} %get-tuple-element.29.grad, bf16[768,384]{1,0:T(8,128)(2,1)S(1)} %pad_maximum_fusion.refs_0_, ...), custom_call_target="tpu_custom_call" | custom-call | bytes 21000000 | tf_op jit(solution)/shard_map/project/pallas_call | solution.py:228
  147.3 3.3 %fusion.3 = (bf16[768,384]{1,0:T(8,128)(2,1)}, bf16[768,384]{1,0:T(8,128)(2,1)}, bf16[768,384]{1,0:T(8,128)(2,1)S(1)}, bf16[768,384]{1,0:T(8,128)(2,1)}) fusion(bf16[4,768,384]{2,1,0:T(8,128)(2,1)} %collective-permute-done, bf16[4,768,384]{2,1,0:T(8,128)(2,1)S(1)} %get-tuple-element.30), kind=kLoop, calls=%fused_computation.8 | loop fusion | flops 4718592 | bytes 7077888 | tf_op jit(solution)/shard_map/convert_element_type | solution.py:293
  150.7 6.8 %backward.1 = bf16[512,2304]{1,0:T(8,128)(2,1)} custom-call(bf16[192,1536]{1,0:T(8,128)(2,1)S(1)} %get-tuple-element.25.q, bf16[192,1536]{1,0:T(8,128)(2,1)S(1)} %copy-done.3, bf16[192,1536]{1,0:T(8,128)(2,1)S(1)} %copy-done.5, bf16[192,1536]{1,0:T(8,128)(2,1)S(1)} %get-tuple-element.34.mixed_grad, bf16[192,1536]{1,0:T(8,128)(2,1)S(1)} %get-tuple-element.35.out, ...), custom_call_target="tpu_custom_call" | custom-call | bytes 21000000 | tf_op jit(solution)/shard_map/backward/pallas_call | solution.py:255
  157.5 6.6 %all-to-all-start.1 = ((bf16[64,8,2304]{2,1,0:T(8,128)(2,1)}), bf16[64,8,2304]{2,1,0:T(8,128)(2,1)S(1)}, u32[]{:S(2)}, u32[]{:S(2)}) async-start(bf16[64,8,2304]{2,1,0:T(8,128)(2,1)} %bitcast.17), calls=%async_computation.1 | async-start | bytes 4718592 | tf_op jit(solution)/shard_map/all_to_all | solution.py:341
  164.1 1.2 fusion.6
  165.3 3.1 %collective-permute-start.18 = (bf16[384,384]{1,0:T(8,128)(2,1)S(1)}, bf16[384,384]{1,0:T(8,128)(2,1)S(1)}, u32[]{:S(2)}, u32[]{:S(2)}) collective-permute-start(bf16[384,384]{1,0:T(8,128)(2,1)S(1)} %get-tuple-element.53), channel_id=1, source_target_pairs={{0,192},{64,0},{128,64},{192,128},{1,193},{65,1},{129,65},{193,129... | collective-permute-start | bytes 884744 | tf_op jit(solution)/shard_map/ppermute | solution.py:297
  168.5 6.4 %collective-permute-done.18 = bf16[384,384]{1,0:T(8,128)(2,1)S(1)} collective-permute-done((bf16[384,384]{1,0:T(8,128)(2,1)S(1)}, bf16[384,384]{1,0:T(8,128)(2,1)S(1)}, u32[]{:S(2)}, u32[]{:S(2)}) %collective-permute-start.18) | collective-permute-done | bytes 294944 | tf_op jit(solution)/shard_map/ppermute | solution.py:297
  175.1 3.8 %collective-permute-start.19 = (bf16[768,384]{1,0:T(8,128)(2,1)S(1)}, bf16[768,384]{1,0:T(8,128)(2,1)S(1)}, u32[]{:S(2)}, u32[]{:S(2)}) collective-permute-start(bf16[768,384]{1,0:T(8,128)(2,1)S(1)} %pad_maximum_fusion.2), channel_id=1, source_target_pairs={{0,192},{64,0},{128,64},{192,128},{1,193},{65,1},{129,65},{193,129... | collective-permute-start | bytes 1769480 | tf_op jit(solution)/shard_map/ppermute | solution.py:297
  179.1 11.8 %collective-permute-done.19 = bf16[768,384]{1,0:T(8,128)(2,1)S(1)} collective-permute-done((bf16[768,384]{1,0:T(8,128)(2,1)S(1)}, bf16[768,384]{1,0:T(8,128)(2,1)S(1)}, u32[]{:S(2)}, u32[]{:S(2)}) %collective-permute-start.19) | collective-permute-done | bytes 589856 | tf_op jit(solution)/shard_map/ppermute | solution.py:297
  190.9 3.6 %collective-permute-done.17 = bf16[768,384]{1,0:T(8,128)(2,1)S(1)} collective-permute-done((bf16[768,384]{1,0:T(8,128)(2,1)S(1)}, bf16[768,384]{1,0:T(8,128)(2,1)S(1)}, u32[]{:S(2)}, u32[]{:S(2)}) %collective-permute-start.17) | collective-permute-done | bytes 589856 | tf_op jit(solution)/shard_map/ppermute | solution.py:297
  194.5 0.2 add_convert_fusion
  194.8 2.4 collective-permute-start.22
  197.2 1.4 collective-permute-start.21
  198.5 0.7 collective-permute-start.20
  199.2 5.5 %collective-permute-done.22 = bf16[192,384]{1,0:T(8,128)(2,1)S(1)} collective-permute-done((bf16[192,384]{1,0:T(8,128)(2,1)S(1)}, bf16[192,384]{1,0:T(8,128)(2,1)S(1)}, u32[]{:S(2)}, u32[]{:S(2)}) %collective-permute-start.22) | collective-permute-done | bytes 147488 | tf_op jit(solution)/shard_map/ppermute | solution.py:311
  204.7 4.3 %collective-permute-done.21 = bf16[192,384]{1,0:T(8,128)(2,1)S(1)} collective-permute-done((bf16[192,384]{1,0:T(8,128)(2,1)S(1)}, bf16[192,384]{1,0:T(8,128)(2,1)S(1)}, u32[]{:S(2)}, u32[]{:S(2)}) %collective-permute-start.21) | collective-permute-done | bytes 147488 | tf_op jit(solution)/shard_map/ppermute | solution.py:311
  209.1 9.5 %collective-permute-start.23 = (bf16[4,24,384]{2,1,0:T(8,128)(2,1)S(1)}, bf16[4,24,384]{2,1,0:T(8,128)(2,1)S(1)}, u32[]{:S(2)}, u32[]{:S(2)}) collective-permute-start(bf16[4,24,384]{2,1,0:T(8,128)(2,1)S(1)} %bitcast.53), channel_id=1, source_target_pairs={{0,8},{1,9},{2,10},{3,11},{4,12},{5,13},{6,14},{7,15},{8,0},{9,1},... | collective-permute-start | bytes 221192 | tf_op jit(solution)/shard_map/ppermute | solution.py:314
  218.6 5.4 %collective-permute-done.23 = bf16[4,24,384]{2,1,0:T(8,128)(2,1)S(1)} collective-permute-done((bf16[4,24,384]{2,1,0:T(8,128)(2,1)S(1)}, bf16[4,24,384]{2,1,0:T(8,128)(2,1)S(1)}, u32[]{:S(2)}, u32[]{:S(2)}) %collective-permute-start.23) | collective-permute-done | bytes 73760 | tf_op jit(solution)/shard_map/ppermute | solution.py:314
  224.2 5.2 %collective-permute-done.24 = bf16[2,24,384]{2,1,0:T(8,128)(2,1)S(1)} collective-permute-done((bf16[2,24,384]{2,1,0:T(8,128)(2,1)S(1)}, bf16[2,24,384]{2,1,0:T(8,128)(2,1)S(1)}, u32[]{:S(2)}, u32[]{:S(2)}) %collective-permute-start.24) | collective-permute-done | bytes 36896 | tf_op jit(solution)/shard_map/ppermute | solution.py:314
  229.4 0.4 collective-permute-start.25
  229.8 3.5 %collective-permute-done.25 = bf16[1,24,384]{2,1,0:T(8,128)(2,1)S(1)} collective-permute-done((bf16[1,24,384]{2,1,0:T(8,128)(2,1)S(1)}, bf16[1,24,384]{2,1,0:T(8,128)(2,1)S(1)}, u32[]{:S(2)}, u32[]{:S(2)}) %collective-permute-start.25) | collective-permute-done | bytes 18464 | tf_op jit(solution)/shard_map/ppermute | solution.py:314
  233.3 1.6 collective-permute-start.27
  234.9 2.5 %collective-permute-start.28 = (f32[24,384]{1,0:T(8,128)S(1)}, f32[24,384]{1,0:T(8,128)S(1)}, u32[]{:S(2)}, u32[]{:S(2)}) collective-permute-start(f32[24,384]{1,0:T(8,128)S(1)} %add_bitcast_fusion), channel_id=1, source_target_pairs={{0,192},{64,0},{128,64},{192,128},{1,193},{65,1},{129,65},{193,129... | collective-permute-start | bytes 110600 | tf_op jit(solution)/shard_map/ppermute | solution.py:297
  237.5 1.3 collective-permute-done.27
  238.8 0.7 collective-permute-done.28
  239.5 3.2 %collective-permute-done.26 = f32[24,384]{1,0:T(8,128)S(1)} collective-permute-done((f32[24,384]{1,0:T(8,128)S(1)}, f32[24,384]{1,0:T(8,128)S(1)}, u32[]{:S(2)}, u32[]{:S(2)}) %collective-permute-start.26) | collective-permute-done | bytes 36896 | tf_op jit(solution)/shard_map/ppermute | solution.py:297
  242.7 0.7 pad_maximum_fusion.4
  243.4 1.4 copy-done.9
  244.8 4.4 %unpack.1 = (bf16[192,1536]{1,0:T(8,128)(2,1)}, bf16[192,1536]{1,0:T(8,128)(2,1)}, bf16[192,1536]{1,0:T(8,128)(2,1)}, bf16[192,1536]{1,0:T(8,128)(2,1)}) custom-call(bf16[512,2304]{1,0:T(8,128)(2,1)} %bitcast.42), custom_call_target="tpu_custom_call" | custom-call | bytes 14000000 | tf_op jit(solution)/shard_map/unpack/pallas_call | solution.py:98
  (63 shorter events, 1.3 us)
Async XLA Ops:
  5.3 12.3 %copy-start.12 = (s32[1,64]{1,0:T(1,128)S(1)}, s32[1,64]{1,0:T(1,128)}, u32[]{:S(2)}) copy-start(s32[1,64]{1,0:T(1,128)} %param.11) | copy-start | bytes 772
  5.3 67.5 %all-to-all-start = ((bf16[64,8,2304]{2,1,0:T(8,128)(2,1)}), bf16[64,8,2304]{2,1,0:T(8,128)(2,1)S(1)}, u32[]{:S(2)}, u32[]{:S(2)}) async-start(bf16[64,8,2304]{2,1,0:T(8,128)(2,1)} %bitcast.43), calls=%async_computation | async-start | bytes 4718592 | tf_op jit(solution)/shard_map/all_to_all | solution.py:341
  72.8 0.8 copy-start.8
  79.3 1.0 copy-start
  80.3 0.8 copy-start.2
  81.1 0.8 copy-start.4
  86.6 0.8 copy-start.6
  87.4 59.9 %collective-permute-start = (bf16[4,768,384]{2,1,0:T(8,128)(2,1)}, bf16[4,768,384]{2,1,0:T(8,128)(2,1)}, u32[]{:S(2)}, u32[]{:S(2)}) collective-permute-start(bf16[4,768,384]{2,1,0:T(8,128)(2,1)} %get-tuple-element.31), channel_id=1, source_target_pairs={{0,1},{1,0},{2,3},{3,2},{4,5},{5,4},{6,7},{7,6},{8,9},{9,8},{10,11... | collective-permute-start | bytes 7077896 | tf_op jit(solution)/shard_map/ppermute | solution.py:357
  89.6 3.8 %collective-permute-start.1 = (bf16[1,24,384]{2,1,0:T(8,128)(2,1)S(1)}, bf16[1,24,384]{2,1,0:T(8,128)(2,1)S(1)}, u32[]{:S(2)}, u32[]{:S(2)}) collective-permute-start(bf16[1,24,384]{2,1,0:T(8,128)(2,1)S(1)} %select_bitcast_fusion), channel_id=1, source_target_pairs={{0,2},{1,3},{2,0},{3,1},{4,6},{5,7},{6,4},{7,5},{8,10},{9,11},{10,... | collective-permute-start | bytes 55304 | tf_op jit(solution)/shard_map/ppermute | solution.py:330
  93.4 5.3 %collective-permute-start.2 = (bf16[2,24,384]{2,1,0:T(8,128)(2,1)S(1)}, bf16[2,24,384]{2,1,0:T(8,128)(2,1)S(1)}, u32[]{:S(2)}, u32[]{:S(2)}) collective-permute-start(bf16[2,24,384]{2,1,0:T(8,128)(2,1)S(1)} %pad_maximum_fusion.6), channel_id=1, source_target_pairs={{0,4},{1,5},{2,6},{3,7},{4,0},{5,1},{6,2},{7,3},{8,12},{9,13},{10,... | collective-permute-start | bytes 110600 | tf_op jit(solution)/shard_map/ppermute | solution.py:330
  98.8 8.4 %collective-permute-start.3 = (bf16[4,24,384]{2,1,0:T(8,128)(2,1)S(1)}, bf16[4,24,384]{2,1,0:T(8,128)(2,1)S(1)}, u32[]{:S(2)}, u32[]{:S(2)}) collective-permute-start(bf16[4,24,384]{2,1,0:T(8,128)(2,1)S(1)} %pad_maximum_fusion.5), channel_id=1, source_target_pairs={{0,8},{1,9},{2,10},{3,11},{4,12},{5,13},{6,14},{7,15},{8,0},{9,1},... | collective-permute-start | bytes 221192 | tf_op jit(solution)/shard_map/ppermute | solution.py:330
  107.2 36.0 %copy-start.7 = (bf16[192,1536]{1,0:T(8,128)(2,1)S(1)}, bf16[192,1536]{1,0:T(8,128)(2,1)}, u32[]{:S(2)}) copy-start(bf16[192,1536]{1,0:T(8,128)(2,1)} %copy-done.6) | copy-start | bytes 1769476
  107.2 5.4 %collective-permute-start.6 = (bf16[192,384]{1,0:T(8,128)(2,1)S(1)}, bf16[192,384]{1,0:T(8,128)(2,1)S(1)}, u32[]{:S(2)}, u32[]{:S(2)}) collective-permute-start(bf16[192,384]{1,0:T(8,128)(2,1)S(1)} %bitcast.48), channel_id=1, source_target_pairs={{0,16},{1,17},{2,18},{3,19},{4,20},{5,21},{6,22},{7,23},{8,24},{9,... | collective-permute-start | bytes 442376 | tf_op jit(solution)/shard_map/ppermute | solution.py:332
  109.6 6.8 %collective-permute-start.5 = (bf16[192,384]{1,0:T(8,128)(2,1)S(1)}, bf16[192,384]{1,0:T(8,128)(2,1)S(1)}, u32[]{:S(2)}, u32[]{:S(2)}) collective-permute-start(bf16[192,384]{1,0:T(8,128)(2,1)S(1)} %bitcast.49), channel_id=1, source_target_pairs={{0,32},{1,33},{2,34},{3,35},{4,36},{5,37},{6,38},{7,39},{8,40},{9,... | collective-permute-start | bytes 442376 | tf_op jit(solution)/shard_map/ppermute | solution.py:332
  109.9 6.7 %collective-permute-start.4 = (bf16[192,384]{1,0:T(8,128)(2,1)S(1)}, bf16[192,384]{1,0:T(8,128)(2,1)S(1)}, u32[]{:S(2)}, u32[]{:S(2)}) collective-permute-start(bf16[192,384]{1,0:T(8,128)(2,1)S(1)} %bitcast.50), channel_id=1, source_target_pairs={{0,48},{1,49},{2,50},{3,51},{4,52},{5,53},{6,54},{7,55},{8,56},{9,... | collective-permute-start | bytes 442376 | tf_op jit(solution)/shard_map/ppermute | solution.py:332
  116.7 13.5 %collective-permute-start.7 = (bf16[768,384]{1,0:T(8,128)(2,1)S(1)}, bf16[768,384]{1,0:T(8,128)(2,1)S(1)}, u32[]{:S(2)}, u32[]{:S(2)}) collective-permute-start(bf16[768,384]{1,0:T(8,128)(2,1)S(1)} %pad_maximum_fusion.refs_0_), channel_id=1, source_target_pairs={{0,64},{64,128},{128,192},{192,0},{1,65},{65,129},{129,193},{193,1... | collective-permute-start | bytes 1769480 | tf_op jit(solution)/shard_map/ppermute | solution.py:297
  118.3 13.5 %collective-permute-start.8 = (bf16[768,384]{1,0:T(8,128)(2,1)S(1)}, bf16[768,384]{1,0:T(8,128)(2,1)S(1)}, u32[]{:S(2)}, u32[]{:S(2)}) collective-permute-start(bf16[768,384]{1,0:T(8,128)(2,1)S(1)} %pad_maximum_fusion.refs_0_), channel_id=1, source_target_pairs={{0,192},{64,0},{128,64},{192,128},{1,193},{65,1},{129,65},{193,129... | collective-permute-start | bytes 1769480 | tf_op jit(solution)/shard_map/ppermute | solution.py:297
  120.0 12.6 %collective-permute-start.11 = (bf16[768,384]{1,0:T(8,128)(2,1)S(1)}, bf16[768,384]{1,0:T(8,128)(2,1)S(1)}, u32[]{:S(2)}, u32[]{:S(2)}) collective-permute-start(bf16[768,384]{1,0:T(8,128)(2,1)S(1)} %pad_maximum_fusion.refs_0_), channel_id=1, source_target_pairs={{0,1},{1,0},{2,3},{3,2},{4,5},{5,4},{6,7},{7,6},{8,9},{9,8},{10,11... | collective-permute-start | bytes 1769480 | tf_op jit(solution)/shard_map/ppermute | solution.py:337
  130.2 8.0 %collective-permute-start.9 = (bf16[384,384]{1,0:T(8,128)(2,1)S(1)}, bf16[384,384]{1,0:T(8,128)(2,1)S(1)}, u32[]{:S(2)}, u32[]{:S(2)}) collective-permute-start(bf16[384,384]{1,0:T(8,128)(2,1)S(1)} %slice.133), channel_id=1, source_target_pairs={{0,64},{64,128},{128,192},{192,0},{1,65},{65,129},{129,193},{193,1... | collective-permute-start | bytes 884744 | tf_op jit(solution)/shard_map/ppermute | solution.py:297
  131.8 9.8 %collective-permute-start.12 = (bf16[768,384]{1,0:T(8,128)(2,1)S(1)}, bf16[768,384]{1,0:T(8,128)(2,1)S(1)}, u32[]{:S(2)}, u32[]{:S(2)}) collective-permute-start(bf16[768,384]{1,0:T(8,128)(2,1)S(1)} %collective-permute-done.7.refs_1_), channel_id=1, source_target_pairs={{0,1},{1,0},{2,3},{3,2},{4,5},{5,4},{6,7},{7,6},{8,9},{9,8},{10,11... | collective-permute-start | bytes 1769480 | tf_op jit(solution)/shard_map/ppermute | solution.py:337
  131.8 9.8 %collective-permute-start.13 = (bf16[768,384]{1,0:T(8,128)(2,1)S(1)}, bf16[768,384]{1,0:T(8,128)(2,1)S(1)}, u32[]{:S(2)}, u32[]{:S(2)}) collective-permute-start(bf16[768,384]{1,0:T(8,128)(2,1)S(1)} %collective-permute-done.8.refs_2_), channel_id=1, source_target_pairs={{0,1},{1,0},{2,3},{3,2},{4,5},{5,4},{6,7},{7,6},{8,9},{9,8},{10,11... | collective-permute-start | bytes 1769480 | tf_op jit(solution)/shard_map/ppermute | solution.py:337
  132.6 9.0 %collective-permute-start.10 = (bf16[384,384]{1,0:T(8,128)(2,1)S(1)}, bf16[384,384]{1,0:T(8,128)(2,1)S(1)}, u32[]{:S(2)}, u32[]{:S(2)}) collective-permute-start(bf16[384,384]{1,0:T(8,128)(2,1)S(1)} %slice.134), channel_id=1, source_target_pairs={{0,192},{64,0},{128,64},{192,128},{1,193},{65,1},{129,65},{193,129... | collective-permute-start | bytes 884744 | tf_op jit(solution)/shard_map/ppermute | solution.py:297
  138.2 3.4 %collective-permute-start.14 = (bf16[384,384]{1,0:T(8,128)(2,1)S(1)}, bf16[384,384]{1,0:T(8,128)(2,1)S(1)}, u32[]{:S(2)}, u32[]{:S(2)}) collective-permute-start(bf16[384,384]{1,0:T(8,128)(2,1)S(1)} %collective-permute-done.9.refs_3_), channel_id=1, source_target_pairs={{0,1},{1,0},{2,3},{3,2},{4,5},{5,4},{6,7},{7,6},{8,9},{9,8},{10,11... | collective-permute-start | bytes 884744 | tf_op jit(solution)/shard_map/ppermute | solution.py:337
  141.6 1.6 collective-permute-start.15
  147.3 3.4 %copy-start.1 = (f32[18,128,128]{2,1,0:T(8,128)S(1)}, f32[18,128,128]{2,1,0:T(8,128)}, u32[]{:S(2)}) copy-start(f32[18,128,128]{2,1,0:T(8,128)} %copy-done) | copy-start | bytes 3538948
  147.3 3.4 %copy-start.3 = (bf16[192,1536]{1,0:T(8,128)(2,1)S(1)}, bf16[192,1536]{1,0:T(8,128)(2,1)}, u32[]{:S(2)}) copy-start(bf16[192,1536]{1,0:T(8,128)(2,1)} %copy-done.2) | copy-start | bytes 1769476
  147.3 3.4 %copy-start.5 = (bf16[192,1536]{1,0:T(8,128)(2,1)S(1)}, bf16[192,1536]{1,0:T(8,128)(2,1)}, u32[]{:S(2)}) copy-start(bf16[192,1536]{1,0:T(8,128)(2,1)} %copy-done.4) | copy-start | bytes 1769476
  157.5 85.9 %all-to-all-start.1 = ((bf16[64,8,2304]{2,1,0:T(8,128)(2,1)}), bf16[64,8,2304]{2,1,0:T(8,128)(2,1)S(1)}, u32[]{:S(2)}, u32[]{:S(2)}) async-start(bf16[64,8,2304]{2,1,0:T(8,128)(2,1)} %bitcast.17), calls=%async_computation.1 | async-start | bytes 4718592 | tf_op jit(solution)/shard_map/all_to_all | solution.py:341
  164.1 4.2 %copy-start.10 = (bf16[768,384]{1,0:T(8,128)(2,1)S(1)}, bf16[768,384]{1,0:T(8,128)(2,1)}, u32[]{:S(2)}) copy-start(bf16[768,384]{1,0:T(8,128)(2,1)} %get-tuple-element.44) | copy-start | bytes 1769476
  165.3 9.6 %collective-permute-start.18 = (bf16[384,384]{1,0:T(8,128)(2,1)S(1)}, bf16[384,384]{1,0:T(8,128)(2,1)S(1)}, u32[]{:S(2)}, u32[]{:S(2)}) collective-permute-start(bf16[384,384]{1,0:T(8,128)(2,1)S(1)} %get-tuple-element.53), channel_id=1, source_target_pairs={{0,192},{64,0},{128,64},{192,128},{1,193},{65,1},{129,65},{193,129... | collective-permute-start | bytes 884744 | tf_op jit(solution)/shard_map/ppermute | solution.py:297
  168.4 10.4 %collective-permute-start.16 = (bf16[384,384]{1,0:T(8,128)(2,1)S(1)}, bf16[384,384]{1,0:T(8,128)(2,1)S(1)}, u32[]{:S(2)}, u32[]{:S(2)}) collective-permute-start(bf16[384,384]{1,0:T(8,128)(2,1)S(1)} %get-tuple-element.52), channel_id=1, source_target_pairs={{0,64},{64,128},{128,192},{192,0},{1,65},{65,129},{129,193},{193,1... | collective-permute-start | bytes 884744 | tf_op jit(solution)/shard_map/ppermute | solution.py:297
  175.0 19.5 %copy-start.11 = (bf16[768,384]{1,0:T(8,128)(2,1)S(1)}, bf16[768,384]{1,0:T(8,128)(2,1)}, u32[]{:S(2)}) copy-start(bf16[768,384]{1,0:T(8,128)(2,1)} %get-tuple-element.41) | copy-start | bytes 1769476
  175.1 15.8 %collective-permute-start.19 = (bf16[768,384]{1,0:T(8,128)(2,1)S(1)}, bf16[768,384]{1,0:T(8,128)(2,1)S(1)}, u32[]{:S(2)}, u32[]{:S(2)}) collective-permute-start(bf16[768,384]{1,0:T(8,128)(2,1)S(1)} %pad_maximum_fusion.2), channel_id=1, source_target_pairs={{0,192},{64,0},{128,64},{192,128},{1,193},{65,1},{129,65},{193,129... | collective-permute-start | bytes 1769480 | tf_op jit(solution)/shard_map/ppermute | solution.py:297
  179.0 15.6 %collective-permute-start.17 = (bf16[768,384]{1,0:T(8,128)(2,1)S(1)}, bf16[768,384]{1,0:T(8,128)(2,1)S(1)}, u32[]{:S(2)}, u32[]{:S(2)}) collective-permute-start(bf16[768,384]{1,0:T(8,128)(2,1)S(1)} %pad_maximum_fusion.1), channel_id=1, source_target_pairs={{0,64},{64,128},{128,192},{192,0},{1,65},{65,129},{129,193},{193,1... | collective-permute-start | bytes 1769480 | tf_op jit(solution)/shard_map/ppermute | solution.py:297
  194.8 9.9 %collective-permute-start.22 = (bf16[192,384]{1,0:T(8,128)(2,1)S(1)}, bf16[192,384]{1,0:T(8,128)(2,1)S(1)}, u32[]{:S(2)}, u32[]{:S(2)}) collective-permute-start(bf16[192,384]{1,0:T(8,128)(2,1)S(1)} %get-tuple-element.50), channel_id=1, source_target_pairs={{0,32},{1,33},{2,34},{3,35},{4,36},{5,37},{6,38},{7,39},{8,40},{9,... | collective-permute-start | bytes 442376 | tf_op jit(solution)/shard_map/ppermute | solution.py:311
  197.2 11.8 %collective-permute-start.21 = (bf16[192,384]{1,0:T(8,128)(2,1)S(1)}, bf16[192,384]{1,0:T(8,128)(2,1)S(1)}, u32[]{:S(2)}, u32[]{:S(2)}) collective-permute-start(bf16[192,384]{1,0:T(8,128)(2,1)S(1)} %get-tuple-element.51), channel_id=1, source_target_pairs={{0,48},{1,49},{2,50},{3,51},{4,52},{5,53},{6,54},{7,55},{8,56},{9,... | collective-permute-start | bytes 442376 | tf_op jit(solution)/shard_map/ppermute | solution.py:311
  198.5 10.5 %collective-permute-start.20 = (bf16[192,384]{1,0:T(8,128)(2,1)S(1)}, bf16[192,384]{1,0:T(8,128)(2,1)S(1)}, u32[]{:S(2)}, u32[]{:S(2)}) collective-permute-start(bf16[192,384]{1,0:T(8,128)(2,1)S(1)} %get-tuple-element.49), channel_id=1, source_target_pairs={{0,16},{1,17},{2,18},{3,19},{4,20},{5,21},{6,22},{7,23},{8,24},{9,... | collective-permute-start | bytes 442376 | tf_op jit(solution)/shard_map/ppermute | solution.py:311
  209.1 14.9 %collective-permute-start.23 = (bf16[4,24,384]{2,1,0:T(8,128)(2,1)S(1)}, bf16[4,24,384]{2,1,0:T(8,128)(2,1)S(1)}, u32[]{:S(2)}, u32[]{:S(2)}) collective-permute-start(bf16[4,24,384]{2,1,0:T(8,128)(2,1)S(1)} %bitcast.53), channel_id=1, source_target_pairs={{0,8},{1,9},{2,10},{3,11},{4,12},{5,13},{6,14},{7,15},{8,0},{9,1},... | collective-permute-start | bytes 221192 | tf_op jit(solution)/shard_map/ppermute | solution.py:314
  224.1 5.3 %collective-permute-start.24 = (bf16[2,24,384]{2,1,0:T(8,128)(2,1)S(1)}, bf16[2,24,384]{2,1,0:T(8,128)(2,1)S(1)}, u32[]{:S(2)}, u32[]{:S(2)}) collective-permute-start(bf16[2,24,384]{2,1,0:T(8,128)(2,1)S(1)} %slice.142), channel_id=1, source_target_pairs={{0,4},{1,5},{2,6},{3,7},{4,0},{5,1},{6,2},{7,3},{8,12},{9,13},{10,... | collective-permute-start | bytes 110600 | tf_op jit(solution)/shard_map/ppermute | solution.py:314
  229.4 3.8 %collective-permute-start.25 = (bf16[1,24,384]{2,1,0:T(8,128)(2,1)S(1)}, bf16[1,24,384]{2,1,0:T(8,128)(2,1)S(1)}, u32[]{:S(2)}, u32[]{:S(2)}) collective-permute-start(bf16[1,24,384]{2,1,0:T(8,128)(2,1)S(1)} %slice.144), channel_id=1, source_target_pairs={{0,2},{1,3},{2,0},{3,1},{4,6},{5,7},{6,4},{7,5},{8,10},{9,11},{10,... | collective-permute-start | bytes 55304 | tf_op jit(solution)/shard_map/ppermute | solution.py:314
  233.3 5.5 %collective-permute-start.27 = (f32[24,384]{1,0:T(8,128)S(1)}, f32[24,384]{1,0:T(8,128)S(1)}, u32[]{:S(2)}, u32[]{:S(2)}) collective-permute-start(f32[24,384]{1,0:T(8,128)S(1)} %add_bitcast_fusion), channel_id=1, source_target_pairs={{0,128},{64,192},{128,0},{192,64},{1,129},{65,193},{129,1},{193,65... | collective-permute-start | bytes 110600 | tf_op jit(solution)/shard_map/ppermute | solution.py:297
  234.9 4.5 %collective-permute-start.28 = (f32[24,384]{1,0:T(8,128)S(1)}, f32[24,384]{1,0:T(8,128)S(1)}, u32[]{:S(2)}, u32[]{:S(2)}) collective-permute-start(f32[24,384]{1,0:T(8,128)S(1)} %add_bitcast_fusion), channel_id=1, source_target_pairs={{0,192},{64,0},{128,64},{192,128},{1,193},{65,1},{129,65},{193,129... | collective-permute-start | bytes 110600 | tf_op jit(solution)/shard_map/ppermute | solution.py:297
  237.5 5.2 %collective-permute-start.26 = (f32[24,384]{1,0:T(8,128)S(1)}, f32[24,384]{1,0:T(8,128)S(1)}, u32[]{:S(2)}, u32[]{:S(2)}) collective-permute-start(f32[24,384]{1,0:T(8,128)S(1)} %add_bitcast_fusion), channel_id=1, source_target_pairs={{0,64},{64,128},{128,192},{192,0},{1,65},{65,129},{129,193},{193,1... | collective-permute-start | bytes 110600 | tf_op jit(solution)/shard_map/ppermute | solution.py:297
  243.4 1.4 copy-start.9

commit v3 on v2

--- a/solution.py
+++ b/solution.py
@@ -297,10 +297,13 @@
     return lax.ppermute(x, "dp", [(i, (i + shift) % NX) for i in range(NX)])
 
 
-def reduce_x(parts):
+def reduce_x_first(parts):
     mid = HALF // 2
-    right = along_x(parts[2][:mid], 1)
-    left = along_x(parts[2][mid:], -1)
+    return along_x(parts[2][:mid], 1), along_x(parts[2][mid:], -1)
+
+
+def reduce_x_second(parts, right, left):
+    mid = HALF // 2
     ahead = jnp.concatenate([add_up([parts[1][:mid], right]).astype(BF), parts[1][mid:]], axis=0)
     back = jnp.concatenate([parts[3][:mid], add_up([parts[3][mid:], left]).astype(BF)], axis=0)
     return add_up([parts[0], along_x(ahead, 1), along_x(back, -1)]).astype(BF)
@@ -342,7 +345,6 @@
 
 
 def local(queries, key_field, value_field, out_grad, out_weight, frame_video):
-    weights = gather_weight(out_weight)
     videos = frame_video[0]
     same = jnp.tile((videos[:, None] == videos[None, :]), (2, 2))
     head = jnp.arange(2 * FRAMES) // FRAMES
@@ -351,14 +353,18 @@
     at = jnp.stack([rank % 2, lax.axis_index("dp"), rank // (2 * NZ), rank // 2 % NZ]).astype(jnp.int32)
 
     flat = [x.reshape(ROWS, WIDTH) for x in (queries, key_field, value_field, out_grad)]
-    arrived = exchange(pack_call(*flat))
+    message, out_weight = lax.optimization_barrier((pack_call(*flat), out_weight))
+    weights = gather_weight(out_weight)
+    arrived, weights = lax.optimization_barrier((exchange(message), weights))
     q, k, v, g, mixed, probs = forward_call(mask, arrived)
     keep, send, ordered = weight_call(at, mixed, g)
     parts = reduce_chip(keep, lax.ppermute(send, "seq", seq_shift(0, 0, 1)))
     out, mixed_grad = project_call(at, ordered, g, weights)
     parts, mixed_grad = lax.optimization_barrier((parts, mixed_grad))
-    chip = reduce_x(parts)
+    right, left = reduce_x_first(parts)
     message = backward_call(q, k, v, mixed_grad, out, probs)
+    message, right, left = lax.optimization_barrier((message, right, left))
+    chip = reduce_x_second(parts, right, left)
     results = unpack_call(exchange(message))
     weight_grad = reduce_rest(chip)
     return tuple(x.reshape(queries.shape) for x in results) + (weight_grad,)

time: 250 us -> 242 us (0.968)
  waiting for transfers between devices: 143 us -> 121 us
  starting transfers between devices: 61.4 us -> 72.4 us
    all_to_all x2, waiting for transfers between devices: 54.1 us -> 0.01 us  [exchange(): lax.all_to_all(message, 'seq', split_axis=0, concat_axis=0, tiled=True)]
    ppermute x3, waiting for transfers between devices: 14.3 us -> 60 us  [gather_weight(): lax.ppermute(own, 'seq', seq_flip(bit))]
    ppermute x11, waiting for transfers between devices: 44.4 us -> 27.9 us  [along_x(): return lax.ppermute(x, 'dp', [(i, (i + shift) % NX) for i in range(NX)])]
    ppermute x3, waiting for transfers between devices: 14.2 us -> 20.1 us  [reduce_rest(): came = lax.ppermute(strips[bit:], 'seq', seq_flip(bit))]
    ppermute x3, starting transfers between devices: 9.97 us -> 14.1 us  [reduce_rest(): came = lax.ppermute(strips[bit:], 'seq', seq_flip(bit))]
    ppermute x3, starting transfers between devices: 3.21 us -> 6.99 us  [gather_weight(): lax.ppermute(own, 'seq', seq_flip(bit))]
    all_to_all x2, starting transfers between devices: 18.8 us -> 21.8 us  [exchange(): lax.all_to_all(message, 'seq', split_axis=0, concat_axis=0, tiled=True)]
    unnamed x26 -> x18, local copies, waits for them, and re-layouts: 5.76 us -> 3.71 us
  transfers between devices with their start and end apart: 31 -> 31, of which waited for: 22 -> 20; matrix products, arithmetic and copies ran while one was open for 2% -> 4% of each run, Pallas kernels for 2% -> 5%
where the time goes in v3:
time: 242 us; the launch traced here: 240 us
  waiting for transfers between devices  121 us (50%)
  starting transfers between devices  72.4 us (30%)
  Pallas kernels  30.5 us (13%)
  local copies, waits for them, and re-layouts  8.58 us (4%)
  other arithmetic  6.4 us (3%)
    ppermute x3, waiting for transfers between devices, gather_weight(): lax.ppermute(own, 'seq', seq_flip(bit))  60 us
    ppermute x11, waiting for transfers between devices, along_x(): return lax.ppermute(x, 'dp', [(i, (i + shift) % NX) for i in range(NX)])  27.9 us
    all_to_all x2, starting transfers between devices, exchange(): lax.all_to_all(message, 'seq', split_axis=0, concat_axis=0, tiled=True)  21.8 us
    ppermute x3, waiting for transfers between devices, reduce_rest(): came = lax.ppermute(strips[bit:], 'seq', seq_flip(bit))  20.1 us
    ppermute x11, starting transfers between devices, along_x(): return lax.ppermute(x, 'dp', [(i, (i + shift) % NX) for i in range(NX)])  19 us
    ppermute x3, starting transfers between devices, reduce_rest(): came = lax.ppermute(strips[bit:], 'seq', seq_flip(bit))  14.1 us
    ppermute x3, waiting for transfers between devices, reduce_rest(): came = [lax.ppermute(chip[d], 'seq', seq_shift(d, 0, 0)) for d in (1, 3, 2)]  9.39 us
    ppermute x3, starting transfers between devices, gather_weight(): lax.ppermute(own, 'seq', seq_flip(bit))  6.99 us
  transfers between devices with their start and end apart: 31, of which 20 were waited for; matrix products, arithmetic and copies ran while one was open for 4% of the time, Pallas kernels for 5%

profile of v3, /device:TPU:8, one launch (start us, length us, event | category | flops | bytes accessed | tf_op | source)
XLA Modules:
  0.0 240.2 jit_solution(5906328031881556209)
XLA Ops:
  0.6 4.7 %pack.1 = bf16[512,2304]{1,0:T(8,128)(2,1)} custom-call(bf16[192,1536]{1,0:T(8,128)(2,1)} %bitcast.44, bf16[192,1536]{1,0:T(8,128)(2,1)} %bitcast.45, bf16[192,1536]{1,0:T(8,128)(2,1)} %bitcast.46, bf16[192,1536]{1,0:T(8,128)(2,1)} %bitcast.47), custom_call_target="tpu_custom_call" | custom-call | bytes 14000000 | tf_op jit(solution)/shard_map/pack/pallas_call | solution.py:85
  5.3 12.2 %all-to-all-start = ((bf16[64,8,2304]{2,1,0:T(8,128)(2,1)}), bf16[64,8,2304]{2,1,0:T(8,128)(2,1)S(1)}, u32[]{:S(2)}, u32[]{:S(2)}) async-start(bf16[64,8,2304]{2,1,0:T(8,128)(2,1)} %bitcast.43), calls=%async_computation | async-start | bytes 4718592 | tf_op jit(solution)/shard_map/all_to_all | solution.py:344
  17.6 1.6 collective-permute-start
  19.2 51.7 %collective-permute-done = bf16[1,24,384]{2,1,0:T(8,128)(2,1)S(1)} collective-permute-done((bf16[1,24,384]{2,1,0:T(8,128)(2,1)S(1)}, bf16[1,24,384]{2,1,0:T(8,128)(2,1)S(1)}, u32[]{:S(2)}, u32[]{:S(2)}) %collective-permute-start) | collective-permute-done | bytes 18464 | tf_op jit(solution)/shard_map/ppermute | solution.py:333
  70.8 0.8 collective-permute-start.1
  71.7 4.1 %collective-permute-done.1 = bf16[2,24,384]{2,1,0:T(8,128)(2,1)S(1)} collective-permute-done((bf16[2,24,384]{2,1,0:T(8,128)(2,1)S(1)}, bf16[2,24,384]{2,1,0:T(8,128)(2,1)S(1)}, u32[]{:S(2)}, u32[]{:S(2)}) %collective-permute-start.1) | collective-permute-done | bytes 36896 | tf_op jit(solution)/shard_map/ppermute | solution.py:333
  75.8 4.6 %collective-permute-start.2 = (bf16[4,24,384]{2,1,0:T(8,128)(2,1)S(1)}, bf16[4,24,384]{2,1,0:T(8,128)(2,1)S(1)}, u32[]{:S(2)}, u32[]{:S(2)}) collective-permute-start(bf16[4,24,384]{2,1,0:T(8,128)(2,1)S(1)} %pad_maximum_fusion.5), channel_id=1, source_target_pairs={{0,8},{1,9},{2,10},{3,11},{4,12},{5,13},{6,14},{7,15},{8,0},{9,1},... | collective-permute-start | bytes 221192 | tf_op jit(solution)/shard_map/ppermute | solution.py:333
  80.4 4.3 %collective-permute-done.2 = bf16[4,24,384]{2,1,0:T(8,128)(2,1)S(1)} collective-permute-done((bf16[4,24,384]{2,1,0:T(8,128)(2,1)S(1)}, bf16[4,24,384]{2,1,0:T(8,128)(2,1)S(1)}, u32[]{:S(2)}, u32[]{:S(2)}) %collective-permute-start.2) | collective-permute-done | bytes 73760 | tf_op jit(solution)/shard_map/ppermute | solution.py:333
  84.7 0.5 collective-permute-start.3
  85.2 2.6 %collective-permute-start.4 = (bf16[192,384]{1,0:T(8,128)(2,1)S(1)}, bf16[192,384]{1,0:T(8,128)(2,1)S(1)}, u32[]{:S(2)}, u32[]{:S(2)}) collective-permute-start(bf16[192,384]{1,0:T(8,128)(2,1)S(1)} %bitcast.49), channel_id=1, source_target_pairs={{0,32},{1,33},{2,34},{3,35},{4,36},{5,37},{6,38},{7,39},{8,40},{9,... | collective-permute-start | bytes 442376 | tf_op jit(solution)/shard_map/ppermute | solution.py:335
  87.8 1.9 collective-permute-start.5
  89.9 2.6 %collective-permute-done.4 = bf16[192,384]{1,0:T(8,128)(2,1)S(1)} collective-permute-done((bf16[192,384]{1,0:T(8,128)(2,1)S(1)}, bf16[192,384]{1,0:T(8,128)(2,1)S(1)}, u32[]{:S(2)}, u32[]{:S(2)}) %collective-permute-start.4) | collective-permute-done | bytes 147488 | tf_op jit(solution)/shard_map/ppermute | solution.py:335
  92.5 1.1 collective-permute-done.5
  93.6 1.6 collective-permute-start.6
  95.2 1.7 collective-permute-start.7
  97.0 9.3 %collective-permute-done.6.refs_1_ = bf16[768,384]{1,0:T(8,128)(2,1)S(1)} collective-permute-done((bf16[768,384]{1,0:T(8,128)(2,1)S(1)}, bf16[768,384]{1,0:T(8,128)(2,1)S(1)}, u32[]{:S(2)}, u32[]{:S(2)}) %collective-permute-start.6) | collective-permute-done | bytes 589856 | tf_op jit(solution)/shard_map/ppermute | solution.py:297
  106.3 0.7 slice.129
  107.0 1.5 collective-permute-start.8
  108.5 1.7 slice.130
  110.2 1.8 collective-permute-start.9
  112.0 0.5 collective-permute-start.12
  112.5 0.7 tile.4
  113.2 1.6 tile.10
  114.8 0.5 collective-permute-done.8.refs_3_
  115.3 2.0 collective-permute-done.9.refs_4_
  117.3 1.4 and_convert_fusion.mask_ref
  118.8 0.7 copy-done
  119.5 0.7 copy-done.2
  120.2 0.8 copy-done.4
  121.1 5.6 %forward.1 = (bf16[192,1536]{1,0:T(8,128)(2,1)S(1)}, bf16[192,1536]{1,0:T(8,128)(2,1)S(1)}, bf16[192,1536]{1,0:T(8,128)(2,1)S(1)}, bf16[192,1536]{1,0:T(8,128)(2...) custom-call(f32[128,128]{1,0:T(8,128)S(1)} %copy-done.4, bf16[512,2304]{1,0:T(8,128)(2,1)S(1)} %bitcast.41), custom_call_target="tpu_custom_call" | custom-call | bytes 21000000 | tf_op jit(solution)/shard_map/forward/pallas_call | solution.py:137
  126.7 3.7 %weight.1 = (bf16[4,768,384]{2,1,0:T(8,128)(2,1)S(1)}, bf16[4,768,384]{2,1,0:T(8,128)(2,1)S(1)}, bf16[192,1536]{1,0:T(8,128)(2,1)S(1)}) custom-call(s32[4]{0:T(128)S(1)} %pad_add_fusion.at, bf16[192,1536]{1,0:T(8,128)(2,1)S(1)} %get-tuple-element.47.mixed, bf16[192,1536]{1,0:T(8,128)(2,1)S(1)} %get-tuple-element.48.grad), custom_call_target="tpu_custom_call" | custom-call | bytes 14000000 | tf_op jit(solution)/shard_map/weight/pallas_call | solution.py:176
  130.4 0.6 collective-permute-start.15
  131.0 5.4 %project.1 = (bf16[192,1536]{1,0:T(8,128)(2,1)S(1)}, bf16[192,1536]{1,0:T(8,128)(2,1)S(1)}) custom-call(s32[4]{0:T(128)S(1)} %pad_add_fusion.at, bf16[192,1536]{1,0:T(8,128)(2,1)S(1)} %get-tuple-element.51.ordered, bf16[192,1536]{1,0:T(8,128)(2,1)S(1)} %get-tuple-element.48.grad, bf16[768,384]{1,0:T(8,128)(2,1)S(1)} %pad_maximum_fusion.refs_0_, ...), custom_call_target="tpu_custom_call" | custom-call | bytes 21000000 | tf_op jit(solution)/shard_map/project/pallas_call | solution.py:228
  136.4 1.5 fusion.3
  137.9 1.6 collective-permute-start.16
  139.5 1.7 collective-permute-start.17
  141.2 6.8 %backward.1 = bf16[512,2304]{1,0:T(8,128)(2,1)} custom-call(bf16[192,1536]{1,0:T(8,128)(2,1)S(1)} %get-tuple-element.44.q, bf16[192,1536]{1,0:T(8,128)(2,1)S(1)} %get-tuple-element.45.k, bf16[192,1536]{1,0:T(8,128)(2,1)S(1)} %get-tuple-element.46.v, bf16[192,1536]{1,0:T(8,128)(2,1)S(1)} %get-tuple-element.63.mixed_grad, ...), custom_call_target="tpu_custom_call" | custom-call | bytes 21000000 | tf_op jit(solution)/shard_map/backward/pallas_call | solution.py:255
  148.3 9.6 %all-to-all-start.1 = ((bf16[64,8,2304]{2,1,0:T(8,128)(2,1)}), bf16[64,8,2304]{2,1,0:T(8,128)(2,1)S(1)}, u32[]{:S(2)}, u32[]{:S(2)}) async-start(bf16[64,8,2304]{2,1,0:T(8,128)(2,1)} %bitcast.17), calls=%async_computation.1 | async-start | bytes 4718592 | tf_op jit(solution)/shard_map/all_to_all | solution.py:344
  157.9 1.0 add_convert_fusion.6
  159.1 1.2 collective-permute-start.18
  160.3 1.0 add_convert_fusion.5
  161.4 2.4 collective-permute-start.19
  163.8 12.0 %collective-permute-done.18 = bf16[768,384]{1,0:T(8,128)(2,1)S(1)} collective-permute-done((bf16[768,384]{1,0:T(8,128)(2,1)S(1)}, bf16[768,384]{1,0:T(8,128)(2,1)S(1)}, u32[]{:S(2)}, u32[]{:S(2)}) %collective-permute-start.18) | collective-permute-done | bytes 589856 | tf_op jit(solution)/shard_map/ppermute | solution.py:297
  175.8 1.0 collective-permute-done.19
  177.1 1.6 collective-permute-start.20
  178.7 0.5 collective-permute-start.21
  179.2 2.3 collective-permute-start.22
  181.4 4.3 %collective-permute-done.20 = bf16[192,384]{1,0:T(8,128)(2,1)S(1)} collective-permute-done((bf16[192,384]{1,0:T(8,128)(2,1)S(1)}, bf16[192,384]{1,0:T(8,128)(2,1)S(1)}, u32[]{:S(2)}, u32[]{:S(2)}) %collective-permute-start.20) | collective-permute-done | bytes 147488 | tf_op jit(solution)/shard_map/ppermute | solution.py:314
  185.8 1.1 collective-permute-done.21
  186.8 4.0 %collective-permute-done.22 = bf16[192,384]{1,0:T(8,128)(2,1)S(1)} collective-permute-done((bf16[192,384]{1,0:T(8,128)(2,1)S(1)}, bf16[192,384]{1,0:T(8,128)(2,1)S(1)}, u32[]{:S(2)}, u32[]{:S(2)}) %collective-permute-start.22) | collective-permute-done | bytes 147488 | tf_op jit(solution)/shard_map/ppermute | solution.py:314
  190.9 9.5 %collective-permute-start.23 = (bf16[4,24,384]{2,1,0:T(8,128)(2,1)S(1)}, bf16[4,24,384]{2,1,0:T(8,128)(2,1)S(1)}, u32[]{:S(2)}, u32[]{:S(2)}) collective-permute-start(bf16[4,24,384]{2,1,0:T(8,128)(2,1)S(1)} %bitcast.53), channel_id=1, source_target_pairs={{0,8},{1,9},{2,10},{3,11},{4,12},{5,13},{6,14},{7,15},{8,0},{9,1},... | collective-permute-start | bytes 221192 | tf_op jit(solution)/shard_map/ppermute | solution.py:317
  200.5 15.7 %collective-permute-done.23 = bf16[4,24,384]{2,1,0:T(8,128)(2,1)S(1)} collective-permute-done((bf16[4,24,384]{2,1,0:T(8,128)(2,1)S(1)}, bf16[4,24,384]{2,1,0:T(8,128)(2,1)S(1)}, u32[]{:S(2)}, u32[]{:S(2)}) %collective-permute-start.23) | collective-permute-done | bytes 73760 | tf_op jit(solution)/shard_map/ppermute | solution.py:317
  216.2 2.2 collective-permute-start.24
  218.4 2.7 %collective-permute-done.24 = bf16[2,24,384]{2,1,0:T(8,128)(2,1)S(1)} collective-permute-done((bf16[2,24,384]{2,1,0:T(8,128)(2,1)S(1)}, bf16[2,24,384]{2,1,0:T(8,128)(2,1)S(1)}, u32[]{:S(2)}, u32[]{:S(2)}) %collective-permute-start.24) | collective-permute-done | bytes 36896 | tf_op jit(solution)/shard_map/ppermute | solution.py:317
  221.2 2.3 collective-permute-start.25
  223.5 1.7 collective-permute-done.25
  225.3 1.1 collective-permute-start.26
  226.4 3.4 %collective-permute-start.27 = (f32[24,384]{1,0:T(8,128)S(1)}, f32[24,384]{1,0:T(8,128)S(1)}, u32[]{:S(2)}, u32[]{:S(2)}) collective-permute-start(f32[24,384]{1,0:T(8,128)S(1)} %add_bitcast_fusion), channel_id=1, source_target_pairs={{0,128},{64,192},{128,0},{192,64},{1,129},{65,193},{129,1},{193,65... | collective-permute-start | bytes 110600 | tf_op jit(solution)/shard_map/ppermute | solution.py:297
  229.8 1.0 collective-permute-start.28
  230.8 1.3 collective-permute-done.27
  232.1 1.6 collective-permute-done.28
  233.8 0.7 pad_maximum_fusion.4
  234.4 1.4 copy-done.5
  235.9 4.4 %unpack.1 = (bf16[192,1536]{1,0:T(8,128)(2,1)}, bf16[192,1536]{1,0:T(8,128)(2,1)}, bf16[192,1536]{1,0:T(8,128)(2,1)}, bf16[192,1536]{1,0:T(8,128)(2,1)}) custom-call(bf16[512,2304]{1,0:T(8,128)(2,1)} %bitcast.42), custom_call_target="tpu_custom_call" | custom-call | bytes 14000000 | tf_op jit(solution)/shard_map/unpack/pallas_call | solution.py:98
  (55 shorter events, 1.5 us)
Async XLA Ops:
  5.3 12.3 %copy-start.7 = (bf16[24,1536]{1,0:T(8,128)(2,1)S(1)}, bf16[24,1536]{1,0:T(8,128)(2,1)}, u32[]{:S(2)}) copy-start(bf16[24,1536]{1,0:T(8,128)(2,1)} %param.10) | copy-start | bytes 221188
  5.3 114.9 %all-to-all-start = ((bf16[64,8,2304]{2,1,0:T(8,128)(2,1)}), bf16[64,8,2304]{2,1,0:T(8,128)(2,1)S(1)}, u32[]{:S(2)}, u32[]{:S(2)}) async-start(bf16[64,8,2304]{2,1,0:T(8,128)(2,1)} %bitcast.43), calls=%async_computation | async-start | bytes 4718592 | tf_op jit(solution)/shard_map/all_to_all | solution.py:344
  17.6 53.2 %collective-permute-start = (bf16[1,24,384]{2,1,0:T(8,128)(2,1)S(1)}, bf16[1,24,384]{2,1,0:T(8,128)(2,1)S(1)}, u32[]{:S(2)}, u32[]{:S(2)}) collective-permute-start(bf16[1,24,384]{2,1,0:T(8,128)(2,1)S(1)} %select_bitcast_fusion), channel_id=1, source_target_pairs={{0,2},{1,3},{2,0},{3,1},{4,6},{5,7},{6,4},{7,5},{8,10},{9,11},{10,... | collective-permute-start | bytes 55304 | tf_op jit(solution)/shard_map/ppermute | solution.py:333
  70.8 4.9 %collective-permute-start.1 = (bf16[2,24,384]{2,1,0:T(8,128)(2,1)S(1)}, bf16[2,24,384]{2,1,0:T(8,128)(2,1)S(1)}, u32[]{:S(2)}, u32[]{:S(2)}) collective-permute-start(bf16[2,24,384]{2,1,0:T(8,128)(2,1)S(1)} %pad_maximum_fusion.6), channel_id=1, source_target_pairs={{0,4},{1,5},{2,6},{3,7},{4,0},{5,1},{6,2},{7,3},{8,12},{9,13},{10,... | collective-permute-start | bytes 110600 | tf_op jit(solution)/shard_map/ppermute | solution.py:333
  75.8 8.9 %collective-permute-start.2 = (bf16[4,24,384]{2,1,0:T(8,128)(2,1)S(1)}, bf16[4,24,384]{2,1,0:T(8,128)(2,1)S(1)}, u32[]{:S(2)}, u32[]{:S(2)}) collective-permute-start(bf16[4,24,384]{2,1,0:T(8,128)(2,1)S(1)} %pad_maximum_fusion.5), channel_id=1, source_target_pairs={{0,8},{1,9},{2,10},{3,11},{4,12},{5,13},{6,14},{7,15},{8,0},{9,1},... | collective-permute-start | bytes 221192 | tf_op jit(solution)/shard_map/ppermute | solution.py:333
  84.7 27.8 %copy-start.8 = (s32[1,64]{1,0:T(1,128)S(1)}, s32[1,64]{1,0:T(1,128)}, u32[]{:S(2)}) copy-start(s32[1,64]{1,0:T(1,128)} %param.11) | copy-start | bytes 772
  84.7 5.2 %collective-permute-start.3 = (bf16[192,384]{1,0:T(8,128)(2,1)S(1)}, bf16[192,384]{1,0:T(8,128)(2,1)S(1)}, u32[]{:S(2)}, u32[]{:S(2)}) collective-permute-start(bf16[192,384]{1,0:T(8,128)(2,1)S(1)} %bitcast.48), channel_id=1, source_target_pairs={{0,48},{1,49},{2,50},{3,51},{4,52},{5,53},{6,54},{7,55},{8,56},{9,... | collective-permute-start | bytes 442376 | tf_op jit(solution)/shard_map/ppermute | solution.py:335
  85.2 7.3 %collective-permute-start.4 = (bf16[192,384]{1,0:T(8,128)(2,1)S(1)}, bf16[192,384]{1,0:T(8,128)(2,1)S(1)}, u32[]{:S(2)}, u32[]{:S(2)}) collective-permute-start(bf16[192,384]{1,0:T(8,128)(2,1)S(1)} %bitcast.49), channel_id=1, source_target_pairs={{0,32},{1,33},{2,34},{3,35},{4,36},{5,37},{6,38},{7,39},{8,40},{9,... | collective-permute-start | bytes 442376 | tf_op jit(solution)/shard_map/ppermute | solution.py:335
  87.8 5.8 %collective-permute-start.5 = (bf16[192,384]{1,0:T(8,128)(2,1)S(1)}, bf16[192,384]{1,0:T(8,128)(2,1)S(1)}, u32[]{:S(2)}, u32[]{:S(2)}) collective-permute-start(bf16[192,384]{1,0:T(8,128)(2,1)S(1)} %bitcast.50), channel_id=1, source_target_pairs={{0,16},{1,17},{2,18},{3,19},{4,20},{5,21},{6,22},{7,23},{8,24},{9,... | collective-permute-start | bytes 442376 | tf_op jit(solution)/shard_map/ppermute | solution.py:335
  93.6 12.6 %collective-permute-start.6 = (bf16[768,384]{1,0:T(8,128)(2,1)S(1)}, bf16[768,384]{1,0:T(8,128)(2,1)S(1)}, u32[]{:S(2)}, u32[]{:S(2)}) collective-permute-start(bf16[768,384]{1,0:T(8,128)(2,1)S(1)} %pad_maximum_fusion.refs_0_), channel_id=1, source_target_pairs={{0,64},{64,128},{128,192},{192,0},{1,65},{65,129},{129,193},{193,1... | collective-permute-start | bytes 1769480 | tf_op jit(solution)/shard_map/ppermute | solution.py:297
  95.2 13.3 %collective-permute-start.7 = (bf16[768,384]{1,0:T(8,128)(2,1)S(1)}, bf16[768,384]{1,0:T(8,128)(2,1)}, u32[]{:S(2)}, u32[]{:S(2)}) collective-permute-start(bf16[768,384]{1,0:T(8,128)(2,1)S(1)} %pad_maximum_fusion.refs_0_), channel_id=1, source_target_pairs={{0,192},{64,0},{128,64},{192,128},{1,193},{65,1},{129,65},{193,129... | collective-permute-start | bytes 1769480 | tf_op jit(solution)/shard_map/ppermute | solution.py:297
  97.0 21.8 %collective-permute-start.10 = (bf16[768,384]{1,0:T(8,128)(2,1)S(1)}, bf16[768,384]{1,0:T(8,128)(2,1)}, u32[]{:S(2)}, u32[]{:S(2)}) collective-permute-start(bf16[768,384]{1,0:T(8,128)(2,1)S(1)} %pad_maximum_fusion.refs_0_), channel_id=1, source_target_pairs={{0,1},{1,0},{2,3},{3,2},{4,5},{5,4},{6,7},{7,6},{8,9},{9,8},{10,11... | collective-permute-start | bytes 1769480 | tf_op jit(solution)/shard_map/ppermute | solution.py:340
  107.0 8.2 %collective-permute-start.8 = (bf16[384,384]{1,0:T(8,128)(2,1)}, bf16[384,384]{1,0:T(8,128)(2,1)}, u32[]{:S(2)}, u32[]{:S(2)}) collective-permute-start(bf16[384,384]{1,0:T(8,128)(2,1)} %slice.129), channel_id=1, source_target_pairs={{0,64},{64,128},{128,192},{192,0},{1,65},{65,129},{129,193},{193,1... | collective-permute-start | bytes 884744 | tf_op jit(solution)/shard_map/ppermute | solution.py:297
  110.2 7.0 %collective-permute-start.9 = (bf16[384,384]{1,0:T(8,128)(2,1)}, bf16[384,384]{1,0:T(8,128)(2,1)}, u32[]{:S(2)}, u32[]{:S(2)}) collective-permute-start(bf16[384,384]{1,0:T(8,128)(2,1)} %slice.130), channel_id=1, source_target_pairs={{0,192},{64,0},{128,64},{192,128},{1,193},{65,1},{129,65},{193,129... | collective-permute-start | bytes 884744 | tf_op jit(solution)/shard_map/ppermute | solution.py:297
  112.0 6.8 %collective-permute-start.11 = (bf16[768,384]{1,0:T(8,128)(2,1)S(1)}, bf16[768,384]{1,0:T(8,128)(2,1)}, u32[]{:S(2)}, u32[]{:S(2)}) collective-permute-start(bf16[768,384]{1,0:T(8,128)(2,1)S(1)} %collective-permute-done.6.refs_1_), channel_id=1, source_target_pairs={{0,1},{1,0},{2,3},{3,2},{4,5},{5,4},{6,7},{7,6},{8,9},{9,8},{10,11... | collective-permute-start | bytes 1769480 | tf_op jit(solution)/shard_map/ppermute | solution.py:340
  112.0 6.8 %collective-permute-start.12 = (bf16[768,384]{1,0:T(8,128)(2,1)}, bf16[768,384]{1,0:T(8,128)(2,1)}, u32[]{:S(2)}, u32[]{:S(2)}) collective-permute-start(bf16[768,384]{1,0:T(8,128)(2,1)} %collective-permute-done.7.refs_2_), channel_id=1, source_target_pairs={{0,1},{1,0},{2,3},{3,2},{4,5},{5,4},{6,7},{7,6},{8,9},{9,8},{10,11... | collective-permute-start | bytes 1769480 | tf_op jit(solution)/shard_map/ppermute | solution.py:340
  115.3 3.5 %collective-permute-start.13 = (bf16[384,384]{1,0:T(8,128)(2,1)}, bf16[384,384]{1,0:T(8,128)(2,1)S(1)}, u32[]{:S(2)}, u32[]{:S(2)}) collective-permute-start(bf16[384,384]{1,0:T(8,128)(2,1)} %collective-permute-done.8.refs_3_), channel_id=1, source_target_pairs={{0,1},{1,0},{2,3},{3,2},{4,5},{5,4},{6,7},{7,6},{8,9},{9,8},{10,11... | collective-permute-start | bytes 884744 | tf_op jit(solution)/shard_map/ppermute | solution.py:340
  117.2 2.3 collective-permute-start.14
  118.8 0.7 copy-start
  119.5 0.7 copy-start.2
  120.2 0.8 copy-start.4
  126.7 4.3 %copy-start.1 = (bf16[384,384]{1,0:T(8,128)(2,1)S(1)}, bf16[384,384]{1,0:T(8,128)(2,1)}, u32[]{:S(2)}) copy-start(bf16[384,384]{1,0:T(8,128)(2,1)} %copy-done) | copy-start | bytes 884740
  126.7 4.3 %copy-start.3 = (bf16[384,384]{1,0:T(8,128)(2,1)S(1)}, bf16[384,384]{1,0:T(8,128)(2,1)}, u32[]{:S(2)}) copy-start(bf16[384,384]{1,0:T(8,128)(2,1)} %copy-done.2) | copy-start | bytes 884740
  130.4 6.0 %collective-permute-start.15 = (bf16[4,768,384]{2,1,0:T(8,128)(2,1)S(1)}, bf16[4,768,384]{2,1,0:T(8,128)(2,1)S(1)}, u32[]{:S(2)}, u32[]{:S(2)}) collective-permute-start(bf16[4,768,384]{2,1,0:T(8,128)(2,1)S(1)} %get-tuple-element.50), channel_id=1, source_target_pairs={{0,1},{1,0},{2,3},{3,2},{4,5},{5,4},{6,7},{7,6},{8,9},{9,8},{10,11... | collective-permute-start | bytes 7077896 | tf_op jit(solution)/shard_map/ppermute | solution.py:361
  137.9 10.4 %collective-permute-start.16 = (bf16[384,384]{1,0:T(8,128)(2,1)S(1)}, bf16[384,384]{1,0:T(8,128)(2,1)}, u32[]{:S(2)}, u32[]{:S(2)}) collective-permute-start(bf16[384,384]{1,0:T(8,128)(2,1)S(1)} %get-tuple-element.85), channel_id=1, source_target_pairs={{0,64},{64,128},{128,192},{192,0},{1,65},{65,129},{129,193},{193,1... | collective-permute-start | bytes 884744 | tf_op jit(solution)/shard_map/ppermute | solution.py:297
  139.5 8.8 %collective-permute-start.17 = (bf16[384,384]{1,0:T(8,128)(2,1)S(1)}, bf16[384,384]{1,0:T(8,128)(2,1)}, u32[]{:S(2)}, u32[]{:S(2)}) collective-permute-start(bf16[384,384]{1,0:T(8,128)(2,1)S(1)} %get-tuple-element.84), channel_id=1, source_target_pairs={{0,192},{64,0},{128,64},{192,128},{1,193},{65,1},{129,65},{193,129... | collective-permute-start | bytes 884744 | tf_op jit(solution)/shard_map/ppermute | solution.py:297
  148.3 86.2 %all-to-all-start.1 = ((bf16[64,8,2304]{2,1,0:T(8,128)(2,1)}), bf16[64,8,2304]{2,1,0:T(8,128)(2,1)S(1)}, u32[]{:S(2)}, u32[]{:S(2)}) async-start(bf16[64,8,2304]{2,1,0:T(8,128)(2,1)} %bitcast.17), calls=%async_computation.1 | async-start | bytes 4718592 | tf_op jit(solution)/shard_map/all_to_all | solution.py:344
  159.1 17.7 %copy-start.6 = (bf16[768,384]{1,0:T(8,128)(2,1)S(1)}, bf16[768,384]{1,0:T(8,128)(2,1)}, u32[]{:S(2)}) copy-start(bf16[768,384]{1,0:T(8,128)(2,1)} %get-tuple-element.72) | copy-start | bytes 1769476
  159.1 16.8 %collective-permute-start.18 = (bf16[768,384]{1,0:T(8,128)(2,1)S(1)}, bf16[768,384]{1,0:T(8,128)(2,1)S(1)}, u32[]{:S(2)}, u32[]{:S(2)}) collective-permute-start(bf16[768,384]{1,0:T(8,128)(2,1)S(1)} %pad_maximum_fusion.1), channel_id=1, source_target_pairs={{0,64},{64,128},{128,192},{192,0},{1,65},{65,129},{129,193},{193,1... | collective-permute-start | bytes 1769480 | tf_op jit(solution)/shard_map/ppermute | solution.py:297
  161.4 15.4 %collective-permute-start.19 = (bf16[768,384]{1,0:T(8,128)(2,1)S(1)}, bf16[768,384]{1,0:T(8,128)(2,1)S(1)}, u32[]{:S(2)}, u32[]{:S(2)}) collective-permute-start(bf16[768,384]{1,0:T(8,128)(2,1)S(1)} %pad_maximum_fusion.2), channel_id=1, source_target_pairs={{0,192},{64,0},{128,64},{192,128},{1,193},{65,1},{129,65},{193,129... | collective-permute-start | bytes 1769480 | tf_op jit(solution)/shard_map/ppermute | solution.py:297
  177.1 8.7 %collective-permute-start.20 = (bf16[192,384]{1,0:T(8,128)(2,1)S(1)}, bf16[192,384]{1,0:T(8,128)(2,1)S(1)}, u32[]{:S(2)}, u32[]{:S(2)}) collective-permute-start(bf16[192,384]{1,0:T(8,128)(2,1)S(1)} %get-tuple-element.81), channel_id=1, source_target_pairs={{0,16},{1,17},{2,18},{3,19},{4,20},{5,21},{6,22},{7,23},{8,24},{9,... | collective-permute-start | bytes 442376 | tf_op jit(solution)/shard_map/ppermute | solution.py:314
  178.7 8.1 %collective-permute-start.21 = (bf16[192,384]{1,0:T(8,128)(2,1)S(1)}, bf16[192,384]{1,0:T(8,128)(2,1)S(1)}, u32[]{:S(2)}, u32[]{:S(2)}) collective-permute-start(bf16[192,384]{1,0:T(8,128)(2,1)S(1)} %get-tuple-element.83), channel_id=1, source_target_pairs={{0,48},{1,49},{2,50},{3,51},{4,52},{5,53},{6,54},{7,55},{8,56},{9,... | collective-permute-start | bytes 442376 | tf_op jit(solution)/shard_map/ppermute | solution.py:314
  179.2 11.7 %collective-permute-start.22 = (bf16[192,384]{1,0:T(8,128)(2,1)S(1)}, bf16[192,384]{1,0:T(8,128)(2,1)S(1)}, u32[]{:S(2)}, u32[]{:S(2)}) collective-permute-start(bf16[192,384]{1,0:T(8,128)(2,1)S(1)} %get-tuple-element.82), channel_id=1, source_target_pairs={{0,32},{1,33},{2,34},{3,35},{4,36},{5,37},{6,38},{7,39},{8,40},{9,... | collective-permute-start | bytes 442376 | tf_op jit(solution)/shard_map/ppermute | solution.py:314
  190.9 25.2 %collective-permute-start.23 = (bf16[4,24,384]{2,1,0:T(8,128)(2,1)S(1)}, bf16[4,24,384]{2,1,0:T(8,128)(2,1)S(1)}, u32[]{:S(2)}, u32[]{:S(2)}) collective-permute-start(bf16[4,24,384]{2,1,0:T(8,128)(2,1)S(1)} %bitcast.53), channel_id=1, source_target_pairs={{0,8},{1,9},{2,10},{3,11},{4,12},{5,13},{6,14},{7,15},{8,0},{9,1},... | collective-permute-start | bytes 221192 | tf_op jit(solution)/shard_map/ppermute | solution.py:317
  216.2 4.9 %collective-permute-start.24 = (bf16[2,24,384]{2,1,0:T(8,128)(2,1)S(1)}, bf16[2,24,384]{2,1,0:T(8,128)(2,1)S(1)}, u32[]{:S(2)}, u32[]{:S(2)}) collective-permute-start(bf16[2,24,384]{2,1,0:T(8,128)(2,1)S(1)} %slice.142), channel_id=1, source_target_pairs={{0,4},{1,5},{2,6},{3,7},{4,0},{5,1},{6,2},{7,3},{8,12},{9,13},{10,... | collective-permute-start | bytes 110600 | tf_op jit(solution)/shard_map/ppermute | solution.py:317
  221.2 4.1 %collective-permute-start.25 = (bf16[1,24,384]{2,1,0:T(8,128)(2,1)S(1)}, bf16[1,24,384]{2,1,0:T(8,128)(2,1)S(1)}, u32[]{:S(2)}, u32[]{:S(2)}) collective-permute-start(bf16[1,24,384]{2,1,0:T(8,128)(2,1)S(1)} %slice.144), channel_id=1, source_target_pairs={{0,2},{1,3},{2,0},{3,1},{4,6},{5,7},{6,4},{7,5},{8,10},{9,11},{10,... | collective-permute-start | bytes 55304 | tf_op jit(solution)/shard_map/ppermute | solution.py:317
  225.3 5.6 %collective-permute-start.26 = (f32[24,384]{1,0:T(8,128)S(1)}, f32[24,384]{1,0:T(8,128)S(1)}, u32[]{:S(2)}, u32[]{:S(2)}) collective-permute-start(f32[24,384]{1,0:T(8,128)S(1)} %add_bitcast_fusion), channel_id=1, source_target_pairs={{0,64},{64,128},{128,192},{192,0},{1,65},{65,129},{129,193},{193,1... | collective-permute-start | bytes 110600 | tf_op jit(solution)/shard_map/ppermute | solution.py:297
  226.4 5.7 %collective-permute-start.27 = (f32[24,384]{1,0:T(8,128)S(1)}, f32[24,384]{1,0:T(8,128)S(1)}, u32[]{:S(2)}, u32[]{:S(2)}) collective-permute-start(f32[24,384]{1,0:T(8,128)S(1)} %add_bitcast_fusion), channel_id=1, source_target_pairs={{0,128},{64,192},{128,0},{192,64},{1,129},{65,193},{129,1},{193,65... | collective-permute-start | bytes 110600 | tf_op jit(solution)/shard_map/ppermute | solution.py:297
  229.8 4.0 %collective-permute-start.28 = (f32[24,384]{1,0:T(8,128)S(1)}, f32[24,384]{1,0:T(8,128)S(1)}, u32[]{:S(2)}, u32[]{:S(2)}) collective-permute-start(f32[24,384]{1,0:T(8,128)S(1)} %add_bitcast_fusion), channel_id=1, source_target_pairs={{0,192},{64,0},{128,64},{192,128},{1,193},{65,1},{129,65},{193,129... | collective-permute-start | bytes 110600 | tf_op jit(solution)/shard_map/ppermute | solution.py:297
  234.4 1.4 copy-start.5

commit v4 on v3

--- a/solution.py
+++ b/solution.py
@@ -101,7 +101,7 @@
         in_specs=[message_block],
         out_specs=[place_block] * 4,
         out_shape=[rows_shape] * 4,
-        compiler_params=params(60),
+        compiler_params=params(10),
         cost_estimate=cost(4),
         name="unpack",
     )(message)
@@ -150,10 +150,10 @@
     for side in range(2):
         core = at[0] if side == 0 else 1 - at[0]
         for dy in range(NY):
-            for dz in range(NZ):
-                y, z = (at[2] + dy) % NY, at[3] ^ dz
+            for z in range(NZ):
+                y = (at[2] + dy) % NY
                 there = pl.multiple_of((y * NZ + z) * 2 * STRIP + core * STRIP, 8)
-                copy(side, (dy * NZ + dz) * STRIP, there)
+                copy(side, (dy * NZ + z) * STRIP, there)
 
 
 def weight_kernel(at, mixed, grad, keep, send, ordered, turned, strips):
@@ -309,35 +309,51 @@
     return add_up([parts[0], along_x(ahead, 1), along_x(back, -1)]).astype(BF)
 
 
-def reduce_rest(chip):
+def reduce_y(chip):
     chip = chip.reshape(NY, NZ * STRIP, QUARTER)
     came = [lax.ppermute(chip[d], "seq", seq_shift(d, 0, 0)) for d in (1, 3, 2)]
-    strips = add_up([chip[0]] + came).astype(BF).reshape(NZ, STRIP, QUARTER)
-    for bit in (4, 2, 1):
-        came = lax.ppermute(strips[bit:], "seq", seq_flip(bit))
-        strips = add_up([strips[:bit], came])
-        if bit > 1:
-            strips = strips.astype(BF)
-    own = strips[0]
-    came = {d: along_x(own, d) for d in (1, 3, 2)}
+    return add_up([chip[0]] + came).astype(BF).reshape(NZ // 2, 2, STRIP, QUARTER)
+
+
+def reduce_z_pairs(pairs):
+    at = lax.axis_index("seq") // 4 % (NZ // 2)
+    pick = lambda n: lax.dynamic_index_in_dim(pairs, at ^ n, 0, keepdims=False)
+    came = [lax.ppermute(pick(n), "seq", seq_flip(2 * n)) for n in (2, 1, 3)]
+    return add_up([pick(0)] + came).astype(BF)
+
+
+def reduce_z_last(pair):
+    odd = lax.axis_index("seq") // 2 % 2 == 1
+    came = lax.ppermute(jnp.where(odd, pair[0], pair[1]), "seq", seq_flip(1))
+    return add_up([jnp.where(odd, pair[1], pair[0]), came])
+
+
+def gather_x(own):
+    flip = lambda x, n: lax.ppermute(x, "dp", [(i, i ^ n) for i in range(NX)])
+    near = flip(own, 1)
+    far = flip(jnp.stack([own, near]), 2)
     place = lax.axis_index("dp")
-    quarters = [lax.select_n((place - n) % NX, own, came[1], came[2], came[3]) for n in range(NX)]
+    quarters = [lax.select_n(place ^ n, own, near, far[0], far[1]) for n in range(NX)]
     return jnp.concatenate(quarters, axis=1)
 
 
-def gather_weight(out_weight):
+def gather_weight_y(out_weight):
     place = lax.axis_index("dp")
     own = lax.select_n(place, *[out_weight[:, QUARTER * n : QUARTER * n + QUARTER] for n in range(NX)])
-    own = own[None]
-    for bit in (1, 2, 4):
-        own = jnp.concatenate([own, lax.ppermute(own, "seq", seq_flip(bit))], axis=0)
-    own = own.reshape(NZ * STRIP, QUARTER)
     came = {d: lax.ppermute(own, "seq", seq_shift(NY - d, 0, 0)) for d in (1, 3, 2)}
-    own = jnp.concatenate([own, came[1], came[2], came[3]], axis=0)
-    mid = HALF // 2
-    left, right = along_x(own, 1), along_x(own, -1)
-    pieces = [own, left, right, along_x(left[:mid], 1), along_x(right[mid:], -1)]
-    return pieces + [lax.ppermute(piece, "seq", seq_shift(0, 0, 1)) for piece in pieces]
+    return jnp.concatenate([own, came[1], came[2], came[3]], axis=0)
+
+
+def gather_weight_z(part):
+    seq = np.arange(SEQ).reshape(NY, NZ * 2)
+    part = lax.all_gather(part, "seq", axis=0, axis_index_groups=[list(map(int, row)) for row in seq])
+    part = part.reshape(NZ, 2, NY, STRIP, QUARTER).transpose(1, 2, 0, 3, 4).reshape(2, HALF, QUARTER)
+    first = lax.axis_index("seq") % 2 == 0
+    return jnp.where(first, part[0], part[1]), jnp.where(first, part[1], part[0])
+
+
+def swap_cores(x):
+    return lax.ppermute(x, "seq", seq_shift(0, 0, 1))
 
 
 def exchange(message):
@@ -353,20 +369,28 @@
     at = jnp.stack([rank % 2, lax.axis_index("dp"), rank // (2 * NZ), rank // 2 % NZ]).astype(jnp.int32)
 
     flat = [x.reshape(ROWS, WIDTH) for x in (queries, key_field, value_field, out_grad)]
-    message, out_weight = lax.optimization_barrier((pack_call(*flat), out_weight))
-    weights = gather_weight(out_weight)
-    arrived, weights = lax.optimization_barrier((exchange(message), weights))
+    message, part = lax.optimization_barrier((pack_call(*flat), gather_weight_y(out_weight)))
+    own, other = gather_weight_z(part)
+    left, right = along_x(own, 1), along_x(own, -1)
+    arrived, mask, own, other, left, right = lax.optimization_barrier(
+        (exchange(message), mask, own, other, left, right)
+    )
+    mid = HALF // 2
+    pieces = [left, right, along_x(left[:mid], 1), along_x(right[mid:], -1)]
     q, k, v, g, mixed, probs = forward_call(mask, arrived)
+    mixed, pieces = lax.optimization_barrier((mixed, pieces))
     keep, send, ordered = weight_call(at, mixed, g)
-    parts = reduce_chip(keep, lax.ppermute(send, "seq", seq_shift(0, 0, 1)))
+    weights = [own] + pieces + [other] + [swap_cores(piece) for piece in pieces]
+    parts = reduce_chip(keep, swap_cores(send))
     out, mixed_grad = project_call(at, ordered, g, weights)
     parts, mixed_grad = lax.optimization_barrier((parts, mixed_grad))
     right, left = reduce_x_first(parts)
     message = backward_call(q, k, v, mixed_grad, out, probs)
     message, right, left = lax.optimization_barrier((message, right, left))
-    chip = reduce_x_second(parts, right, left)
-    results = unpack_call(exchange(message))
-    weight_grad = reduce_rest(chip)
+    pair = reduce_z_pairs(reduce_y(reduce_x_second(parts, right, left)))
+    came, pair = lax.optimization_barrier((exchange(message), pair))
+    results = unpack_call(came)
+    weight_grad = gather_x(reduce_z_last(pair))
     return tuple(x.reshape(queries.shape) for x in results) + (weight_grad,)
 
 

time: 242 us -> 230 us (0.950)
  starting transfers between devices: 72.4 us -> 53.7 us
  between operations: 0.9 us -> 14.3 us
  waiting for transfers between devices: 121 us -> 117 us
    ppermute x18 -> x17, waiting for transfers between devices: 93.5 us -> 40.1 us  [the longest x3 15 us: reduce_z_pairs(): came = [lax.ppermute(pick(n), 'seq', seq_flip(2 * n)) for n in (2, 1, 3)]]
    all_gather x0 -> x1, waiting for transfers between devices: none -> 48.8 us  [gather_weight_z(): lax.all_gather(part, 'seq', axis=0, axis_index_groups=[list(map(int, row)...]
    ppermute x18 -> x17, starting transfers between devices: 31.6 us -> 22 us  [the longest x3 7.7 us: reduce_z_pairs(): came = [lax.ppermute(pick(n), 'seq', seq_flip(2 * n)) for n in (2, 1, 3)]]
    ppermute x11 -> x8, starting transfers between devices: 19 us -> 12.4 us  [along_x(): return lax.ppermute(x, 'dp', [(i, (i + shift) % NX) for i in range(NX)])]
    all_to_all x2, starting transfers between devices: 21.8 us -> 19.3 us  [exchange(): lax.all_to_all(message, 'seq', split_axis=0, concat_axis=0, tiled=True)]
    ppermute x11 -> x8, waiting for transfers between devices: 27.9 us -> 27.7 us  [along_x(): return lax.ppermute(x, 'dp', [(i, (i + shift) % NX) for i in range(NX)])]
  transfers between devices with their start and end apart: 31 -> 28, of which waited for: 20 -> 15; matrix products, arithmetic and copies ran while one was open for 4% -> 3% of each run, Pallas kernels for 5% -> 11%
where the time goes in v4:
time: 230 us
  waiting for transfers between devices  117 us (51%)
  starting transfers between devices  53.7 us (23%)
  Pallas kernels  28.3 us (12%)
  between operations  14.3 us (6%)
  local copies, waits for them, and re-layouts  9.8 us (4%)
  other arithmetic  6.38 us (3%)
    all_gather x1, waiting for transfers between devices, gather_weight_z(): lax.all_gather(part, 'seq', axis=0, axis_index_groups=[list(map(int, row)...  48.8 us
    ppermute x8, waiting for transfers between devices, along_x(): return lax.ppermute(x, 'dp', [(i, (i + shift) % NX) for i in range(NX)])  27.7 us
    all_to_all x2, starting transfers between devices, exchange(): lax.all_to_all(message, 'seq', split_axis=0, concat_axis=0, tiled=True)  19.3 us
    ppermute x3, waiting for transfers between devices, reduce_z_pairs(): came = [lax.ppermute(pick(n), 'seq', seq_flip(2 * n)) for n in (2, 1, 3)]  15 us
    ppermute x8, starting transfers between devices, along_x(): return lax.ppermute(x, 'dp', [(i, (i + shift) % NX) for i in range(NX)])  12.4 us
    ppermute x3, waiting for transfers between devices, reduce_y(): came = [lax.ppermute(chip[d], 'seq', seq_shift(d, 0, 0)) for d in (1, 3, 2)]  11.4 us
    ppermute x3, starting transfers between devices, reduce_z_pairs(): came = [lax.ppermute(pick(n), 'seq', seq_flip(2 * n)) for n in (2, 1, 3)]  7.7 us
    pallas_call x1, Pallas kernels, backward_call(): pl.pallas_call(backward_kernel, grid=(PLACES,), in_specs=[place_block] *...  6.82 us
  transfers between devices with their start and end apart: 28, of which 15 were waited for; matrix products, arithmetic and copies ran while one was open for 3% of the time, Pallas kernels for 11%

profile of v4, /device:TPU:8, one launch (start us, length us, event | category | flops | bytes accessed | tf_op | source)
XLA Modules:
  0.0 229.8 jit_solution(11891024898255627753)
XLA Ops:
  7.2 0.8 select_select_fusion
  8.0 1.6 collective-permute-start.2
  9.6 2.7 %collective-permute-start.1 = (bf16[24,384]{1,0:T(8,128)(2,1)S(1)}, bf16[24,384]{1,0:T(8,128)(2,1)S(1)}, u32[]{:S(2)}, u32[]{:S(2)}) collective-permute-start(bf16[24,384]{1,0:T(8,128)(2,1)S(1)} %select_select_fusion), channel_id=1, source_target_pairs={{0,32},{1,33},{2,34},{3,35},{4,36},{5,37},{6,38},{7,39},{8,40},{9,... | collective-permute-start | bytes 55304 | tf_op jit(solution)/shard_map/ppermute | solution.py:343
  12.3 0.7 collective-permute-start
  13.0 4.7 %pack.1 = bf16[512,2304]{1,0:T(8,128)(2,1)} custom-call(bf16[192,1536]{1,0:T(8,128)(2,1)} %bitcast.65, bf16[192,1536]{1,0:T(8,128)(2,1)} %bitcast.66, bf16[192,1536]{1,0:T(8,128)(2,1)} %bitcast.67, bf16[192,1536]{1,0:T(8,128)(2,1)} %bitcast.68), custom_call_target="tpu_custom_call" | custom-call | bytes 14000000 | tf_op jit(solution)/shard_map/pack/pallas_call | solution.py:85
  17.6 0.6 pad_maximum_fusion.3
  18.3 10.5 %all-to-all-start = ((bf16[64,8,2304]{2,1,0:T(8,128)(2,1)}), bf16[64,8,2304]{2,1,0:T(8,128)(2,1)S(1)}, u32[]{:S(2)}, u32[]{:S(2)}) async-start(bf16[64,8,2304]{2,1,0:T(8,128)(2,1)} %bitcast.62), calls=%async_computation | async-start | bytes 4718592 | tf_op jit(solution)/shard_map/all_to_all | solution.py:360
  28.8 0.7 all-gather.3.cloned.1.call-update
  29.5 48.8 %all-gather.3.cloned.1.call-done = bf16[1536,384]{1,0:T(8,128)(2,1)} async-done(((bf16[96,384]{1,0:T(8,128)(2,1)}), bf16[1536,384]{1,0:T(8,128)(2,1)}) %all-gather.3.cloned.1.call-update) | async-done | bytes 1179664 | tf_op jit(solution)/shard_map/all_gather | solution.py:349
  78.4 1.4 copy.14
  79.8 0.1 broadcast_select_fusion
  80.0 1.5 collective-permute-start.3
  81.5 1.8 collective-permute-start.4
  83.4 0.7 tile.4
  84.0 0.9 tile.10
  85.0 0.7 and_convert_fusion.mask_ref
  85.7 11.1 %collective-permute-done.3.refs_1_ = bf16[768,384]{1,0:T(8,128)(2,1)} collective-permute-done((bf16[768,384]{1,0:T(8,128)(2,1)S(1)}, bf16[768,384]{1,0:T(8,128)(2,1)}, u32[]{:S(2)}, u32[]{:S(2)}) %collective-permute-start.3) | collective-permute-done | bytes 589856 | tf_op jit(solution)/shard_map/ppermute | solution.py:297
  96.8 1.7 slice.112
  98.5 1.4 collective-permute-start.5
  100.0 1.7 slice.113
  101.7 1.8 collective-permute-start.6
  103.6 0.8 copy-done
  104.4 5.6 %forward.1 = (bf16[192,1536]{1,0:T(8,128)(2,1)S(1)}, bf16[192,1536]{1,0:T(8,128)(2,1)S(1)}, bf16[192,1536]{1,0:T(8,128)(2,1)S(1)}, bf16[192,1536]{1,0:T(8,128)(2...) custom-call(f32[128,128]{1,0:T(8,128)S(1)} %copy-done, bf16[512,2304]{1,0:T(8,128)(2,1)S(1)} %bitcast.57), custom_call_target="tpu_custom_call" | custom-call | bytes 21000000 | tf_op jit(solution)/shard_map/forward/pallas_call | solution.py:137
  110.0 3.7 %weight.1 = (bf16[4,768,384]{2,1,0:T(8,128)(2,1)S(1)}, bf16[4,768,384]{2,1,0:T(8,128)(2,1)S(1)}, bf16[192,1536]{1,0:T(8,128)(2,1)S(1)}) custom-call(s32[4]{0:T(128)S(1)} %pad_add_fusion.at, bf16[192,1536]{1,0:T(8,128)(2,1)S(1)} %get-tuple-element.53.mixed, bf16[192,1536]{1,0:T(8,128)(2,1)S(1)} %get-tuple-element.54.grad), custom_call_target="tpu_custom_call" | custom-call | bytes 14000000 | tf_op jit(solution)/shard_map/weight/pallas_call | solution.py:176
  113.7 0.1 collective-permute-start.7
  113.8 0.5 collective-permute-start.8
  114.3 0.1 collective-permute-start.9
  114.4 0.4 collective-permute-start.10
  114.8 0.1 collective-permute-start.11
  114.9 5.5 %collective-permute-done.10.refs_8_ = bf16[384,384]{1,0:T(8,128)(2,1)S(1)} collective-permute-done((bf16[384,384]{1,0:T(8,128)(2,1)}, bf16[384,384]{1,0:T(8,128)(2,1)S(1)}, u32[]{:S(2)}, u32[]{:S(2)}) %collective-permute-start.10) | collective-permute-done | bytes 294944 | tf_op jit(solution)/shard_map/ppermute | solution.py:356
  120.4 0.7 collective-permute-done.11.refs_9_
  121.1 5.0 %project.1 = (bf16[192,1536]{1,0:T(8,128)(2,1)S(1)}, bf16[192,1536]{1,0:T(8,128)(2,1)S(1)}) custom-call(s32[4]{0:T(128)S(1)} %pad_add_fusion.at, bf16[192,1536]{1,0:T(8,128)(2,1)S(1)} %get-tuple-element.57.ordered, bf16[192,1536]{1,0:T(8,128)(2,1)S(1)} %get-tuple-element.54.grad, bf16[768,384]{1,0:T(8,128)(2,1)S(1)} %bitcast.61, ...), custom_call_target="tpu_custom_call" | custom-call | bytes 21000000 | tf_op jit(solution)/shard_map/project/pallas_call | solution.py:228
  126.1 1.7 fusion.3
  127.8 1.0 collective-permute-start.12
  128.8 2.3 %collective-permute-start.13 = (bf16[384,384]{1,0:T(8,128)(2,1)S(1)}, bf16[384,384]{1,0:T(8,128)(2,1)S(1)}, u32[]{:S(2)}, u32[]{:S(2)}) collective-permute-start(bf16[384,384]{1,0:T(8,128)(2,1)S(1)} %get-tuple-element.90), channel_id=1, source_target_pairs={{0,192},{64,0},{128,64},{192,128},{1,193},{65,1},{129,65},{193,129... | collective-permute-start | bytes 884744 | tf_op jit(solution)/shard_map/ppermute | solution.py:297
  131.1 6.8 %backward.1 = bf16[512,2304]{1,0:T(8,128)(2,1)} custom-call(bf16[192,1536]{1,0:T(8,128)(2,1)S(1)} %get-tuple-element.47.q, bf16[192,1536]{1,0:T(8,128)(2,1)S(1)} %get-tuple-element.48.k, bf16[192,1536]{1,0:T(8,128)(2,1)S(1)} %get-tuple-element.49.v, bf16[192,1536]{1,0:T(8,128)(2,1)S(1)} %get-tuple-element.65.mixed_grad, ...), custom_call_target="tpu_custom_call" | custom-call | bytes 21000000 | tf_op jit(solution)/shard_map/backward/pallas_call | solution.py:255
  137.9 0.3 collective-permute-done.12
  138.2 0.7 copy-done.4
  138.9 0.7 copy-done.6
  139.6 8.8 %all-to-all-start.1 = ((bf16[64,8,2304]{2,1,0:T(8,128)(2,1)}), bf16[64,8,2304]{2,1,0:T(8,128)(2,1)S(1)}, u32[]{:S(2)}, u32[]{:S(2)}) async-start(bf16[64,8,2304]{2,1,0:T(8,128)(2,1)} %bitcast.19), calls=%async_computation.1 | async-start | bytes 4718592 | tf_op jit(solution)/shard_map/all_to_all | solution.py:360
  148.6 0.9 copy-done.7
  149.6 2.4 %collective-permute-start.15 = (bf16[768,384]{1,0:T(8,128)(2,1)S(1)}, bf16[768,384]{1,0:T(8,128)(2,1)S(1)}, u32[]{:S(2)}, u32[]{:S(2)}) collective-permute-start(bf16[768,384]{1,0:T(8,128)(2,1)S(1)} %pad_maximum_fusion.1), channel_id=1, source_target_pairs={{0,192},{64,0},{128,64},{192,128},{1,193},{65,1},{129,65},{193,129... | collective-permute-start | bytes 1769480 | tf_op jit(solution)/shard_map/ppermute | solution.py:297
  152.3 12.8 %collective-permute-done.15 = bf16[768,384]{1,0:T(8,128)(2,1)S(1)} collective-permute-done((bf16[768,384]{1,0:T(8,128)(2,1)S(1)}, bf16[768,384]{1,0:T(8,128)(2,1)S(1)}, u32[]{:S(2)}, u32[]{:S(2)}) %collective-permute-start.15) | collective-permute-done | bytes 589856 | tf_op jit(solution)/shard_map/ppermute | solution.py:297
  165.1 3.5 %collective-permute-done.14 = bf16[768,384]{1,0:T(8,128)(2,1)S(1)} collective-permute-done((bf16[768,384]{1,0:T(8,128)(2,1)S(1)}, bf16[768,384]{1,0:T(8,128)(2,1)S(1)}, u32[]{:S(2)}, u32[]{:S(2)}) %collective-permute-start.14) | collective-permute-done | bytes 589856 | tf_op jit(solution)/shard_map/ppermute | solution.py:297
  168.6 0.2 add_convert_fusion
  168.8 2.4 %collective-permute-start.18 = (bf16[192,384]{1,0:T(8,128)(2,1)S(1)}, bf16[192,384]{1,0:T(8,128)(2,1)S(1)}, u32[]{:S(2)}, u32[]{:S(2)}) collective-permute-start(bf16[192,384]{1,0:T(8,128)(2,1)S(1)} %get-tuple-element.88), channel_id=1, source_target_pairs={{0,32},{1,33},{2,34},{3,35},{4,36},{5,37},{6,38},{7,39},{8,40},{9,... | collective-permute-start | bytes 442376 | tf_op jit(solution)/shard_map/ppermute | solution.py:314
  171.2 1.4 collective-permute-start.17
  172.5 0.7 collective-permute-start.16
  173.2 5.5 %collective-permute-done.18 = bf16[192,384]{1,0:T(8,128)(2,1)S(1)} collective-permute-done((bf16[192,384]{1,0:T(8,128)(2,1)S(1)}, bf16[192,384]{1,0:T(8,128)(2,1)S(1)}, u32[]{:S(2)}, u32[]{:S(2)}) %collective-permute-start.18) | collective-permute-done | bytes 147488 | tf_op jit(solution)/shard_map/ppermute | solution.py:314
  178.7 4.2 %collective-permute-done.17 = bf16[192,384]{1,0:T(8,128)(2,1)} collective-permute-done((bf16[192,384]{1,0:T(8,128)(2,1)S(1)}, bf16[192,384]{1,0:T(8,128)(2,1)}, u32[]{:S(2)}, u32[]{:S(2)}) %collective-permute-start.17) | collective-permute-done | bytes 147488 | tf_op jit(solution)/shard_map/ppermute | solution.py:314
  182.9 1.7 collective-permute-done.16
  184.6 1.1 add_convert_fusion.7
  185.7 4.7 %collective-permute-start.21 = (bf16[2,24,384]{2,1,0:T(8,128)(2,1)S(1)}, bf16[2,24,384]{2,1,0:T(8,128)(2,1)S(1)}, u32[]{:S(2)}, u32[]{:S(2)}) collective-permute-start(bf16[2,24,384]{2,1,0:T(8,128)(2,1)S(1)} %get-tuple-element.96), channel_id=1, source_target_pairs={{0,12},{1,13},{2,14},{3,15},{4,8},{5,9},{6,10},{7,11},{8,4},{9,5},... | collective-permute-start | bytes 110600 | tf_op jit(solution)/shard_map/ppermute | solution.py:321
  190.3 3.0 %collective-permute-start.20 = (bf16[2,24,384]{2,1,0:T(8,128)(2,1)S(1)}, bf16[2,24,384]{2,1,0:T(8,128)(2,1)S(1)}, u32[]{:S(2)}, u32[]{:S(2)}) collective-permute-start(bf16[2,24,384]{2,1,0:T(8,128)(2,1)S(1)} %get-tuple-element.97), channel_id=1, source_target_pairs={{0,4},{1,5},{2,6},{3,7},{4,0},{5,1},{6,2},{7,3},{8,12},{9,13},{10,... | collective-permute-start | bytes 110600 | tf_op jit(solution)/shard_map/ppermute | solution.py:321
  193.4 12.1 %collective-permute-done.21 = bf16[2,24,384]{2,1,0:T(8,128)(2,1)S(1)} collective-permute-done((bf16[2,24,384]{2,1,0:T(8,128)(2,1)S(1)}, bf16[2,24,384]{2,1,0:T(8,128)(2,1)S(1)}, u32[]{:S(2)}, u32[]{:S(2)}) %collective-permute-start.21) | collective-permute-done | bytes 36896 | tf_op jit(solution)/shard_map/ppermute | solution.py:321
  205.4 3.0 %collective-permute-done.19 = bf16[2,24,384]{2,1,0:T(8,128)(2,1)S(1)} collective-permute-done((bf16[2,24,384]{2,1,0:T(8,128)(2,1)S(1)}, bf16[2,24,384]{2,1,0:T(8,128)(2,1)S(1)}, u32[]{:S(2)}, u32[]{:S(2)}) %collective-permute-start.19) | collective-permute-done | bytes 36896 | tf_op jit(solution)/shard_map/ppermute | solution.py:321
  208.5 0.7 collective-permute-start.22
  209.2 3.2 %collective-permute-done.22 = bf16[24,384]{1,0:T(8,128)(2,1)S(1)} collective-permute-done((bf16[24,384]{1,0:T(8,128)(2,1)S(1)}, bf16[24,384]{1,0:T(8,128)(2,1)S(1)}, u32[]{:S(2)}, u32[]{:S(2)}) %collective-permute-start.22) | collective-permute-done | bytes 18464 | tf_op jit(solution)/shard_map/ppermute | solution.py:327
  212.3 0.5 collective-permute-start.23
  212.9 3.5 %collective-permute-done.23 = f32[24,384]{1,0:T(8,128)S(1)} collective-permute-done((f32[24,384]{1,0:T(8,128)S(1)}, f32[24,384]{1,0:T(8,128)S(1)}, u32[]{:S(2)}, u32[]{:S(2)}) %collective-permute-start.23) | collective-permute-done | bytes 36896 | tf_op jit(solution)/shard_map/ppermute | solution.py:332
  216.4 2.5 %collective-permute-start.24 = (f32[2,24,384]{2,1,0:T(8,128)S(1)}, f32[2,24,384]{2,1,0:T(8,128)S(1)}, u32[]{:S(2)}, u32[]{:S(2)}) collective-permute-start(f32[2,24,384]{2,1,0:T(8,128)S(1)} %pad_maximum_fusion.4), channel_id=1, source_target_pairs={{0,128},{64,192},{128,0},{192,64},{1,129},{65,193},{129,1},{193,65... | collective-permute-start | bytes 221192 | tf_op jit(solution)/shard_map/ppermute | solution.py:332
  218.9 2.5 %unpack.1 = (bf16[192,1536]{1,0:T(8,128)(2,1)}, bf16[192,1536]{1,0:T(8,128)(2,1)}, bf16[192,1536]{1,0:T(8,128)(2,1)}, bf16[192,1536]{1,0:T(8,128)(2,1)}) custom-call(bf16[512,2304]{1,0:T(8,128)(2,1)S(1)} %bitcast.56), custom_call_target="tpu_custom_call" | custom-call | bytes 14000000 | tf_op jit(solution)/shard_map/unpack/pallas_call | solution.py:98
  221.5 0.8 collective-permute-done.24
  222.3 0.7 pad_maximum_fusion.2
  (48 shorter events, 0.9 us)
Async XLA Ops:
  8.0 9.7 %collective-permute-start.2 = (bf16[24,384]{1,0:T(8,128)(2,1)S(1)}, bf16[24,384]{1,0:T(8,128)(2,1)S(1)}, u32[]{:S(2)}, u32[]{:S(2)}) collective-permute-start(bf16[24,384]{1,0:T(8,128)(2,1)S(1)} %select_select_fusion), channel_id=1, source_target_pairs={{0,16},{1,17},{2,18},{3,19},{4,20},{5,21},{6,22},{7,23},{8,24},{9,... | collective-permute-start | bytes 55304 | tf_op jit(solution)/shard_map/ppermute | solution.py:343
  9.6 8.0 %collective-permute-start.1 = (bf16[24,384]{1,0:T(8,128)(2,1)S(1)}, bf16[24,384]{1,0:T(8,128)(2,1)S(1)}, u32[]{:S(2)}, u32[]{:S(2)}) collective-permute-start(bf16[24,384]{1,0:T(8,128)(2,1)S(1)} %select_select_fusion), channel_id=1, source_target_pairs={{0,32},{1,33},{2,34},{3,35},{4,36},{5,37},{6,38},{7,39},{8,40},{9,... | collective-permute-start | bytes 55304 | tf_op jit(solution)/shard_map/ppermute | solution.py:343
  12.3 5.4 %collective-permute-start = (bf16[24,384]{1,0:T(8,128)(2,1)S(1)}, bf16[24,384]{1,0:T(8,128)(2,1)S(1)}, u32[]{:S(2)}, u32[]{:S(2)}) collective-permute-start(bf16[24,384]{1,0:T(8,128)(2,1)S(1)} %select_select_fusion), channel_id=1, source_target_pairs={{0,48},{1,49},{2,50},{3,51},{4,52},{5,53},{6,54},{7,55},{8,56},{9,... | collective-permute-start | bytes 55304 | tf_op jit(solution)/shard_map/ppermute | solution.py:343
  18.3 78.5 %all-to-all-start = ((bf16[64,8,2304]{2,1,0:T(8,128)(2,1)}), bf16[64,8,2304]{2,1,0:T(8,128)(2,1)S(1)}, u32[]{:S(2)}, u32[]{:S(2)}) async-start(bf16[64,8,2304]{2,1,0:T(8,128)(2,1)} %bitcast.62), calls=%async_computation | async-start | bytes 4718592 | tf_op jit(solution)/shard_map/all_to_all | solution.py:360
  28.8 49.6 %all-gather.3.cloned.1.call-start = ((), (), s32[]{:S(2)}) async-start(), calls=%async_computation.2 | async-start | bytes 1253376 | tf_op jit(solution)/shard_map/all_gather | solution.py:349
  79.8 3.5 %copy-start.8 = (s32[1,64]{1,0:T(1,128)S(1)}, s32[1,64]{1,0:T(1,128)}, u32[]{:S(2)}) copy-start(s32[1,64]{1,0:T(1,128)} %param.11) | copy-start | bytes 772
  80.0 16.9 %collective-permute-start.3 = (bf16[768,384]{1,0:T(8,128)(2,1)S(1)}, bf16[768,384]{1,0:T(8,128)(2,1)}, u32[]{:S(2)}, u32[]{:S(2)}) collective-permute-start(bf16[768,384]{1,0:T(8,128)(2,1)S(1)} %bitcast.59), channel_id=1, source_target_pairs={{0,64},{64,128},{128,192},{192,0},{1,65},{65,129},{129,193},{193,1... | collective-permute-start | bytes 1769480 | tf_op jit(solution)/shard_map/ppermute | solution.py:297
  81.5 15.3 %collective-permute-start.4 = (bf16[768,384]{1,0:T(8,128)(2,1)S(1)}, bf16[768,384]{1,0:T(8,128)(2,1)}, u32[]{:S(2)}, u32[]{:S(2)}) collective-permute-start(bf16[768,384]{1,0:T(8,128)(2,1)S(1)} %bitcast.60), channel_id=1, source_target_pairs={{0,192},{64,0},{128,64},{192,128},{1,193},{65,1},{129,65},{193,129... | collective-permute-start | bytes 1769480 | tf_op jit(solution)/shard_map/ppermute | solution.py:297
  98.5 11.5 %collective-permute-start.5 = (bf16[384,384]{1,0:T(8,128)(2,1)}, bf16[384,384]{1,0:T(8,128)(2,1)}, u32[]{:S(2)}, u32[]{:S(2)}) collective-permute-start(bf16[384,384]{1,0:T(8,128)(2,1)} %slice.112), channel_id=1, source_target_pairs={{0,64},{64,128},{128,192},{192,0},{1,65},{65,129},{129,193},{193,1... | collective-permute-start | bytes 884744 | tf_op jit(solution)/shard_map/ppermute | solution.py:297
  101.7 8.4 %collective-permute-start.6 = (bf16[384,384]{1,0:T(8,128)(2,1)}, bf16[384,384]{1,0:T(8,128)(2,1)}, u32[]{:S(2)}, u32[]{:S(2)}) collective-permute-start(bf16[384,384]{1,0:T(8,128)(2,1)} %slice.113), channel_id=1, source_target_pairs={{0,192},{64,0},{128,64},{192,128},{1,193},{65,1},{129,65},{193,129... | collective-permute-start | bytes 884744 | tf_op jit(solution)/shard_map/ppermute | solution.py:297
  103.6 0.8 copy-start
  113.7 12.4 %collective-permute-start.7 = (bf16[4,768,384]{2,1,0:T(8,128)(2,1)S(1)}, bf16[4,768,384]{2,1,0:T(8,128)(2,1)S(1)}, u32[]{:S(2)}, u32[]{:S(2)}) collective-permute-start(bf16[4,768,384]{2,1,0:T(8,128)(2,1)S(1)} %get-tuple-element.56), channel_id=1, source_target_pairs={{0,1},{1,0},{2,3},{3,2},{4,5},{5,4},{6,7},{7,6},{8,9},{9,8},{10,11... | collective-permute-start | bytes 7077896 | tf_op jit(solution)/shard_map/ppermute | solution.py:356
  113.8 7.3 %collective-permute-start.8 = (bf16[768,384]{1,0:T(8,128)(2,1)}, bf16[768,384]{1,0:T(8,128)(2,1)S(1)}, u32[]{:S(2)}, u32[]{:S(2)}) collective-permute-start(bf16[768,384]{1,0:T(8,128)(2,1)} %collective-permute-done.3.refs_1_), channel_id=1, source_target_pairs={{0,1},{1,0},{2,3},{3,2},{4,5},{5,4},{6,7},{7,6},{8,9},{9,8},{10,11... | collective-permute-start | bytes 1769480 | tf_op jit(solution)/shard_map/ppermute | solution.py:356
  114.3 6.8 %collective-permute-start.9 = (bf16[768,384]{1,0:T(8,128)(2,1)}, bf16[768,384]{1,0:T(8,128)(2,1)S(1)}, u32[]{:S(2)}, u32[]{:S(2)}) collective-permute-start(bf16[768,384]{1,0:T(8,128)(2,1)} %collective-permute-done.4.refs_2_), channel_id=1, source_target_pairs={{0,1},{1,0},{2,3},{3,2},{4,5},{5,4},{6,7},{7,6},{8,9},{9,8},{10,11... | collective-permute-start | bytes 1769480 | tf_op jit(solution)/shard_map/ppermute | solution.py:356
  114.4 6.0 %collective-permute-start.10 = (bf16[384,384]{1,0:T(8,128)(2,1)}, bf16[384,384]{1,0:T(8,128)(2,1)S(1)}, u32[]{:S(2)}, u32[]{:S(2)}) collective-permute-start(bf16[384,384]{1,0:T(8,128)(2,1)} %collective-permute-done.5.refs_3_), channel_id=1, source_target_pairs={{0,1},{1,0},{2,3},{3,2},{4,5},{5,4},{6,7},{7,6},{8,9},{9,8},{10,11... | collective-permute-start | bytes 884744 | tf_op jit(solution)/shard_map/ppermute | solution.py:356
  114.8 6.3 %collective-permute-start.11 = (bf16[384,384]{1,0:T(8,128)(2,1)}, bf16[384,384]{1,0:T(8,128)(2,1)S(1)}, u32[]{:S(2)}, u32[]{:S(2)}) collective-permute-start(bf16[384,384]{1,0:T(8,128)(2,1)} %collective-permute-done.6.refs_4_), channel_id=1, source_target_pairs={{0,1},{1,0},{2,3},{3,2},{4,5},{5,4},{6,7},{7,6},{8,9},{9,8},{10,11... | collective-permute-start | bytes 884744 | tf_op jit(solution)/shard_map/ppermute | solution.py:356
  127.8 10.4 %collective-permute-start.12 = (bf16[384,384]{1,0:T(8,128)(2,1)S(1)}, bf16[384,384]{1,0:T(8,128)(2,1)S(1)}, u32[]{:S(2)}, u32[]{:S(2)}) collective-permute-start(bf16[384,384]{1,0:T(8,128)(2,1)S(1)} %get-tuple-element.91), channel_id=1, source_target_pairs={{0,64},{64,128},{128,192},{192,0},{1,65},{65,129},{129,193},{193,1... | collective-permute-start | bytes 884744 | tf_op jit(solution)/shard_map/ppermute | solution.py:297
  128.8 9.4 %collective-permute-start.13 = (bf16[384,384]{1,0:T(8,128)(2,1)S(1)}, bf16[384,384]{1,0:T(8,128)(2,1)S(1)}, u32[]{:S(2)}, u32[]{:S(2)}) collective-permute-start(bf16[384,384]{1,0:T(8,128)(2,1)S(1)} %get-tuple-element.90), channel_id=1, source_target_pairs={{0,192},{64,0},{128,64},{192,128},{1,193},{65,1},{129,65},{193,129... | collective-permute-start | bytes 884744 | tf_op jit(solution)/shard_map/ppermute | solution.py:297
  138.2 0.7 copy-start.4
  138.9 0.7 copy-start.6
  139.6 8.9 %copy-start.2 = (bf16[768,384]{1,0:T(8,128)(2,1)S(1)}, bf16[768,384]{1,0:T(8,128)(2,1)}, u32[]{:S(2)}) copy-start(bf16[768,384]{1,0:T(8,128)(2,1)} %get-tuple-element.73) | copy-start | bytes 1769476
  139.6 8.9 %copy-start.1 = (bf16[768,384]{1,0:T(8,128)(2,1)S(1)}, bf16[768,384]{1,0:T(8,128)(2,1)}, u32[]{:S(2)}) copy-start(bf16[768,384]{1,0:T(8,128)(2,1)} %get-tuple-element.71) | copy-start | bytes 1769476
  139.6 68.8 %all-to-all-start.1 = ((bf16[64,8,2304]{2,1,0:T(8,128)(2,1)}), bf16[64,8,2304]{2,1,0:T(8,128)(2,1)S(1)}, u32[]{:S(2)}, u32[]{:S(2)}) async-start(bf16[64,8,2304]{2,1,0:T(8,128)(2,1)} %bitcast.19), calls=%async_computation.1 | async-start | bytes 4718592 | tf_op jit(solution)/shard_map/all_to_all | solution.py:360
  148.5 1.0 copy-start.7
  148.5 3.5 %copy-start.5 = (bf16[384,384]{1,0:T(8,128)(2,1)S(1)}, bf16[384,384]{1,0:T(8,128)(2,1)}, u32[]{:S(2)}) copy-start(bf16[384,384]{1,0:T(8,128)(2,1)} %copy-done.4) | copy-start | bytes 884740
  149.6 19.0 %copy-start.3 = (bf16[768,384]{1,0:T(8,128)(2,1)S(1)}, bf16[768,384]{1,0:T(8,128)(2,1)}, u32[]{:S(2)}) copy-start(bf16[768,384]{1,0:T(8,128)(2,1)} %get-tuple-element.70) | copy-start | bytes 1769476
  149.6 15.5 %collective-permute-start.15 = (bf16[768,384]{1,0:T(8,128)(2,1)S(1)}, bf16[768,384]{1,0:T(8,128)(2,1)S(1)}, u32[]{:S(2)}, u32[]{:S(2)}) collective-permute-start(bf16[768,384]{1,0:T(8,128)(2,1)S(1)} %pad_maximum_fusion.1), channel_id=1, source_target_pairs={{0,192},{64,0},{128,64},{192,128},{1,193},{65,1},{129,65},{193,129... | collective-permute-start | bytes 1769480 | tf_op jit(solution)/shard_map/ppermute | solution.py:297
  152.2 16.4 %collective-permute-start.14 = (bf16[768,384]{1,0:T(8,128)(2,1)S(1)}, bf16[768,384]{1,0:T(8,128)(2,1)S(1)}, u32[]{:S(2)}, u32[]{:S(2)}) collective-permute-start(bf16[768,384]{1,0:T(8,128)(2,1)S(1)} %pad_maximum_fusion), channel_id=1, source_target_pairs={{0,64},{64,128},{128,192},{192,0},{1,65},{65,129},{129,193},{193,1... | collective-permute-start | bytes 1769480 | tf_op jit(solution)/shard_map/ppermute | solution.py:297
  168.8 9.9 %collective-permute-start.18 = (bf16[192,384]{1,0:T(8,128)(2,1)S(1)}, bf16[192,384]{1,0:T(8,128)(2,1)S(1)}, u32[]{:S(2)}, u32[]{:S(2)}) collective-permute-start(bf16[192,384]{1,0:T(8,128)(2,1)S(1)} %get-tuple-element.88), channel_id=1, source_target_pairs={{0,32},{1,33},{2,34},{3,35},{4,36},{5,37},{6,38},{7,39},{8,40},{9,... | collective-permute-start | bytes 442376 | tf_op jit(solution)/shard_map/ppermute | solution.py:314
  171.2 11.7 %collective-permute-start.17 = (bf16[192,384]{1,0:T(8,128)(2,1)S(1)}, bf16[192,384]{1,0:T(8,128)(2,1)}, u32[]{:S(2)}, u32[]{:S(2)}) collective-permute-start(bf16[192,384]{1,0:T(8,128)(2,1)S(1)} %get-tuple-element.89), channel_id=1, source_target_pairs={{0,48},{1,49},{2,50},{3,51},{4,52},{5,53},{6,54},{7,55},{8,56},{9,... | collective-permute-start | bytes 442376 | tf_op jit(solution)/shard_map/ppermute | solution.py:314
  172.5 12.1 %collective-permute-start.16 = (bf16[192,384]{1,0:T(8,128)(2,1)S(1)}, bf16[192,384]{1,0:T(8,128)(2,1)}, u32[]{:S(2)}, u32[]{:S(2)}) collective-permute-start(bf16[192,384]{1,0:T(8,128)(2,1)S(1)} %get-tuple-element.87), channel_id=1, source_target_pairs={{0,16},{1,17},{2,18},{3,19},{4,20},{5,21},{6,22},{7,23},{8,24},{9,... | collective-permute-start | bytes 442376 | tf_op jit(solution)/shard_map/ppermute | solution.py:314
  185.7 19.8 %collective-permute-start.21 = (bf16[2,24,384]{2,1,0:T(8,128)(2,1)S(1)}, bf16[2,24,384]{2,1,0:T(8,128)(2,1)S(1)}, u32[]{:S(2)}, u32[]{:S(2)}) collective-permute-start(bf16[2,24,384]{2,1,0:T(8,128)(2,1)S(1)} %get-tuple-element.96), channel_id=1, source_target_pairs={{0,12},{1,13},{2,14},{3,15},{4,8},{5,9},{6,10},{7,11},{8,4},{9,5},... | collective-permute-start | bytes 110600 | tf_op jit(solution)/shard_map/ppermute | solution.py:321
  190.3 15.1 %collective-permute-start.20 = (bf16[2,24,384]{2,1,0:T(8,128)(2,1)S(1)}, bf16[2,24,384]{2,1,0:T(8,128)(2,1)S(1)}, u32[]{:S(2)}, u32[]{:S(2)}) collective-permute-start(bf16[2,24,384]{2,1,0:T(8,128)(2,1)S(1)} %get-tuple-element.97), channel_id=1, source_target_pairs={{0,4},{1,5},{2,6},{3,7},{4,0},{5,1},{6,2},{7,3},{8,12},{9,13},{10,... | collective-permute-start | bytes 110600 | tf_op jit(solution)/shard_map/ppermute | solution.py:321
  193.4 15.1 %collective-permute-start.19 = (bf16[2,24,384]{2,1,0:T(8,128)(2,1)S(1)}, bf16[2,24,384]{2,1,0:T(8,128)(2,1)S(1)}, u32[]{:S(2)}, u32[]{:S(2)}) collective-permute-start(bf16[2,24,384]{2,1,0:T(8,128)(2,1)S(1)} %get-tuple-element.95), channel_id=1, source_target_pairs={{0,8},{1,9},{2,10},{3,11},{4,12},{5,13},{6,14},{7,15},{8,0},{9,1},... | collective-permute-start | bytes 110600 | tf_op jit(solution)/shard_map/ppermute | solution.py:321
  208.5 3.8 %collective-permute-start.22 = (bf16[24,384]{1,0:T(8,128)(2,1)S(1)}, bf16[24,384]{1,0:T(8,128)(2,1)S(1)}, u32[]{:S(2)}, u32[]{:S(2)}) collective-permute-start(bf16[24,384]{1,0:T(8,128)(2,1)S(1)} %select_bitcast_fusion), channel_id=1, source_target_pairs={{0,2},{1,3},{2,0},{3,1},{4,6},{5,7},{6,4},{7,5},{8,10},{9,11},{10,... | collective-permute-start | bytes 55304 | tf_op jit(solution)/shard_map/ppermute | solution.py:327
  212.3 4.0 %collective-permute-start.23 = (f32[24,384]{1,0:T(8,128)S(1)}, f32[24,384]{1,0:T(8,128)S(1)}, u32[]{:S(2)}, u32[]{:S(2)}) collective-permute-start(f32[24,384]{1,0:T(8,128)S(1)} %convert_add_fusion.1), channel_id=1, source_target_pairs={{0,64},{64,0},{128,192},{192,128},{1,65},{65,1},{129,193},{193,129... | collective-permute-start | bytes 110600 | tf_op jit(solution)/shard_map/ppermute | solution.py:332
  216.4 5.9 %collective-permute-start.24 = (f32[2,24,384]{2,1,0:T(8,128)S(1)}, f32[2,24,384]{2,1,0:T(8,128)S(1)}, u32[]{:S(2)}, u32[]{:S(2)}) collective-permute-start(f32[2,24,384]{2,1,0:T(8,128)S(1)} %pad_maximum_fusion.4), channel_id=1, source_target_pairs={{0,128},{64,192},{128,0},{192,64},{1,129},{65,193},{129,1},{193,65... | collective-permute-start | bytes 221192 | tf_op jit(solution)/shard_map/ppermute | solution.py:332
Sparse Core Ops, SparseCore 0:
  32.0 46.3 all-gather.2
